TPU v7x, 32 devices: a whole 2x2x4 slice. The times are simulated.
32 devices in a mesh: rows: 4 (over z), centers: 8 (over y, x, core).
Axes of the slice: x: 2, y: 2, z: 4, core: 2. Of those that a mesh axis runs over, the one named last changes fastest.
Arguments:
- features: float32 [4096, 128], P('rows'), may hold values from -6 to 6
- centers: float32 [16384, 128], P('centers'), may hold values from -6 to 6
- labels: int32 [4096, 64], P('rows'), may hold values 0 or 1
- coeffs: float32 [16384, 64], P('centers'), may hold values from -3 to 3
- precond: float32 [16384, 16384], P('rows', 'centers'), may hold values from -2 to 2, as said below
Outputs:
- coeffs_out: float32 [16384, 64], P('centers')
Inputs may be any that keep to these rules, and one draw needn't show every extreme that they name: precond is lower triangular: every entry above the diagonal is zero, and its diagonal is positive.
All inputs are finite; a program needn't handle non-finite values. No bound on the sum of `labels` on one device may be relied on, other than what follows from the above.
Results may differ from a plain program's by a relative error of at most 0.0003.
Values sent between devices are 32-bit elements; how exact they have to be, the bound alone decides.
No kernel may reach another device: no remote copies, remote signals or barrier semaphores. Data moves between devices by JAX's collectives and lax.ppermute only.
A program may use at most 128 MiB of HBM per device.

v0:
```python
import jax
import jax.numpy as jnp
from jax import lax
from jax.sharding import PartitionSpec as P

STEPS = 2


step_size = 0.5
epsilon = 1e-06


def kernel_tile(rows_x, centers_x):
    width = rows_x.shape[1]
    left = jnp.sum(rows_x * rows_x, axis=1)
    right = jnp.sum(centers_x * centers_x, axis=1)
    cross = jnp.dot(rows_x, centers_x.T, precision=lax.Precision.HIGHEST)
    return jnp.exp(-2.0 * (left[:, None] + right[None, :] - 2.0 * cross) / width)


def body(features, centers, labels, coeffs, precond):
    rows_total = features.shape[0] * lax.axis_size("rows")
    center_total = coeffs.shape[0] * lax.axis_size("centers")
    targets = labels.astype(jnp.float32)
    for step in range(STEPS):
        tile = kernel_tile(features, centers)
        share_rows = features.shape[0] // lax.axis_size("centers")

        def partial_logits(start, count, tile=tile, coeffs=coeffs):
            return jnp.dot(tile, coeffs, precision=lax.Precision.HIGHEST)

        share = lax.psum_scatter(
            partial_logits(jnp.int32(0), share_rows * lax.axis_size("centers")),
            "centers",
            scatter_dimension=0,
            tiled=True,
        )
        offset = lax.axis_index("centers") * share_rows
        share_y = lax.dynamic_slice_in_dim(targets, offset, share_rows, 0)
        share_resid = (jax.nn.sigmoid(share) - share_y) / rows_total
        resid = lax.all_gather(share_resid, "centers", axis=0, tiled=True)
        local_grad = lax.dot_general(
            tile, resid, (((0,), (0,)), ((), ())), precision=lax.Precision.HIGHEST
        )
        grad = lax.psum(local_grad, "rows")
        fwd = lax.psum(jnp.dot(precond, grad, precision=lax.Precision.HIGHEST), "centers")
        local_square = jnp.sum(fwd * fwd)
        back_local = lax.dot_general(
            precond, fwd, (((0,), (0,)), ((), ())), precision=lax.Precision.HIGHEST
        )
        back = lax.psum(back_local, "rows")
        total = lax.psum(local_square, "rows")
        scale = step_size / jnp.sqrt(total / (center_total * fwd.shape[1]) + epsilon)
        coeffs = coeffs - scale * back
    return coeffs


def solution(mesh):
    in_specs = (
        P("rows", None),
        P("centers", None),
        P("rows", None),
        P("centers", None),
        P("rows", "centers"),
    )
    out_specs = P("centers", None)
    return jax.shard_map(body, mesh=mesh, in_specs=in_specs, out_specs=out_specs, check_vma=False)
```

profile of v0, /device:TPU:0, one launch (start us, length us, event | category | flops | bytes accessed | tf_op | source)
XLA Modules:
  0.0 603.2 jit_solution(10818199397413174952)
XLA Ops:
  6.5 1.3 multiply_reduce_fusion.3
  7.9 1.6 multiply_reduce_fusion.2
  9.4 9.3 %multiply_exponential_fusion = f32[1024,2048]{1,0:T(8,128)S(1)} fusion(f32[1024,128]{1,0:T(8,128)} %param.5, f32[2048,128]{1,0:T(8,128)} %param.6, f32[2048]{0:T(1024)S(1)} %multiply_reduce_fusion.2, f32[1024]{0:T(1024)S(1)} %multiply_reduce_fusion.3), kind=kOutput, calls=%fused_computation | convolution fusion | flops 3229614080 | bytes 9973760 | tf_op jit(solution)/shard_map/dot_general | solution.py:17
  18.7 3.2 copy-done
  21.9 9.1 %fusion.1 = f32[1024,64]{0,1:T(8,128)} fusion(f32[1024,2048]{1,0:T(8,128)S(1)} %multiply_exponential_fusion, f32[2048,64]{0,1:T(8,128)S(1)} %copy-done.1), kind=kOutput, calls=%fused_computation.15 | convolution fusion | flops 1610612736 | bytes 9175040 | tf_op jit(solution)/shard_map/dot_general | solution.py:30
  31.1 0.0 all-reduce.7.cloned.1.call-start
  31.1 36.4 %reduce-scatter.3.cloned.1.call-done = f32[128,64]{0,1:T(8,128)} async-done(((f32[1024,64]{0,1:T(8,128)}), f32[128,64]{0,1:T(8,128)}) %reduce-scatter.3.cloned.1.call-update) | async-done | bytes 32784 | tf_op jit(solution)/shard_map/reduce_scatter | solution.py:32
  67.5 0.8 subtract_multiply_fusion.1
  68.3 9.8 %all_gather.6 = f32[1024,64]{0,1:T(8,128)S(1)} all-gather(f32[128,64]{0,1:T(8,128)S(1)} %subtract_multiply_fusion.1), channel_id=1, replica_groups=mesh['rows'=4,'centers'=8] {'centers'}, dimensions={0}, use_global_device_ids=true | all-gather | bytes 294912 | tf_op jit(solution)/shard_map/all_gather | solution.py:41
  78.1 16.3 %fusion.2 = f32[2048,64]{1,0:T(8,128)} fusion(f32[1024,2048]{1,0:T(8,128)} %copy-done, f32[1024,64]{0,1:T(8,128)S(1)} %all_gather.6), kind=kOutput, calls=%fused_computation.16 | convolution fusion | flops 1610612736 | bytes 9175040 | tf_op jit(solution)/shard_map/dot_general | solution.py:42
  94.4 0.0 all-reduce.9.cloned.1.call-start
  94.5 51.9 %all-reduce.7.cloned.1.call-done = f32[2048,64]{1,0:T(8,128)} async-done(((f32[2048,64]{1,0:T(8,128)}), f32[2048,64]{1,0:T(8,128)}) %all-reduce.7.cloned.1.call-update) | async-done | bytes 524304 | tf_op jit(solution)/shard_map/psum | solution.py:45
  146.4 40.4 %convolution_bitcast_fusion.1 = f32[4096,64]{0,1:T(8,128)} fusion(f32[2048,64]{1,0:T(8,128)} %all-reduce.7.cloned.1.call-done, f32[4096,2048]{1,0:T(8,128)} %param.9), kind=kOutput, calls=%fused_computation.2 | convolution fusion | flops 6442450944 | bytes 35127296 | tf_op jit(solution)/shard_map/dot_general | solution.py:46
  186.9 56.1 %all-reduce.9.cloned.1.call-done = f32[4096,64]{0,1:T(8,128)} async-done(((f32[4096,64]{0,1:T(8,128)}), f32[4096,64]{0,1:T(8,128)}) %all-reduce.9.cloned.1.call-update) | async-done | bytes 1048592 | tf_op jit(solution)/shard_map/psum | solution.py:46
  243.0 27.1 %convolution_bitcast_fusion.3 = f32[2048,64]{0,1:T(8,128)} fusion(f32[4096,64]{0,1:T(8,128)} %all-reduce.9.cloned.1.call-done, f32[4096,2048]{1,0:T(8,128)} %param.9), kind=kOutput, calls=%fused_computation.4 | convolution fusion | flops 6442450944 | bytes 35127296 | tf_op jit(solution)/shard_map/dot_general | solution.py:48
  270.1 0.0 reduce-scatter.5.cloned.1.call-start
  270.2 0.8 multiply_reduce_fusion.1
  271.0 12.3 %psum.58 = f32[]{:T(128)} all-reduce(f32[]{:T(128)} %multiply_reduce_fusion.1), channel_id=1, replica_groups=mesh['rows'=4,'centers'=8] {'rows'}, use_global_device_ids=true, to_apply=%region_6.0 | all-reduce | flops 1 | bytes 8 | tf_op jit(solution)/shard_map/psum | solution.py:52
  284.0 23.9 %all-reduce.11.cloned.1.call-done = f32[2048,64]{0,1:T(8,128)} async-done(((f32[2048,64]{0,1:T(8,128)}), f32[2048,64]{0,1:T(8,128)}) %all-reduce.11.cloned.1.call-update) | async-done | bytes 524304 | tf_op jit(solution)/shard_map/psum | solution.py:51
  307.8 12.3 %fusion = f32[1024,64]{0,1:T(8,128)} fusion(f32[1024,2048]{1,0:T(8,128)} %copy-done, f32[2048,64]{0,1:T(8,128)S(1)} %copy-done.1, f32[2048,64]{0,1:T(8,128)} %all-reduce.11.cloned.1.call-done, f32[]{:T(128)S(6)} %div.35), kind=kOutput, calls=%fused_computation.11 | convolution fusion | flops 1610874880 | bytes 9699332 | tf_op jit(solution)/shard_map/dot_general | solution.py:30
  320.2 33.7 %reduce-scatter.5.cloned.1.call-done = f32[128,64]{0,1:T(8,128)} async-done(((f32[1024,64]{0,1:T(8,128)}), f32[128,64]{0,1:T(8,128)}) %reduce-scatter.5.cloned.1.call-update) | async-done | bytes 32784 | tf_op jit(solution)/shard_map/reduce_scatter | solution.py:32
  353.9 0.8 subtract_multiply_fusion
  354.7 9.8 %all_gather.7 = f32[1024,64]{0,1:T(8,128)S(1)} all-gather(f32[128,64]{0,1:T(8,128)S(1)} %subtract_multiply_fusion), channel_id=1, replica_groups=mesh['rows'=4,'centers'=8] {'centers'}, dimensions={0}, use_global_device_ids=true | all-gather | bytes 294912 | tf_op jit(solution)/shard_map/all_gather | solution.py:41
  364.5 16.4 %fusion.3 = f32[2048,64]{1,0:T(8,128)} fusion(f32[1024,2048]{1,0:T(8,128)} %copy-done, f32[1024,64]{0,1:T(8,128)S(1)} %all_gather.7), kind=kOutput, calls=%fused_computation.17 | convolution fusion | flops 1610612736 | bytes 9175040 | tf_op jit(solution)/shard_map/dot_general | solution.py:42
  381.0 51.9 %all-reduce.13.cloned.1.call-done = f32[2048,64]{1,0:T(8,128)} async-done(((f32[2048,64]{1,0:T(8,128)}), f32[2048,64]{1,0:T(8,128)}) %all-reduce.13.cloned.1.call-update) | async-done | bytes 524304 | tf_op jit(solution)/shard_map/psum | solution.py:45
  433.0 40.4 %convolution_bitcast_fusion = f32[4096,64]{0,1:T(8,128)} fusion(f32[2048,64]{1,0:T(8,128)} %all-reduce.13.cloned.1.call-done, f32[4096,2048]{1,0:T(8,128)} %param.9), kind=kOutput, calls=%fused_computation.1 | convolution fusion | flops 6442450944 | bytes 35127296 | tf_op jit(solution)/shard_map/dot_general | solution.py:46
  473.5 56.1 %all-reduce.15.cloned.1.call-done = f32[4096,64]{0,1:T(8,128)} async-done(((f32[4096,64]{0,1:T(8,128)}), f32[4096,64]{0,1:T(8,128)}) %all-reduce.15.cloned.1.call-update) | async-done | bytes 1048592 | tf_op jit(solution)/shard_map/psum | solution.py:46
  529.6 27.1 %convolution_bitcast_fusion.2 = f32[2048,64]{0,1:T(8,128)} fusion(f32[4096,64]{0,1:T(8,128)} %all-reduce.15.cloned.1.call-done, f32[4096,2048]{1,0:T(8,128)} %param.9), kind=kOutput, calls=%fused_computation.3 | convolution fusion | flops 6442450944 | bytes 35127296 | tf_op jit(solution)/shard_map/dot_general | solution.py:48
  556.7 0.9 multiply_reduce_fusion
  557.7 12.5 %psum.62 = f32[]{:T(128)} all-reduce(f32[]{:T(128)} %multiply_reduce_fusion), channel_id=1, replica_groups=mesh['rows'=4,'centers'=8] {'rows'}, use_global_device_ids=true, to_apply=%region_12.0 | all-reduce | flops 1 | bytes 8 | tf_op jit(solution)/shard_map/psum | solution.py:52
  570.9 23.4 %all-reduce.17.cloned.1.call-done = f32[2048,64]{0,1:T(8,128)} async-done(((f32[2048,64]{0,1:T(8,128)}), f32[2048,64]{0,1:T(8,128)}) %all-reduce.17.cloned.1.call-update) | async-done | bytes 524304 | tf_op jit(solution)/shard_map/psum | solution.py:51
  594.3 1.9 multiply_subtract_fusion
  (22 shorter events, 0.3 us)
Async XLA Ops:
  6.5 15.4 %copy-start.1 = (f32[2048,64]{0,1:T(8,128)S(1)}, f32[2048,64]{0,1:T(8,128)}, u32[]{:S(2)}) copy-start(f32[2048,64]{0,1:T(8,128)} %param.8) | copy-start | bytes 1572868
  6.5 61.0 %reduce-scatter.3.cloned.1.call-start = ((), (), s32[]{:S(2)}) async-start(), calls=%async_computation.2 | async-start | bytes 294912 | tf_op jit(solution)/shard_map/reduce_scatter | solution.py:32
  18.7 3.2 copy-start
  31.1 115.3 %all-reduce.7.cloned.1.call-start = ((), (), s32[]{:S(2)}) async-start(), calls=%async_computation.3 | async-start | bytes 2097152 | tf_op jit(solution)/shard_map/psum | solution.py:45
  94.4 148.5 %all-reduce.9.cloned.1.call-start = ((), (), s32[]{:S(2)}) async-start(), calls=%async_computation.4 | async-start | bytes 2097152 | tf_op jit(solution)/shard_map/psum | solution.py:46
  186.8 121.0 %all-reduce.11.cloned.1.call-start = ((), (), s32[]{:S(2)}) async-start(), calls=%async_computation.5 | async-start | bytes 1048576 | tf_op jit(solution)/shard_map/psum | solution.py:51
  243.0 27.2 %copy-start.2 = (f32[4096,64]{0,1:T(8,128)S(1)}, f32[4096,64]{0,1:T(8,128)}, u32[]{:S(2)}) copy-start(f32[4096,64]{0,1:T(8,128)} %all-reduce.9.cloned.1.call-done) | copy-start | bytes 3145732
  270.1 83.8 %reduce-scatter.5.cloned.1.call-start = ((), (), s32[]{:S(2)}) async-start(), calls=%async_computation.6 | async-start | bytes 294912 | tf_op jit(solution)/shard_map/reduce_scatter | solution.py:32
  320.2 112.8 %all-reduce.13.cloned.1.call-start = ((), (), s32[]{:S(2)}) async-start(), calls=%async_computation.7 | async-start | bytes 2097152 | tf_op jit(solution)/shard_map/psum | solution.py:45
  381.0 148.6 %all-reduce.15.cloned.1.call-start = ((), (), s32[]{:S(2)}) async-start(), calls=%async_computation.8 | async-start | bytes 2097152 | tf_op jit(solution)/shard_map/psum | solution.py:46
  473.4 120.8 %copy-start.4 = (f32[2048,64]{0,1:T(8,128)S(1)}, f32[2048,64]{0,1:T(8,128)}, u32[]{:S(2)}) copy-start(f32[2048,64]{0,1:T(8,128)} %all-reduce.11.cloned.1.call-done) | copy-start | bytes 1572868
  473.4 120.8 %all-reduce.17.cloned.1.call-start = ((), (), s32[]{:S(2)}) async-start(), calls=%async_computation.9 | async-start | bytes 1048576 | tf_op jit(solution)/shard_map/psum | solution.py:51
  529.6 27.1 %copy-start.3 = (f32[4096,64]{0,1:T(8,128)S(1)}, f32[4096,64]{0,1:T(8,128)}, u32[]{:S(2)}) copy-start(f32[4096,64]{0,1:T(8,128)} %all-reduce.15.cloned.1.call-done) | copy-start | bytes 3145732
Sparse Core Ops, SparseCore 0:
  31.2 36.2 reduce-scatter.2
  94.6 51.8 all-reduce.6
  187.0 55.9 all-reduce.8
  270.2 37.5 all-reduce.10
  320.3 33.6 reduce-scatter.4
  381.1 51.8 all-reduce.12
  473.6 55.9 all-reduce.14
  556.8 37.4 all-reduce.16
where the time goes:
time: 612 us; the launch traced here: 603 us
  waiting for transfers between devices  334 us (55%)
  matrix products  198 us (32%)
  blocking collectives  44.4 us (7%)
  between operations  15.1 us (2%)
  other arithmetic  8.16 us (1%)
    psum x2, waiting for transfers between devices, body(): lax.psum(jnp.dot(precond, grad, precision=lax.Precision.HIGHEST), 'centers')  112 us
    psum x2, waiting for transfers between devices, body(): grad = lax.psum(local_grad, 'rows')  104 us
    dot_general x2, matrix products, body(): jnp.dot(precond, grad, precision=lax.Precision.HIGHEST)  80.8 us
    reduce_scatter x2, waiting for transfers between devices, body(): lax.psum_scatter(partial_logits(jnp.int32(0), share_rows * lax.axis_size(...  70.1 us
    dot_general x2, matrix products, body(): lax.dot_general(precond, fwd, (((0,), (0,)), ((), ())), precision=lax.Pre...  54.2 us
    psum x2, waiting for transfers between devices, body(): back = lax.psum(back_local, 'rows')  47.3 us
    dot_general x2, matrix products, body(): lax.dot_general(tile, resid, (((0,), (0,)), ((), ())), precision=lax.Prec...  32.7 us
    psum x2, blocking collectives, body(): total = lax.psum(local_square, 'rows')  24.8 us
  transfers between devices with their start and end apart: 8, of which 8 were waited for; matrix products, arithmetic and copies ran while one was open for 0% of the time, Pallas kernels for 0%

commit v1 on v0

v1 whole, which is shorter than its diff:
```python
import functools

import jax
import jax.numpy as jnp
from jax import lax
from jax.experimental import pallas as pl
from jax.experimental.pallas import tpu as pltpu
from jax.sharding import PartitionSpec as P

STEPS = 2
step_size = 0.5
epsilon = 1e-06

f32 = jnp.float32
bf16 = jnp.bfloat16
LOG2E = 1.4426950408889634
NN = (((1,), (0,)), ((), ()))
NT = (((1,), (1,)), ((), ()))
WHOLE = pl.BlockSpec(memory_space=pltpu.VMEM)
VMEM_LIMIT = 30 << 20
SLOTS = 6


def dot(a, b, dims):
    return lax.dot_general(a, b, dims, preferred_element_type=f32)


def split(x):
    high = x.astype(bf16)
    return high, (x - high.astype(f32)).astype(bf16)


def split3(x):
    high = x.astype(bf16)
    rest = x - high.astype(f32)
    mid = rest.astype(bf16)
    return high, mid, (rest - mid.astype(f32)).astype(bf16)


def core_of():
    return lax.rem(lax.axis_index("centers"), 2)


def chip_of():
    return lax.div(lax.axis_index("centers"), 2)


def rows_at(start, count):
    return pl.ds(pl.multiple_of(start, count), count)


def stage(x_ref, pieces, places, full, parts):
    for piece, (start, lanes) in zip(pieces, places()):
        full[rows_at(start, piece.shape[0]), lanes] = piece[...]
    high, low = split(full[...])
    out = full.shape[0]
    parts[0:out] = high
    parts[out : 2 * out] = low


def stream(count, copy, use):
    slots = min(SLOTS, count)
    for i in range(slots):
        copy(i, i).start()

    def one(i, carry):
        slot = lax.rem(i, slots)
        copy(i, slot).wait()
        use(i, slot)

        @pl.when(i + slots < count)
        def _():
            copy(i + slots, slot).start()

        return carry

    lax.fori_loop(0, count, one, 0)


def block_of(total, most):
    size = min(total, most)
    while total % size:
        size //= 2
    return size


def down(weights, pieces, places, out, chunks, chunk_at, first, count, squares, name):
    depth = weights.shape[0]
    size = block_of(depth, 512)
    n_pieces = len(pieces)
    share = out // chunks
    extra = 128 if squares else 0

    def kernel(*refs):
        piece_refs = refs[:n_pieces]
        w_ref = refs[n_pieces]
        outs = refs[n_pieces + 1 : n_pieces + 1 + chunks]
        full, parts, total, held, sems = refs[n_pieces + 1 + chunks :]

        def copy(i, slot):
            return pltpu.make_async_copy(
                w_ref.at[pl.ds(i * size, size), pl.ds(first, count)], held.at[slot], sems.at[slot]
            )

        def use(i, slot):
            x = parts[:, pl.ds(pl.multiple_of(i * size, size), size)]
            high, low = split(held[slot])
            both = dot(x, high, NN)
            total[...] += both[:out] + both[out:] + dot(x[:out], low, NN)

        total[...] = jnp.zeros_like(total)
        stage(None, piece_refs, places, full, parts)
        stream(depth // size, copy, use)
        for k in range(chunks):
            outs[k][:, 0:count] = total[rows_at(chunk_at(k) * share, share), :]
        if squares:
            sum_sq = jnp.sum(full[...] * full[...])
            for k in range(chunks):
                outs[k][:, count : count + extra] = jnp.full((share, extra), sum_sq, f32)

    slots = min(SLOTS, depth // size)
    return pl.pallas_call(
        kernel,
        in_specs=[WHOLE] * n_pieces + [pl.BlockSpec(memory_space=pl.ANY)],
        out_specs=[WHOLE] * chunks,
        out_shape=[jax.ShapeDtypeStruct((share, count + extra), f32)] * chunks,
        scratch_shapes=[
            pltpu.VMEM((out, depth), f32),
            pltpu.VMEM((2 * out, depth), bf16),
            pltpu.VMEM((out, count), f32),
            pltpu.VMEM((slots, size, count), f32),
            pltpu.SemaphoreType.DMA((slots,)),
        ],
        compiler_params=pltpu.CompilerParams(vmem_limit_bytes=VMEM_LIMIT),
        cost_estimate=pl.CostEstimate(
            flops=6 * out * depth * count, bytes_accessed=4 * depth * count, transcendentals=0
        ),
        name=name,
    )(*pieces, weights)


def across(weights, pieces, places, out, first, count, name):
    width = weights.shape[1]
    size = block_of(count, 512)
    n_pieces = len(pieces)
    half = out // 2

    def kernel(*refs):
        piece_refs = refs[:n_pieces]
        w_ref, theirs, mine, full, parts, total, held, sems = refs[n_pieces:]

        def copy(i, slot):
            return pltpu.make_async_copy(w_ref.at[pl.ds(first + i * size, size)], held.at[slot], sems.at[slot])

        def use(i, slot):
            high, low = split(held[slot])
            both = dot(parts[...], high, NT)
            at = pl.ds(pl.multiple_of(i * size, size), size)
            total[:, at] = both[:out] + both[out:] + dot(parts[0:out], low, NT)

        stage(None, piece_refs, places, full, parts)
        stream(count // size, copy, use)
        core = core_of()
        theirs[...] = total[rows_at((1 - core) * half, half), :]
        mine[...] = total[rows_at(core * half, half), :]

    slots = min(SLOTS, count // size)
    return pl.pallas_call(
        kernel,
        in_specs=[WHOLE] * n_pieces + [pl.BlockSpec(memory_space=pl.ANY)],
        out_specs=[WHOLE] * 2,
        out_shape=[jax.ShapeDtypeStruct((half, count), f32)] * 2,
        scratch_shapes=[
            pltpu.VMEM((out, width), f32),
            pltpu.VMEM((2 * out, width), bf16),
            pltpu.VMEM((out, count), f32),
            pltpu.VMEM((slots, size, width), f32),
            pltpu.SemaphoreType.DMA((slots,)),
        ],
        compiler_params=pltpu.CompilerParams(vmem_limit_bytes=VMEM_LIMIT),
        cost_estimate=pl.CostEstimate(
            flops=6 * out * width * count, bytes_accessed=4 * width * count, transcendentals=0
        ),
        name=name,
    )(*pieces, weights)


def tile_and_logits(features, centers, coeffs):
    rows, width = features.shape
    count = centers.shape[0]
    out = coeffs.shape[0]
    half = out // 2
    size = block_of(rows, 512)
    gain = 2.0 * LOG2E / width

    def kernel(x_ref, c_ref, a_ref, tile_ref, theirs, mine, wide, norms, parts, total):
        @pl.when(pl.program_id(0) == 0)
        def _():
            c = c_ref[...]
            high, mid, low = split3(c * (2.0 * gain))
            wide[...] = jnp.concatenate([high, high, mid, mid, low, high], axis=1)
            norms[...] = lax.dot_general(
                jnp.full((8, width), gain, f32),
                c * c,
                NT,
                precision=lax.Precision.HIGHEST,
                preferred_element_type=f32,
            )
            high, low = split(a_ref[...])
            parts[0:out] = high
            parts[out : 2 * out] = low

        x = x_ref[...]
        high, mid, low = split3(x)
        cross = dot(jnp.concatenate([high, mid, high, mid, high, low], axis=1), wide[...], NT)
        norm = jnp.sum(x * x, axis=1, keepdims=True) * gain
        tile = jnp.exp2((cross - norm) - norms[0:1, :])
        tile_ref[...] = tile
        high, low = split(tile)
        both = dot(parts[...], high, NT)
        total[...] = both[:out] + both[out:] + dot(parts[0:out], low, NT)
        core = core_of()
        theirs[...] = total[rows_at((1 - core) * half, half), :]
        mine[...] = total[rows_at(core * half, half), :]

    return pl.pallas_call(
        kernel,
        grid=(rows // size,),
        in_specs=[
            pl.BlockSpec((size, width), lambda i: (i, 0)),
            pl.BlockSpec((count, width), lambda i: (0, 0)),
            pl.BlockSpec((out, count), lambda i: (0, 0)),
        ],
        out_specs=[
            pl.BlockSpec((size, count), lambda i: (i, 0)),
            pl.BlockSpec((half, size), lambda i: (0, i)),
            pl.BlockSpec((half, size), lambda i: (0, i)),
        ],
        out_shape=[
            jax.ShapeDtypeStruct((rows, count), f32),
            jax.ShapeDtypeStruct((half, rows), f32),
            jax.ShapeDtypeStruct((half, rows), f32),
        ],
        scratch_shapes=[
            pltpu.VMEM((count, 6 * width), bf16),
            pltpu.VMEM((8, count), f32),
            pltpu.VMEM((2 * out, count), bf16),
            pltpu.VMEM((out, size), f32),
        ],
        compiler_params=pltpu.CompilerParams(vmem_limit_bytes=VMEM_LIMIT),
        cost_estimate=pl.CostEstimate(
            flops=12 * rows * width * count, bytes_accessed=4 * rows * count, transcendentals=rows * count
        ),
        name="tile_and_logits",
    )(features, centers, coeffs)


def add_and_cut(first, second, chips, name):
    half, count = first.shape
    share = half // chips

    def kernel(a_ref, b_ref, *outs):
        chip = chip_of()
        for k in range(chips):
            at = rows_at((chip ^ k) * share, share)
            outs[k][...] = a_ref[at, :] + b_ref[at, :]

    return pl.pallas_call(
        kernel,
        in_specs=[WHOLE] * 2,
        out_specs=[WHOLE] * chips,
        out_shape=[jax.ShapeDtypeStruct((share, count), f32)] * chips,
        name=name,
    )(first, second)


def assemble(pieces, places, shape, name):
    n_pieces = len(pieces)

    def kernel(*refs):
        for piece, (start, lanes) in zip(refs[:n_pieces], places()):
            refs[n_pieces][rows_at(start, piece.shape[0]), lanes] = piece[...]

    return pl.pallas_call(
        kernel,
        in_specs=[WHOLE] * n_pieces,
        out_specs=WHOLE,
        out_shape=jax.ShapeDtypeStruct(shape, f32),
        name=name,
    )(*pieces)


def swap(x, axis, mask):
    size = lax.axis_size(axis)
    return lax.ppermute(x, axis, [(i, i ^ mask) for i in range(size)])


def body(features, centers, labels, coeffs, precond):
    depth_ranks = lax.axis_size("rows")
    chips = lax.axis_size("centers") // 2
    rows_total = features.shape[0] * depth_ranks
    count, out = coeffs.shape
    center_total = count * lax.axis_size("centers")
    p_rows = precond.shape[0]
    half = out // 2
    share = out // depth_ranks
    part = half // chips
    cols = count // 2
    row_half = p_rows // 2

    rank = lax.axis_index("rows")
    core = core_of()
    targets = lax.dynamic_slice_in_dim(labels.T, core * half, half, 0).astype(f32)
    a = coeffs.T
    a_share = lax.dynamic_slice_in_dim(a, rank * share, share, 0)

    def rank_of(k):
        return lax.axis_index("rows") ^ k

    def core_places():
        me = core_of()
        return [(me * half, slice(None)), ((1 - me) * half, slice(None))]

    def rank_places():
        return [(rank_of(k) * share, slice(None)) for k in range(depth_ranks)]

    def rank_places_cols():
        return [
            (rank_of(k) * share, slice(h * cols, (h + 1) * cols)) for h in range(2) for k in range(depth_ranks)
        ]

    def fwd_places():
        me, chip = core_of(), chip_of()
        return [
            (who * half + (chip ^ k) * part, slice(h * row_half, (h + 1) * row_half))
            for h in range(2)
            for who in (me, 1 - me)
            for k in range(chips)
        ]

    a_pieces = None
    for step in range(STEPS):
        if step == 0:
            tile, theirs, mine = tile_and_logits(features, centers, a)
        else:
            theirs, mine = across(tile, a_pieces, rank_places_cols, out, 0, tile.shape[0], "logits")
        logits = mine + swap(theirs, "centers", 1)
        full = logits
        for k in range(1, chips):
            full = full + swap(logits, "centers", 2 * k)
        resid = (jax.nn.sigmoid(full) - targets) / rows_total
        cuts = down(
            tile, [resid, swap(resid, "centers", 1)], core_places, out, depth_ranks, rank_of, 0, count, False, "grad"
        )
        grad = cuts[0]
        for k in range(1, depth_ranks):
            grad = grad + swap(cuts[k], "rows", k)
        grads = [grad] + [swap(grad, "rows", k) for k in range(1, depth_ranks)]
        fwd = []
        for h in range(2):
            theirs, mine = across(precond, grads, rank_places, out, h * row_half, row_half, f"fwd{'ab'[h]}")
            cuts = add_and_cut(mine, swap(theirs, "centers", 1), chips, f"cut{'ab'[h]}")
            total = cuts[0]
            for k in range(1, chips):
                total = total + swap(cuts[k], "centers", 2 * k)
            own = [total] + [swap(total, "centers", 2 * k) for k in range(1, chips)]
            other = swap(jnp.concatenate(own, axis=0), "centers", 1)
            fwd += own + [other[k * part : (k + 1) * part] for k in range(chips)]
        scale = None
        updated = []
        for h in range(2):
            cuts = down(
                precond, fwd, fwd_places, out, depth_ranks, rank_of, h * cols, cols, h == 0, f"back{'ab'[h]}"
            )
            back = cuts[0]
            for k in range(1, depth_ranks):
                back = back + swap(cuts[k], "rows", k)
            if h == 0:
                scale = step_size / jnp.sqrt(back[0, cols] / (center_total * out) + epsilon)
                back = back[:, :cols]
            updated.append(a_share[:, h * cols : (h + 1) * cols] - scale * back)
        a_pieces = [u if k == 0 else swap(u, "rows", k) for u in updated for k in range(depth_ranks)]
        a_share = jnp.concatenate(updated, axis=1)
    return assemble(a_pieces, rank_places_cols, (out, count), "result").T


def plain_tile(rows_x, centers_x):
    width = rows_x.shape[1]
    left = jnp.sum(rows_x * rows_x, axis=1)
    right = jnp.sum(centers_x * centers_x, axis=1)
    cross = jnp.dot(rows_x, centers_x.T, precision=lax.Precision.HIGHEST)
    return jnp.exp(-2.0 * (left[:, None] + right[None, :] - 2.0 * cross) / width)


def plain_body(features, centers, labels, coeffs, precond):
    rows_total = features.shape[0] * lax.axis_size("rows")
    center_total = coeffs.shape[0] * lax.axis_size("centers")
    targets = labels.astype(f32)
    share_rows = features.shape[0] // lax.axis_size("centers")
    highest = lax.Precision.HIGHEST
    tile = plain_tile(features, centers)
    for step in range(STEPS):
        part = jnp.dot(tile, coeffs, precision=highest)
        share = lax.psum_scatter(part, "centers", scatter_dimension=0, tiled=True)
        offset = lax.axis_index("centers") * share_rows
        share_y = lax.dynamic_slice_in_dim(targets, offset, share_rows, 0)
        share_resid = (jax.nn.sigmoid(share) - share_y) / rows_total
        resid = lax.all_gather(share_resid, "centers", axis=0, tiled=True)
        grad = lax.psum(lax.dot_general(tile, resid, (((0,), (0,)), ((), ())), precision=highest), "rows")
        fwd = lax.psum(jnp.dot(precond, grad, precision=highest), "centers")
        back = lax.psum(lax.dot_general(precond, fwd, (((0,), (0,)), ((), ())), precision=highest), "rows")
        total = lax.psum(jnp.sum(fwd * fwd), "rows")
        scale = step_size / jnp.sqrt(total / (center_total * fwd.shape[1]) + epsilon)
        coeffs = coeffs - scale * back
    return coeffs


def fits(ranks, cols, features, coeffs, precond):
    if cols % 2 or ranks & (ranks - 1) or cols & (cols - 1):
        return False
    out = coeffs.shape[1]
    lanes = (features.shape[0] // ranks, coeffs.shape[0] // cols // 2, precond.shape[0] // ranks // 2)
    return out % (8 * ranks) == 0 and out % (8 * cols) == 0 and all(n % 128 == 0 for n in lanes)


def solution(mesh):
    in_specs = (
        P("rows", None),
        P("centers", None),
        P("rows", None),
        P("centers", None),
        P("rows", "centers"),
    )
    out_specs = P("centers", None)

    def program(features, centers, labels, coeffs, precond):
        fit = fits(mesh.shape["rows"], mesh.shape["centers"], features, coeffs, precond)
        one = jax.shard_map(
            body if fit else plain_body, mesh=mesh, in_specs=in_specs, out_specs=out_specs, check_vma=False
        )
        return one(features, centers, labels, coeffs, precond)

    return program
```

time: 612 us -> 284 us (0.46); the launches traced: 603 us -> 283 us
  waiting for transfers between devices: 334 us -> 80.6 us
  matrix products: 198 us -> 0 us
  starting transfers between devices: 0.3 us -> 91.5 us
  Pallas kernels: 0 us -> 85.9 us
  blocking collectives: 44.4 us -> 0 us
  local copies, waits for them, and re-layouts: 3.23 us -> 18.4 us
  between operations: 15.1 us -> 1.92 us
    psum x6 -> x0, waiting for transfers between devices: 263 us -> none  [the longest x2 112 us: body(): lax.psum(jnp.dot(precond, grad, precision=lax.Precision.HIGHEST), 'centers')]
    dot_general x9 -> x0, matrix products: 198 us -> none  [the longest x2 80.8 us: body(): jnp.dot(precond, grad, precision=lax.Precision.HIGHEST)]
    ppermute x0 -> x78, starting transfers between devices: none -> 91.5 us  [swap(): return lax.ppermute(x, axis, [(i, i ^ mask) for i in range(size)])]
    pallas_call x0 -> x17, Pallas kernels: none -> 85.9 us  [the longest x5 36 us: across(): pl.pallas_call(kernel, in_specs=[WHOLE] * n_pieces + [pl.BlockSpec(memory...]
    ppermute x0 -> x78, waiting for transfers between devices: none -> 80.6 us  [swap(): return lax.ppermute(x, axis, [(i, i ^ mask) for i in range(size)])]
    reduce_scatter x2 -> x0, waiting for transfers between devices: 70.1 us -> none  [body(): lax.psum_scatter(partial_logits(jnp.int32(0), share_rows * lax.axis_size(...]
    psum x2 -> x0, blocking collectives: 24.8 us -> none  [body(): total = lax.psum(local_square, 'rows')]
    all_gather x2 -> x0, blocking collectives: 19.6 us -> none  [body(): resid = lax.all_gather(share_resid, 'centers', axis=0, tiled=True)]
  transfers between devices with their start and end apart: 8 -> 78, of which waited for: 8 -> 36; matrix products, arithmetic and copies ran while one was open for 0% -> 2% of each run, Pallas kernels for 0% -> 13%
where the time goes in v1:
time: 284 us; the launch traced here: 283 us
  starting transfers between devices  91.5 us (32%)
  Pallas kernels  85.9 us (30%)
  waiting for transfers between devices  80.6 us (28%)
  local copies, waits for them, and re-layouts  18.4 us (6%)
  other arithmetic  4.72 us (2%)
    ppermute x78, starting transfers between devices, swap(): return lax.ppermute(x, axis, [(i, i ^ mask) for i in range(size)])  91.5 us
    ppermute x78, waiting for transfers between devices, swap(): return lax.ppermute(x, axis, [(i, i ^ mask) for i in range(size)])  80.6 us
    pallas_call x5, Pallas kernels, across(): pl.pallas_call(kernel, in_specs=[WHOLE] * n_pieces + [pl.BlockSpec(memory...  36 us
    pallas_call x6, Pallas kernels, down(): pl.pallas_call(kernel, in_specs=[WHOLE] * n_pieces + [pl.BlockSpec(memory...  33.4 us
    unnamed x48, local copies, waits for them, and re-layouts  16.4 us
    pallas_call x1, Pallas kernels, tile_and_logits(): pl.pallas_call(kernel, grid=(rows // size,), in_specs=[pl.BlockSpec((size...  7.58 us
    pallas_call x4, Pallas kernels, add_and_cut(): pl.pallas_call(kernel, in_specs=[WHOLE] * 2, out_specs=[WHOLE] * chips, o...  6.96 us
  transfers between devices with their start and end apart: 78, of which 36 were waited for; matrix products, arithmetic and copies ran while one was open for 2% of the time, Pallas kernels for 13%

profile of v1, /device:TPU:0, one launch (start us, length us, event | category | flops | bytes accessed | tf_op | source)
XLA Modules:
  0.0 283.0 jit_solution(9677259427354593998)
XLA Ops:
  3.3 7.6 %tile_and_logits.1 = (f32[1024,2048]{1,0:T(8,128)S(1)}, f32[32,1024]{1,0:T(8,128)S(1)}, f32[32,1024]{1,0:T(8,128)S(1)}) custom-call(f32[1024,128]{1,0:T(8,128)S(1)} %copy-done.8, f32[2048,128]{1,0:T(8,128)S(1)} %copy-done.7, f32[64,2048]{1,0:T(8,128)S(1)} %bitcast.15), custom_call_target="tpu_custom_call" | custom-call | flops 3221225472 | bytes 8388608 | tf_op jit(solution)/shard_map/tile_and_logits/pallas_call | solution.py:226
  10.9 3.3 %copy-done = f32[1024,2048]{1,0:T(8,128)} copy-done((f32[1024,2048]{1,0:T(8,128)}, f32[1024,2048]{1,0:T(8,128)S(1)}, u32[]{:S(2)}) %copy-start) | copy-done | bytes 8388632
  15.7 2.9 %collective-permute-start.1 = (f32[32,1024]{1,0:T(8,128)S(1)}, f32[32,1024]{1,0:T(8,128)S(1)}, u32[]{:S(2)}, u32[]{:S(2)}) collective-permute-start(f32[32,1024]{1,0:T(8,128)S(1)} %add.135), channel_id=1, source_target_pairs={{0,2},{1,3},{2,0},{3,1},{4,6},{5,7},{6,4},{7,5},{8,10},{9,11},{10,... | collective-permute-start | bytes 393224 | tf_op jit(solution)/shard_map/ppermute | solution.py:295
  20.2 2.4 collective-permute-done.1
  22.5 4.2 %collective-permute-done.2 = f32[32,1024]{1,0:T(8,128)S(1)} collective-permute-done((f32[32,1024]{1,0:T(8,128)S(1)}, f32[32,1024]{1,0:T(8,128)S(1)}, u32[]{:S(2)}, u32[]{:S(2)}) %collective-permute-start.2) | collective-permute-done | bytes 131104 | tf_op jit(solution)/shard_map/ppermute | solution.py:295
  29.1 3.4 %copy-done.1 = f32[1024,2048]{1,0:T(8,128)S(1)} copy-done((f32[1024,2048]{1,0:T(8,128)S(1)}, f32[1024,2048]{1,0:T(8,128)}, u32[]{:S(2)}) %copy-start.1) | copy-done | bytes 8388632
  32.5 2.6 grad.2
  36.7 2.6 collective-permute-start.6
  39.5 3.1 %collective-permute-done.5 = f32[16,2048]{1,0:T(8,128)S(1)} collective-permute-done((f32[16,2048]{1,0:T(8,128)S(1)}, f32[16,2048]{1,0:T(8,128)S(1)}, u32[]{:S(2)}, u32[]{:S(2)}) %collective-permute-start.5) | collective-permute-done | bytes 131104 | tf_op jit(solution)/shard_map/ppermute | solution.py:295
  42.7 7.0 %collective-permute-done.6 = f32[16,2048]{1,0:T(8,128)S(1)} collective-permute-done((f32[16,2048]{1,0:T(8,128)S(1)}, f32[16,2048]{1,0:T(8,128)S(1)}, u32[]{:S(2)}, u32[]{:S(2)}) %collective-permute-start.6) | collective-permute-done | bytes 131104 | tf_op jit(solution)/shard_map/ppermute | solution.py:295
  49.7 2.5 collective-permute-start.10
  54.1 3.7 %collective-permute-done.10.refs_3_ = f32[16,2048]{1,0:T(8,128)S(1)} collective-permute-done((f32[16,2048]{1,0:T(8,128)S(1)}, f32[16,2048]{1,0:T(8,128)S(1)}, u32[]{:S(2)}, u32[]{:S(2)}) %collective-permute-start.10) | collective-permute-done | bytes 131104 | tf_op jit(solution)/shard_map/ppermute | solution.py:295
  58.5 4.9 %collective-permute-done.9.refs_2_ = f32[16,2048]{1,0:T(8,128)S(1)} collective-permute-done((f32[16,2048]{1,0:T(8,128)S(1)}, f32[16,2048]{1,0:T(8,128)S(1)}, u32[]{:S(2)}, u32[]{:S(2)}) %collective-permute-start.9) | collective-permute-done | bytes 131104 | tf_op jit(solution)/shard_map/ppermute | solution.py:295
  63.5 8.1 %fwdb.2 = (f32[32,2048]{1,0:T(8,128)S(1)}, f32[32,2048]{1,0:T(8,128)S(1)}) custom-call(f32[16,2048]{1,0:T(8,128)S(1)} %add_add_fusion.1.refs_0_, f32[16,2048]{1,0:T(8,128)S(1)} %collective-permute-done.8.refs_1_, f32[16,2048]{1,0:T(8,128)S(1)} %collective-permute-done.9.refs_2_, f32[16,2048]{1,0:T(8,128)S(1)} %collective-permute-done.10.refs_3_, ...), custom_call_target="tpu_custom_call" | custom-call | flops 1610612736 | bytes 16777216 | tf_op jit(solution)/shard_map/fwdb/pallas_call | solution.py:168
  72.3 8.1 %fwda.2 = (f32[32,2048]{1,0:T(8,128)S(1)}, f32[32,2048]{1,0:T(8,128)S(1)}) custom-call(f32[16,2048]{1,0:T(8,128)S(1)} %add_add_fusion.1.refs_0_, f32[16,2048]{1,0:T(8,128)S(1)} %collective-permute-done.8.refs_1_, f32[16,2048]{1,0:T(8,128)S(1)} %collective-permute-done.9.refs_2_, f32[16,2048]{1,0:T(8,128)S(1)} %collective-permute-done.10.refs_3_, ...), custom_call_target="tpu_custom_call" | custom-call | flops 1610612736 | bytes 16777216 | tf_op jit(solution)/shard_map/fwda/pallas_call | solution.py:168
  107.8 7.3 %backa.2 = (f32[16,1152]{1,0:T(8,128)S(1)}, f32[16,1152]{1,0:T(8,128)S(1)}, f32[16,1152]{1,0:T(8,128)S(1)}, f32[16,1152]{1,0:T(8,128)S(1)}) custom-call(f32[8,2048]{1,0:T(8,128)S(1)} %add_add_fusion.7.refs_0_, f32[8,2048]{1,0:T(8,128)S(1)} %collective-permute-done.15.refs_1_, f32[8,2048]{1,0:T(8,128)S(1)} %collective-permute-done.16.refs_2_, ...), custom_call_target="tpu_custom_call" | custom-call | flops 1610612736 | bytes 16777216 | tf_op jit(solution)/shard_map/backa/pallas_call | solution.py:122
  115.2 3.0 %collective-permute-start.28 = (f32[16,1152]{1,0:T(8,128)S(1)}, f32[16,1152]{1,0:T(8,128)S(1)}, u32[]{:S(2)}, u32[]{:S(2)}) collective-permute-start(f32[16,1152]{1,0:T(8,128)S(1)} %get-tuple-element.79), channel_id=1, source_target_pairs={{0,16},{8,24},{16,0},{24,8},{1,17},{9,25},{17,1},{25,9},{2,18},{10... | collective-permute-start | bytes 221192 | tf_op jit(solution)/shard_map/ppermute | solution.py:295
  119.5 6.9 %backb.2 = (f32[16,1024]{1,0:T(8,128)S(1)}, f32[16,1024]{1,0:T(8,128)S(1)}, f32[16,1024]{1,0:T(8,128)S(1)}, f32[16,1024]{1,0:T(8,128)S(1)}) custom-call(f32[8,2048]{1,0:T(8,128)S(1)} %add_add_fusion.7.refs_0_, f32[8,2048]{1,0:T(8,128)S(1)} %collective-permute-done.15.refs_1_, f32[8,2048]{1,0:T(8,128)S(1)} %collective-permute-done.16.refs_2_, ...), custom_call_target="tpu_custom_call" | custom-call | flops 1610612736 | bytes 16777216 | tf_op jit(solution)/shard_map/backb/pallas_call | solution.py:122
  126.6 3.0 %collective-permute-start.34 = (f32[16,1024]{1,0:T(8,128)S(1)}, f32[16,1024]{1,0:T(8,128)S(1)}, u32[]{:S(2)}, u32[]{:S(2)}) collective-permute-start(f32[16,1024]{1,0:T(8,128)S(1)} %get-tuple-element.83), channel_id=1, source_target_pairs={{0,16},{8,24},{16,0},{24,8},{1,17},{9,25},{17,1},{25,9},{2,18},{10... | collective-permute-start | bytes 196616 | tf_op jit(solution)/shard_map/ppermute | solution.py:295
  137.8 2.4 collective-permute-start.32
  148.8 3.6 %logits.1 = (f32[32,1024]{1,0:T(8,128)S(1)}, f32[32,1024]{1,0:T(8,128)S(1)}) custom-call(f32[16,1024]{1,0:T(8,128)S(1)} %get-tuple-element.128.refs_0_, f32[16,1024]{1,0:T(8,128)S(1)} %collective-permute-done.30.refs_1_, f32[16,1024]{1,0:T(8,128)S(1)} %collective-permute-done.31.refs_2_, f32[16,1024]{1,0:T(8,128)S(1)} %collective-permute-done.32.refs_3_, ...), custom_call_target="tpu_custom_call" | custom-call | flops 805306368 | bytes 8388608 | tf_op jit(solution)/shard_map/logits/pallas_call | solution.py:168
  157.4 2.4 collective-permute-done.40
  159.8 3.6 %collective-permute-done.41 = f32[32,1024]{1,0:T(8,128)S(1)} collective-permute-done((f32[32,1024]{1,0:T(8,128)S(1)}, f32[32,1024]{1,0:T(8,128)S(1)}, u32[]{:S(2)}, u32[]{:S(2)}) %collective-permute-start.41) | collective-permute-done | bytes 131104 | tf_op jit(solution)/shard_map/ppermute | solution.py:295
  165.0 2.6 grad.3
  172.0 3.4 %collective-permute-done.44 = f32[16,2048]{1,0:T(8,128)S(1)} collective-permute-done((f32[16,2048]{1,0:T(8,128)S(1)}, f32[16,2048]{1,0:T(8,128)S(1)}, u32[]{:S(2)}, u32[]{:S(2)}) %collective-permute-start.44) | collective-permute-done | bytes 131104 | tf_op jit(solution)/shard_map/ppermute | solution.py:295
  175.4 5.7 %collective-permute-done.45 = f32[16,2048]{1,0:T(8,128)S(1)} collective-permute-done((f32[16,2048]{1,0:T(8,128)S(1)}, f32[16,2048]{1,0:T(8,128)S(1)}, u32[]{:S(2)}, u32[]{:S(2)}) %collective-permute-start.45) | collective-permute-done | bytes 131104 | tf_op jit(solution)/shard_map/ppermute | solution.py:295
  181.2 2.4 collective-permute-start.47
  187.9 7.8 %collective-permute-done.48.refs_2_ = f32[16,2048]{1,0:T(8,128)S(1)} collective-permute-done((f32[16,2048]{1,0:T(8,128)S(1)}, f32[16,2048]{1,0:T(8,128)S(1)}, u32[]{:S(2)}, u32[]{:S(2)}) %collective-permute-start.48) | collective-permute-done | bytes 131104 | tf_op jit(solution)/shard_map/ppermute | solution.py:295
  195.7 8.1 %fwdb.3 = (f32[32,2048]{1,0:T(8,128)S(1)}, f32[32,2048]{1,0:T(8,128)S(1)}) custom-call(f32[16,2048]{1,0:T(8,128)S(1)} %add_add_fusion.refs_0_, f32[16,2048]{1,0:T(8,128)S(1)} %collective-permute-done.47.refs_1_, f32[16,2048]{1,0:T(8,128)S(1)} %collective-permute-done.48.refs_2_, f32[16,2048]{1,0:T(8,128)S(1)} %collective-permute-done.49.refs_3_, ...), custom_call_target="tpu_custom_call" | custom-call | flops 1610612736 | bytes 16777216 | tf_op jit(solution)/shard_map/fwdb/pallas_call | solution.py:168
  204.5 8.1 %fwda.3 = (f32[32,2048]{1,0:T(8,128)S(1)}, f32[32,2048]{1,0:T(8,128)S(1)}) custom-call(f32[16,2048]{1,0:T(8,128)S(1)} %add_add_fusion.refs_0_, f32[16,2048]{1,0:T(8,128)S(1)} %collective-permute-done.47.refs_1_, f32[16,2048]{1,0:T(8,128)S(1)} %collective-permute-done.48.refs_2_, f32[16,2048]{1,0:T(8,128)S(1)} %collective-permute-done.49.refs_3_, ...), custom_call_target="tpu_custom_call" | custom-call | flops 1610612736 | bytes 16777216 | tf_op jit(solution)/shard_map/fwda/pallas_call | solution.py:168
  239.6 7.2 %backa.3 = (f32[16,1152]{1,0:T(8,128)S(1)}, f32[16,1152]{1,0:T(8,128)S(1)}, f32[16,1152]{1,0:T(8,128)S(1)}, f32[16,1152]{1,0:T(8,128)S(1)}) custom-call(f32[8,2048]{1,0:T(8,128)S(1)} %add_add_fusion.5.refs_0_, f32[8,2048]{1,0:T(8,128)S(1)} %collective-permute-done.54.refs_1_, f32[8,2048]{1,0:T(8,128)S(1)} %collective-permute-done.55.refs_2_, ...), custom_call_target="tpu_custom_call" | custom-call | flops 1610612736 | bytes 16777216 | tf_op jit(solution)/shard_map/backa/pallas_call | solution.py:122
  251.4 6.8 %backb.3 = (f32[16,1024]{1,0:T(8,128)S(1)}, f32[16,1024]{1,0:T(8,128)S(1)}, f32[16,1024]{1,0:T(8,128)S(1)}, f32[16,1024]{1,0:T(8,128)S(1)}) custom-call(f32[8,2048]{1,0:T(8,128)S(1)} %add_add_fusion.5.refs_0_, f32[8,2048]{1,0:T(8,128)S(1)} %collective-permute-done.54.refs_1_, f32[8,2048]{1,0:T(8,128)S(1)} %collective-permute-done.55.refs_2_, ...), custom_call_target="tpu_custom_call" | custom-call | flops 1610612736 | bytes 16777216 | tf_op jit(solution)/shard_map/backb/pallas_call | solution.py:122
  (216 shorter events, 130.4 us)
Async XLA Ops:
  18.6 8.1 %collective-permute-start.2 = (f32[32,1024]{1,0:T(8,128)S(1)}, f32[32,1024]{1,0:T(8,128)S(1)}, u32[]{:S(2)}, u32[]{:S(2)}) collective-permute-start(f32[32,1024]{1,0:T(8,128)S(1)} %add.135), channel_id=1, source_target_pairs={{0,4},{1,5},{2,6},{3,7},{4,0},{5,1},{6,2},{7,3},{8,12},{9,13},{10,... | collective-permute-start | bytes 393224 | tf_op jit(solution)/shard_map/ppermute | solution.py:295
  35.1 7.6 %collective-permute-start.5 = (f32[16,2048]{1,0:T(8,128)S(1)}, f32[16,2048]{1,0:T(8,128)S(1)}, u32[]{:S(2)}, u32[]{:S(2)}) collective-permute-start(f32[16,2048]{1,0:T(8,128)S(1)} %get-tuple-element.62), channel_id=1, source_target_pairs={{0,8},{8,0},{16,24},{24,16},{1,9},{9,1},{17,25},{25,17},{2,10},{10... | collective-permute-start | bytes 393224 | tf_op jit(solution)/shard_map/ppermute | solution.py:295
  36.7 12.9 %collective-permute-start.6 = (f32[16,2048]{1,0:T(8,128)S(1)}, f32[16,2048]{1,0:T(8,128)S(1)}, u32[]{:S(2)}, u32[]{:S(2)}) collective-permute-start(f32[16,2048]{1,0:T(8,128)S(1)} %get-tuple-element.63), channel_id=1, source_target_pairs={{0,16},{8,24},{16,0},{24,8},{1,17},{9,25},{17,1},{25,9},{2,18},{10... | collective-permute-start | bytes 393224 | tf_op jit(solution)/shard_map/ppermute | solution.py:295
  39.3 10.3 %collective-permute-start.7 = (f32[16,2048]{1,0:T(8,128)S(1)}, f32[16,2048]{1,0:T(8,128)S(1)}, u32[]{:S(2)}, u32[]{:S(2)}) collective-permute-start(f32[16,2048]{1,0:T(8,128)S(1)} %get-tuple-element.64), channel_id=1, source_target_pairs={{0,24},{8,16},{16,8},{24,0},{1,25},{9,17},{17,9},{25,1},{2,26},{10... | collective-permute-start | bytes 393224 | tf_op jit(solution)/shard_map/ppermute | solution.py:295
  49.7 8.2 %collective-permute-start.10 = (f32[16,2048]{1,0:T(8,128)S(1)}, f32[16,2048]{1,0:T(8,128)S(1)}, u32[]{:S(2)}, u32[]{:S(2)}) collective-permute-start(f32[16,2048]{1,0:T(8,128)S(1)} %add_add_fusion.1.refs_0_), channel_id=1, source_target_pairs={{0,24},{8,16},{16,8},{24,0},{1,25},{9,17},{17,9},{25,1},{2,26},{10... | collective-permute-start | bytes 393224 | tf_op jit(solution)/shard_map/ppermute | solution.py:295
  53.6 9.8 %collective-permute-start.9 = (f32[16,2048]{1,0:T(8,128)S(1)}, f32[16,2048]{1,0:T(8,128)S(1)}, u32[]{:S(2)}, u32[]{:S(2)}) collective-permute-start(f32[16,2048]{1,0:T(8,128)S(1)} %add_add_fusion.1.refs_0_), channel_id=1, source_target_pairs={{0,16},{8,24},{16,0},{24,8},{1,17},{9,25},{17,1},{25,9},{2,18},{10... | collective-permute-start | bytes 393224 | tf_op jit(solution)/shard_map/ppermute | solution.py:295
  72.3 9.3 %collective-permute-start.19 = (f32[32,2048]{1,0:T(8,128)S(1)}, f32[32,2048]{1,0:T(8,128)S(1)}, u32[]{:S(2)}, u32[]{:S(2)}) collective-permute-start(f32[32,2048]{1,0:T(8,128)S(1)} %get-tuple-element.72), channel_id=1, source_target_pairs={{0,1},{1,0},{2,3},{3,2},{4,5},{5,4},{6,7},{7,6},{8,9},{9,8},{10,11... | collective-permute-start | bytes 786440 | tf_op jit(solution)/shard_map/ppermute | solution.py:295
  84.1 8.0 %collective-permute-start.20 = (f32[8,2048]{1,0:T(8,128)}, f32[8,2048]{1,0:T(8,128)S(1)}, u32[]{:S(2)}, u32[]{:S(2)}) collective-permute-start(f32[8,2048]{1,0:T(8,128)} %get-tuple-element.74), channel_id=1, source_target_pairs={{0,2},{1,3},{2,0},{3,1},{4,6},{5,7},{6,4},{7,5},{8,10},{9,11},{10,... | collective-permute-start | bytes 196616 | tf_op jit(solution)/shard_map/ppermute | solution.py:295
  85.3 8.2 %collective-permute-start.21 = (f32[8,2048]{1,0:T(8,128)}, f32[8,2048]{1,0:T(8,128)S(1)}, u32[]{:S(2)}, u32[]{:S(2)}) collective-permute-start(f32[8,2048]{1,0:T(8,128)} %get-tuple-element.75), channel_id=1, source_target_pairs={{0,4},{1,5},{2,6},{3,7},{4,0},{5,1},{6,2},{7,3},{8,12},{9,13},{10,... | collective-permute-start | bytes 196616 | tf_op jit(solution)/shard_map/ppermute | solution.py:295
  86.1 7.4 %collective-permute-start.22 = (f32[8,2048]{1,0:T(8,128)}, f32[8,2048]{1,0:T(8,128)S(1)}, u32[]{:S(2)}, u32[]{:S(2)}) collective-permute-start(f32[8,2048]{1,0:T(8,128)} %get-tuple-element.76), channel_id=1, source_target_pairs={{0,6},{1,7},{2,4},{3,5},{4,2},{5,3},{6,0},{7,1},{8,14},{9,15},{10,... | collective-permute-start | bytes 196616 | tf_op jit(solution)/shard_map/ppermute | solution.py:295
  115.1 14.5 %collective-permute-start.27 = (f32[16,1152]{1,0:T(8,128)S(1)}, f32[16,1152]{1,0:T(8,128)S(1)}, u32[]{:S(2)}, u32[]{:S(2)}) collective-permute-start(f32[16,1152]{1,0:T(8,128)S(1)} %get-tuple-element.78), channel_id=1, source_target_pairs={{0,8},{8,0},{16,24},{24,16},{1,9},{9,1},{17,25},{25,17},{2,10},{10... | collective-permute-start | bytes 221192 | tf_op jit(solution)/shard_map/ppermute | solution.py:295
  115.2 15.8 %collective-permute-start.28 = (f32[16,1152]{1,0:T(8,128)S(1)}, f32[16,1152]{1,0:T(8,128)S(1)}, u32[]{:S(2)}, u32[]{:S(2)}) collective-permute-start(f32[16,1152]{1,0:T(8,128)S(1)} %get-tuple-element.79), channel_id=1, source_target_pairs={{0,16},{8,24},{16,0},{24,8},{1,17},{9,25},{17,1},{25,9},{2,18},{10... | collective-permute-start | bytes 221192 | tf_op jit(solution)/shard_map/ppermute | solution.py:295
  118.1 12.8 %collective-permute-start.29 = (f32[16,1152]{1,0:T(8,128)S(1)}, f32[16,1152]{1,0:T(8,128)S(1)}, u32[]{:S(2)}, u32[]{:S(2)}) collective-permute-start(f32[16,1152]{1,0:T(8,128)S(1)} %get-tuple-element.80), channel_id=1, source_target_pairs={{0,24},{8,16},{16,8},{24,0},{1,25},{9,17},{17,9},{25,1},{2,26},{10... | collective-permute-start | bytes 221192 | tf_op jit(solution)/shard_map/ppermute | solution.py:295
  126.6 7.6 %collective-permute-start.34 = (f32[16,1024]{1,0:T(8,128)S(1)}, f32[16,1024]{1,0:T(8,128)S(1)}, u32[]{:S(2)}, u32[]{:S(2)}) collective-permute-start(f32[16,1024]{1,0:T(8,128)S(1)} %get-tuple-element.83), channel_id=1, source_target_pairs={{0,16},{8,24},{16,0},{24,8},{1,17},{9,25},{17,1},{25,9},{2,18},{10... | collective-permute-start | bytes 196616 | tf_op jit(solution)/shard_map/ppermute | solution.py:295
  135.8 8.8 %collective-permute-start.31 = (f32[16,1024]{1,0:T(8,128)S(1)}, f32[16,1024]{1,0:T(8,128)S(1)}, u32[]{:S(2)}, u32[]{:S(2)}) collective-permute-start(f32[16,1024]{1,0:T(8,128)S(1)} %get-tuple-element.128.refs_0_), channel_id=1, source_target_pairs={{0,16},{8,24},{16,0},{24,8},{1,17},{9,25},{17,1},{25,9},{2,18},{10... | collective-permute-start | bytes 196616 | tf_op jit(solution)/shard_map/ppermute | solution.py:295
  155.4 8.1 %collective-permute-start.41 = (f32[32,1024]{1,0:T(8,128)S(1)}, f32[32,1024]{1,0:T(8,128)S(1)}, u32[]{:S(2)}, u32[]{:S(2)}) collective-permute-start(f32[32,1024]{1,0:T(8,128)S(1)} %add.157), channel_id=1, source_target_pairs={{0,4},{1,5},{2,6},{3,7},{4,0},{5,1},{6,2},{7,3},{8,12},{9,13},{10,... | collective-permute-start | bytes 393224 | tf_op jit(solution)/shard_map/ppermute | solution.py:295
  155.8 7.7 %collective-permute-start.42 = (f32[32,1024]{1,0:T(8,128)S(1)}, f32[32,1024]{1,0:T(8,128)S(1)}, u32[]{:S(2)}, u32[]{:S(2)}) collective-permute-start(f32[32,1024]{1,0:T(8,128)S(1)} %add.157), channel_id=1, source_target_pairs={{0,6},{1,7},{2,4},{3,5},{4,2},{5,3},{6,0},{7,1},{8,14},{9,15},{10,... | collective-permute-start | bytes 393224 | tf_op jit(solution)/shard_map/ppermute | solution.py:295
  167.6 7.9 %collective-permute-start.44 = (f32[16,2048]{1,0:T(8,128)S(1)}, f32[16,2048]{1,0:T(8,128)S(1)}, u32[]{:S(2)}, u32[]{:S(2)}) collective-permute-start(f32[16,2048]{1,0:T(8,128)S(1)} %get-tuple-element.88), channel_id=1, source_target_pairs={{0,8},{8,0},{16,24},{24,16},{1,9},{9,1},{17,25},{25,17},{2,10},{10... | collective-permute-start | bytes 393224 | tf_op jit(solution)/shard_map/ppermute | solution.py:295
  168.2 12.9 %collective-permute-start.45 = (f32[16,2048]{1,0:T(8,128)S(1)}, f32[16,2048]{1,0:T(8,128)S(1)}, u32[]{:S(2)}, u32[]{:S(2)}) collective-permute-start(f32[16,2048]{1,0:T(8,128)S(1)} %get-tuple-element.89), channel_id=1, source_target_pairs={{0,16},{8,24},{16,0},{24,8},{1,17},{9,25},{17,1},{25,9},{2,18},{10... | collective-permute-start | bytes 393224 | tf_op jit(solution)/shard_map/ppermute | solution.py:295
  170.2 11.0 %collective-permute-start.46 = (f32[16,2048]{1,0:T(8,128)S(1)}, f32[16,2048]{1,0:T(8,128)S(1)}, u32[]{:S(2)}, u32[]{:S(2)}) collective-permute-start(f32[16,2048]{1,0:T(8,128)S(1)} %get-tuple-element.90), channel_id=1, source_target_pairs={{0,24},{8,16},{16,8},{24,0},{1,25},{9,17},{17,9},{25,1},{2,26},{10... | collective-permute-start | bytes 393224 | tf_op jit(solution)/shard_map/ppermute | solution.py:295
  183.5 12.1 %collective-permute-start.48 = (f32[16,2048]{1,0:T(8,128)S(1)}, f32[16,2048]{1,0:T(8,128)S(1)}, u32[]{:S(2)}, u32[]{:S(2)}) collective-permute-start(f32[16,2048]{1,0:T(8,128)S(1)} %add_add_fusion.refs_0_), channel_id=1, source_target_pairs={{0,16},{8,24},{16,0},{24,8},{1,17},{9,25},{17,1},{25,9},{2,18},{10... | collective-permute-start | bytes 393224 | tf_op jit(solution)/shard_map/ppermute | solution.py:295
  184.6 11.0 %collective-permute-start.49 = (f32[16,2048]{1,0:T(8,128)S(1)}, f32[16,2048]{1,0:T(8,128)S(1)}, u32[]{:S(2)}, u32[]{:S(2)}) collective-permute-start(f32[16,2048]{1,0:T(8,128)S(1)} %add_add_fusion.refs_0_), channel_id=1, source_target_pairs={{0,24},{8,16},{16,8},{24,0},{1,25},{9,17},{17,9},{25,1},{2,26},{10... | collective-permute-start | bytes 393224 | tf_op jit(solution)/shard_map/ppermute | solution.py:295
  204.5 9.3 %collective-permute-start.58 = (f32[32,2048]{1,0:T(8,128)S(1)}, f32[32,2048]{1,0:T(8,128)S(1)}, u32[]{:S(2)}, u32[]{:S(2)}) collective-permute-start(f32[32,2048]{1,0:T(8,128)S(1)} %get-tuple-element.98), channel_id=1, source_target_pairs={{0,1},{1,0},{2,3},{3,2},{4,5},{5,4},{6,7},{7,6},{8,9},{9,8},{10,11... | collective-permute-start | bytes 786440 | tf_op jit(solution)/shard_map/ppermute | solution.py:295
  216.3 7.7 %collective-permute-start.59 = (f32[8,2048]{1,0:T(8,128)}, f32[8,2048]{1,0:T(8,128)S(1)}, u32[]{:S(2)}, u32[]{:S(2)}) collective-permute-start(f32[8,2048]{1,0:T(8,128)} %get-tuple-element.100), channel_id=1, source_target_pairs={{0,2},{1,3},{2,0},{3,1},{4,6},{5,7},{6,4},{7,5},{8,10},{9,11},{10,... | collective-permute-start | bytes 196616 | tf_op jit(solution)/shard_map/ppermute | solution.py:295
  216.8 8.9 %collective-permute-start.60 = (f32[8,2048]{1,0:T(8,128)}, f32[8,2048]{1,0:T(8,128)S(1)}, u32[]{:S(2)}, u32[]{:S(2)}) collective-permute-start(f32[8,2048]{1,0:T(8,128)} %get-tuple-element.101), channel_id=1, source_target_pairs={{0,4},{1,5},{2,6},{3,7},{4,0},{5,1},{6,2},{7,3},{8,12},{9,13},{10,... | collective-permute-start | bytes 196616 | tf_op jit(solution)/shard_map/ppermute | solution.py:295
  218.0 7.7 %collective-permute-start.61 = (f32[8,2048]{1,0:T(8,128)}, f32[8,2048]{1,0:T(8,128)S(1)}, u32[]{:S(2)}, u32[]{:S(2)}) collective-permute-start(f32[8,2048]{1,0:T(8,128)} %get-tuple-element.102), channel_id=1, source_target_pairs={{0,6},{1,7},{2,4},{3,5},{4,2},{5,3},{6,0},{7,1},{8,14},{9,15},{10,... | collective-permute-start | bytes 196616 | tf_op jit(solution)/shard_map/ppermute | solution.py:295
  222.7 7.4 %collective-permute-start.52 = (f32[8,2048]{1,0:T(8,128)}, f32[8,2048]{1,0:T(8,128)S(1)}, u32[]{:S(2)}, u32[]{:S(2)}) collective-permute-start(f32[8,2048]{1,0:T(8,128)} %get-tuple-element.95), channel_id=1, source_target_pairs={{0,4},{1,5},{2,6},{3,7},{4,0},{5,1},{6,2},{7,3},{8,12},{9,13},{10,... | collective-permute-start | bytes 196616 | tf_op jit(solution)/shard_map/ppermute | solution.py:295
  246.8 14.4 %collective-permute-start.66 = (f32[16,1152]{1,0:T(8,128)S(1)}, f32[16,1152]{1,0:T(8,128)S(1)}, u32[]{:S(2)}, u32[]{:S(2)}) collective-permute-start(f32[16,1152]{1,0:T(8,128)S(1)} %get-tuple-element.104), channel_id=1, source_target_pairs={{0,8},{8,0},{16,24},{24,16},{1,9},{9,1},{17,25},{25,17},{2,10},{10... | collective-permute-start | bytes 221192 | tf_op jit(solution)/shard_map/ppermute | solution.py:295
  248.8 13.8 %collective-permute-start.67 = (f32[16,1152]{1,0:T(8,128)S(1)}, f32[16,1152]{1,0:T(8,128)S(1)}, u32[]{:S(2)}, u32[]{:S(2)}) collective-permute-start(f32[16,1152]{1,0:T(8,128)S(1)} %get-tuple-element.105), channel_id=1, source_target_pairs={{0,16},{8,24},{16,0},{24,8},{1,17},{9,25},{17,1},{25,9},{2,18},{10... | collective-permute-start | bytes 221192 | tf_op jit(solution)/shard_map/ppermute | solution.py:295
  250.0 12.6 %collective-permute-start.68 = (f32[16,1152]{1,0:T(8,128)S(1)}, f32[16,1152]{1,0:T(8,128)S(1)}, u32[]{:S(2)}, u32[]{:S(2)}) collective-permute-start(f32[16,1152]{1,0:T(8,128)S(1)} %get-tuple-element.106), channel_id=1, source_target_pairs={{0,24},{8,16},{16,8},{24,0},{1,25},{9,17},{17,9},{25,1},{2,26},{10... | collective-permute-start | bytes 221192 | tf_op jit(solution)/shard_map/ppermute | solution.py:295
  267.5 8.9 %collective-permute-start.76 = (f32[16,1024]{1,0:T(8,128)S(1)}, f32[16,1024]{1,0:T(8,128)S(1)}, u32[]{:S(2)}, u32[]{:S(2)}) collective-permute-start(f32[16,1024]{1,0:T(8,128)S(1)} %multiply_subtract_fusion.refs_4_), channel_id=1, source_target_pairs={{0,16},{8,24},{16,0},{24,8},{1,17},{9,25},{17,1},{25,9},{2,18},{10... | collective-permute-start | bytes 196616 | tf_op jit(solution)/shard_map/ppermute | solution.py:295
  272.0 7.4 %collective-permute-start.70 = (f32[16,1024]{1,0:T(8,128)S(1)}, f32[16,1024]{1,0:T(8,128)S(1)}, u32[]{:S(2)}, u32[]{:S(2)}) collective-permute-start(f32[16,1024]{1,0:T(8,128)S(1)} %fusion.2.refs_0_), channel_id=1, source_target_pairs={{0,16},{8,24},{16,0},{24,8},{1,17},{9,25},{17,1},{25,9},{2,18},{10... | collective-permute-start | bytes 196616 | tf_op jit(solution)/shard_map/ppermute | solution.py:295
  (70 other events, 431.6 us)

commit v2 on v1

v2 whole, which is shorter than its diff:
```python
import functools

import jax
import jax.numpy as jnp
from jax import lax
from jax.experimental import pallas as pl
from jax.experimental.pallas import tpu as pltpu
from jax.sharding import PartitionSpec as P

STEPS = 2
step_size = 0.5
epsilon = 1e-06

f32 = jnp.float32
bf16 = jnp.bfloat16
LOG2E = 1.4426950408889634
NN = (((1,), (0,)), ((), ()))
NT = (((1,), (1,)), ((), ()))
WHOLE = pl.BlockSpec(memory_space=pltpu.VMEM)
FAR = pl.BlockSpec(memory_space=pltpu.HBM)
VMEM_LIMIT = 26 << 20
TILE_LIMIT = 62 << 20
NEAR_LIMIT = 26 << 20
SMALL_LIMIT = 8 << 20
IN_FLIGHT = 12 << 20


def dot(a, b, dims):
    return lax.dot_general(a, b, dims, preferred_element_type=f32)


def split(x):
    high = x.astype(bf16)
    return high, (x - high.astype(f32)).astype(bf16)


def split3(x):
    high = x.astype(bf16)
    rest = x - high.astype(f32)
    mid = rest.astype(bf16)
    return high, mid, (rest - mid.astype(f32)).astype(bf16)


def core_of():
    return lax.rem(lax.axis_index("centers"), 2)


def chip_of():
    return lax.div(lax.axis_index("centers"), 2)


def rows_at(start, count):
    return pl.ds(pl.multiple_of(start, count), count)


def stage(pieces, places, full, parts):
    for piece, (start, lanes) in zip(pieces, places()):
        full[rows_at(start, piece.shape[0]), lanes] = piece[...]
    high, low = split(full[...])
    out = full.shape[0]
    parts[0:out] = high
    parts[out : 2 * out] = low


def block_of(total, most):
    size = min(total, most)
    while total % size:
        size //= 2
    return size


def offset(first, size):
    return first if isinstance(first, int) else pl.multiple_of(first(), size)


def stream(w_ref, held, sems, first, count, size, lanes, use):
    blocks = count // size
    start = offset(first, size)

    def at(i):
        return pl.ds(pl.multiple_of(i * size, size), size)

    def rows(i):
        return pl.ds(pl.multiple_of(start + i * size, size), size)

    def copy(i, slot):
        return pltpu.make_async_copy(w_ref.at[rows(i), lanes], held.at[slot], sems.at[slot])

    slots = min(held.shape[0], blocks)
    for i in range(slots):
        copy(i, i).start()

    def one(i, carry):
        slot = lax.rem(i, slots)
        copy(i, slot).wait()
        use(at(i), held[slot])

        @pl.when(i + slots < blocks)
        def _():
            copy(i + slots, slot).start()

        return carry

    lax.fori_loop(0, blocks, one, 0)


def call(kernel, weights, others, outs, scratch, count, size, n_lanes, out, name, limit):
    n_in, n_out, n_scratch = len(others), len(outs), len(scratch)

    def whole(*refs):
        ins, rest = refs[1 : 1 + n_in], refs[1 + n_in :]
        held, sems = rest[n_out + n_scratch :]
        kernel(refs[0], ins, rest[:n_out], rest[n_out : n_out + n_scratch], held, sems)

    slots = max(2, min(count // size, IN_FLIGHT // (4 * size * n_lanes)))
    scratch = list(scratch) + [pltpu.VMEM((slots, size, n_lanes), f32), pltpu.SemaphoreType.DMA((slots,))]
    return pl.pallas_call(
        whole,
        in_specs=[FAR] + [WHOLE] * n_in,
        out_specs=[WHOLE] * n_out,
        out_shape=[jax.ShapeDtypeStruct(shape, f32) for shape in outs],
        scratch_shapes=scratch,
        compiler_params=pltpu.CompilerParams(vmem_limit_bytes=limit),
        cost_estimate=pl.CostEstimate(
            flops=6 * out * count * n_lanes, bytes_accessed=4 * count * n_lanes, transcendentals=0
        ),
        name=name,
    )(weights, *others)


def down(weights, pieces, places, out, first, count, lanes, name, chunks=0, before=None, squares=None, limit=VMEM_LIMIT):
    size = block_of(count, 512)
    n_lanes = lanes.stop - lanes.start
    n_pieces = len(pieces)
    share = out // chunks if chunks else out
    gives = isinstance(squares, str)
    takes = squares is not None and not gives
    extra = 128 if takes else 0
    others = list(pieces) + ([before] if before is not None else []) + ([squares] if takes else [])
    outs = [(share, n_lanes + extra)] * (chunks or 1) + ([(8, 128)] if gives else [])

    def kernel(w_ref, ins, out_refs, scratch, held, sems):
        full, parts, total = scratch

        def use(at, block):
            x = parts[:, at]
            high, low = split(block)
            both = dot(x, high, NN)
            total[...] += both[:out] + both[out:] + dot(x[:out], low, NN)

        total[...] = jnp.zeros_like(total) if before is None else ins[n_pieces][...]
        stage(ins[:n_pieces], places, full, parts)
        stream(w_ref, held, sems, first, count, size, lanes, use)
        if not chunks:
            out_refs[0][...] = total[...]
        for k in range(chunks):
            at = rows_at((lax.axis_index("rows") ^ k) * share, share)
            out_refs[k][:, 0:n_lanes] = total[at, :]
        if gives:
            out_refs[-1][...] = jnp.full((8, 128), jnp.sum(full[...] * full[...]), f32)
        if takes:
            sum_sq = jnp.sum(full[...] * full[...]) + jnp.max(ins[-1][0:1, :])
            for k in range(chunks):
                out_refs[k][:, n_lanes : n_lanes + extra] = jnp.full((share, extra), sum_sq, f32)

    scratch = [pltpu.VMEM((out, count), f32), pltpu.VMEM((2 * out, count), bf16), pltpu.VMEM((out, n_lanes), f32)]
    return call(kernel, weights, others, outs, scratch, count, size, n_lanes, out, name, limit)


def across(weights, pieces, places, out, first, count, lanes, name, before=None, halves=False, limit=VMEM_LIMIT):
    width = lanes.stop - lanes.start
    size = block_of(count, 512)
    half = out // 2
    n_pieces = len(pieces)
    outs = [(half, count)] * 2 if halves else [(out, count)]
    others = list(pieces) + ([before] if before is not None else [])

    def kernel(w_ref, ins, out_refs, scratch, held, sems):
        full, parts = scratch[:2]
        total = scratch[2] if halves else out_refs[0]

        def use(at, block):
            high, low = split(block)
            both = dot(parts[...], high, NT)
            sums = both[:out] + both[out:] + dot(parts[0:out], low, NT)
            if before is not None:
                sums = sums + ins[n_pieces][:, pl.ds(pl.multiple_of(offset(first, size) + at.start, size), size)]
            total[:, at] = sums

        stage(ins[:n_pieces], places, full, parts)
        stream(w_ref, held, sems, first, count, size, lanes, use)
        if halves:
            core = core_of()
            out_refs[0][...] = total[rows_at((1 - core) * half, half), :]
            out_refs[1][...] = total[rows_at(core * half, half), :]

    scratch = [pltpu.VMEM((out, width), f32), pltpu.VMEM((2 * out, width), bf16)]
    scratch += [pltpu.VMEM((out, count), f32)] if halves else []
    return call(kernel, weights, others, outs, scratch, count, size, width, out, name, limit)


def tile_and_logits(features, centers, coeffs):
    rows, width = features.shape
    count = centers.shape[0]
    out = coeffs.shape[0]
    half = out // 2
    size = block_of(rows, 512)
    gain = 2.0 * LOG2E / width

    def kernel(x_ref, c_ref, a_ref, tile_ref, theirs, mine, wide, norms, parts, total):
        @pl.when(pl.program_id(0) == 0)
        def _():
            c = c_ref[...]
            high, mid, low = split3(c * (2.0 * gain))
            wide[...] = jnp.concatenate([high, high, mid, mid, low, high], axis=1)
            norms[...] = lax.dot_general(
                jnp.full((8, width), gain, f32),
                c * c,
                NT,
                precision=lax.Precision.HIGHEST,
                preferred_element_type=f32,
            )
            high, low = split(a_ref[...])
            parts[0:out] = high
            parts[out : 2 * out] = low

        x = x_ref[...]
        high, mid, low = split3(x)
        cross = dot(jnp.concatenate([high, mid, high, mid, high, low], axis=1), wide[...], NT)
        norm = jnp.sum(x * x, axis=1, keepdims=True) * gain
        tile = jnp.exp2((cross - norm) - norms[0:1, :])
        tile_ref[...] = tile
        high, low = split(tile)
        both = dot(parts[...], high, NT)
        total[...] = both[:out] + both[out:] + dot(parts[0:out], low, NT)
        core = core_of()
        theirs[...] = total[rows_at((1 - core) * half, half), :]
        mine[...] = total[rows_at(core * half, half), :]

    return pl.pallas_call(
        kernel,
        grid=(rows // size,),
        in_specs=[
            pl.BlockSpec((size, width), lambda i: (i, 0)),
            pl.BlockSpec((count, width), lambda i: (0, 0)),
            pl.BlockSpec((out, count), lambda i: (0, 0)),
        ],
        out_specs=[
            pl.BlockSpec((size, count), lambda i: (i, 0)),
            pl.BlockSpec((half, size), lambda i: (0, i)),
            pl.BlockSpec((half, size), lambda i: (0, i)),
        ],
        out_shape=[
            jax.ShapeDtypeStruct((rows, count), f32),
            jax.ShapeDtypeStruct((half, rows), f32),
            jax.ShapeDtypeStruct((half, rows), f32),
        ],
        scratch_shapes=[
            pltpu.VMEM((count, 6 * width), bf16),
            pltpu.VMEM((8, count), f32),
            pltpu.VMEM((2 * out, count), bf16),
            pltpu.VMEM((out, size), f32),
        ],
        compiler_params=pltpu.CompilerParams(vmem_limit_bytes=TILE_LIMIT),
        cost_estimate=pl.CostEstimate(
            flops=12 * rows * width * count, bytes_accessed=4 * rows * count, transcendentals=rows * count
        ),
        name="tile_and_logits",
    )(features, centers, coeffs)


def add_and_cut(first, second, chips, name):
    rows, count = first.shape
    share = rows // chips

    def kernel(a_ref, b_ref, *outs):
        chip = chip_of()
        for k in range(chips):
            at = rows_at((chip ^ k) * share, share)
            outs[k][...] = a_ref[at, :] + b_ref[at, :]

    return pl.pallas_call(
        kernel,
        in_specs=[WHOLE] * 2,
        out_specs=[WHOLE] * chips,
        out_shape=[jax.ShapeDtypeStruct((share, count), f32)] * chips,
        compiler_params=pltpu.CompilerParams(vmem_limit_bytes=SMALL_LIMIT),
        name=name,
    )(first, second)


def update(cuts, a, elements, scale=None):
    rows, count = a.shape
    n_cuts = len(cuts)

    def kernel(*refs):
        back = refs[0][...]
        for ref in refs[1:n_cuts]:
            back = back + ref[...]
        if scale is None:
            step = step_size / jnp.sqrt(back[0:8, count:] / elements + epsilon)
            refs[-1][...] = step
        else:
            step = refs[n_cuts + 1][...]
        refs[n_cuts + (1 if scale is None else 2)][...] = refs[n_cuts][...] - step[0:1, 0:1] * back[:, 0:count]

    return pl.pallas_call(
        kernel,
        in_specs=[WHOLE] * (n_cuts + (1 if scale is None else 2)),
        out_specs=[WHOLE] * (2 if scale is None else 1),
        out_shape=[jax.ShapeDtypeStruct((rows, count), f32)] + ([jax.ShapeDtypeStruct((8, 128), f32)] if scale is None else []),
        compiler_params=pltpu.CompilerParams(vmem_limit_bytes=SMALL_LIMIT),
        name="update",
    )(*cuts, a, *([] if scale is None else [scale]))


def assemble(pieces, places, shape, name):
    n_pieces = len(pieces)

    def kernel(*refs):
        for piece, (start, lanes) in zip(refs[:n_pieces], places()):
            refs[n_pieces][rows_at(start, piece.shape[0]), lanes] = piece[...]

    return pl.pallas_call(
        kernel,
        in_specs=[WHOLE] * n_pieces,
        out_specs=WHOLE,
        out_shape=jax.ShapeDtypeStruct(shape, f32),
        compiler_params=pltpu.CompilerParams(vmem_limit_bytes=SMALL_LIMIT),
        name=name,
    )(*pieces)


def swap(x, axis, mask):
    size = lax.axis_size(axis)
    return lax.ppermute(x, axis, [(i, i ^ mask) for i in range(size)])


def body(features, centers, labels, coeffs, precond):
    depth_ranks = lax.axis_size("rows")
    chips = lax.axis_size("centers") // 2
    rows_here = features.shape[0]
    rows_total = rows_here * depth_ranks
    count, out = coeffs.shape
    center_total = count * lax.axis_size("centers")
    half = out // 2
    share = out // depth_ranks
    part = out // chips
    cols = count // 2
    row_half = precond.shape[0] // 2
    p_rows = precond.shape[0]
    left, right = slice(0, cols), slice(cols, count)
    every = slice(None)

    rank = lax.axis_index("rows")
    core = core_of()
    targets = lax.dynamic_slice_in_dim(labels.T, core * half, half, 0).astype(f32)
    a = coeffs.T
    a_share = lax.dynamic_slice_in_dim(a, rank * share, share, 0)
    a_halves = [a_share[:, left], a_share[:, right]]

    def core_places():
        me = core_of()
        return [(me * half, every), ((1 - me) * half, every)]

    def rank_places():
        return [((lax.axis_index("rows") ^ k) * share, every) for k in range(depth_ranks)]

    def rank_places_both():
        return [(at, lanes) for lanes in (left, right) for at, _ in rank_places()]

    def chip_places():
        return [((chip_of() ^ k) * part, every) for k in range(chips)]

    def chip_places_both():
        me = core_of()
        lanes = [pl.ds(pl.multiple_of(who * row_half, row_half), row_half) for who in (me, 1 - me)]
        return [(at, both) for both in lanes for at, _ in chip_places()]

    def my_rows():
        return core_of() * row_half

    def other_rows():
        return (1 - core_of()) * row_half

    def to_rank(cuts):
        return [cuts[0]] + [swap(cuts[k], "rows", k) for k in range(1, depth_ranks)]

    def sum_of(cuts):
        total = cuts[0]
        for cut in cuts[1:]:
            total = total + cut
        return total

    def all_rows(x):
        return [x] + [swap(x, "rows", k) for k in range(1, depth_ranks)]

    a_pieces = None
    for step in range(STEPS):
        if step == 0:
            tile, theirs, mine = tile_and_logits(features, centers, a)
        else:
            theirs, mine = across(
                tile, a_pieces, rank_places_both, out, 0, rows_here, slice(0, count), "logits", halves=True, limit=NEAR_LIMIT
            )
        logits = mine + swap(theirs, "centers", 1)
        full = logits
        for k in range(1, chips):
            full = full + swap(logits, "centers", 2 * k)
        resid = (jax.nn.sigmoid(full) - targets) / rows_total
        resids = [resid, swap(resid, "centers", 1)]
        grads = []
        for lanes, name in ((left, "grada"), (right, "gradb")):
            cuts = down(tile, resids, core_places, out, 0, rows_here, lanes, name, chunks=depth_ranks, limit=NEAR_LIMIT)
            grads.append(all_rows(sum_of(to_rank(cuts))))
        (begun,) = across(precond, grads[0], rank_places, out, 0, p_rows, left, "fwda")
        (theirs,) = across(precond, grads[1], rank_places, out, other_rows, row_half, right, "fwdb", before=begun)
        (mine,) = across(precond, grads[1], rank_places, out, my_rows, row_half, right, "fwdc", before=begun)
        cuts = add_and_cut(mine, swap(theirs, "centers", 1), chips, "cut")
        fwd = cuts[0]
        for k in range(1, chips):
            fwd = fwd + swap(cuts[k], "centers", 2 * k)
        fwds = [fwd] + [swap(fwd, "centers", 2 * k) for k in range(1, chips)]
        others = swap(jnp.concatenate(fwds, axis=0), "centers", 1)
        others = [others[k * part : (k + 1) * part] for k in range(chips)]
        begun, squares = down(precond, fwds, chip_places, out, my_rows, row_half, left, "backa", squares="sum")
        cuts = down(
            precond,
            others,
            chip_places,
            out,
            other_rows,
            row_half,
            left,
            "backb",
            chunks=depth_ranks,
            before=begun,
            squares=squares,
        )
        first, scale = update(to_rank(cuts), a_halves[0], center_total * out)
        cuts = down(
            precond, fwds + others, chip_places_both, out, 0, p_rows, right, "backc", chunks=depth_ranks
        )
        (second,) = update(to_rank(cuts), a_halves[1], center_total * out, scale)
        a_halves = [first, second]
        a_pieces = all_rows(first) + all_rows(second)
    return assemble(a_pieces, rank_places_both, (out, count), "result").T


def plain_tile(rows_x, centers_x):
    width = rows_x.shape[1]
    left = jnp.sum(rows_x * rows_x, axis=1)
    right = jnp.sum(centers_x * centers_x, axis=1)
    cross = jnp.dot(rows_x, centers_x.T, precision=lax.Precision.HIGHEST)
    return jnp.exp(-2.0 * (left[:, None] + right[None, :] - 2.0 * cross) / width)


def plain_body(features, centers, labels, coeffs, precond):
    rows_total = features.shape[0] * lax.axis_size("rows")
    center_total = coeffs.shape[0] * lax.axis_size("centers")
    targets = labels.astype(f32)
    share_rows = features.shape[0] // lax.axis_size("centers")
    highest = lax.Precision.HIGHEST
    tile = plain_tile(features, centers)
    for step in range(STEPS):
        part = jnp.dot(tile, coeffs, precision=highest)
        share = lax.psum_scatter(part, "centers", scatter_dimension=0, tiled=True)
        offset = lax.axis_index("centers") * share_rows
        share_y = lax.dynamic_slice_in_dim(targets, offset, share_rows, 0)
        share_resid = (jax.nn.sigmoid(share) - share_y) / rows_total
        resid = lax.all_gather(share_resid, "centers", axis=0, tiled=True)
        grad = lax.psum(lax.dot_general(tile, resid, (((0,), (0,)), ((), ())), precision=highest), "rows")
        fwd = lax.psum(jnp.dot(precond, grad, precision=highest), "centers")
        back = lax.psum(lax.dot_general(precond, fwd, (((0,), (0,)), ((), ())), precision=highest), "rows")
        total = lax.psum(jnp.sum(fwd * fwd), "rows")
        scale = step_size / jnp.sqrt(total / (center_total * fwd.shape[1]) + epsilon)
        coeffs = coeffs - scale * back
    return coeffs


def fits(ranks, cols, features, coeffs, precond):
    if cols % 2 or ranks & (ranks - 1) or cols & (cols - 1):
        return False
    out = coeffs.shape[1]
    lanes = (features.shape[0] // ranks, coeffs.shape[0] // cols // 2, precond.shape[0] // ranks // 2)
    return out % (8 * ranks) == 0 and out % (4 * cols) == 0 and out % 16 == 0 and all(n % 128 == 0 for n in lanes)


def solution(mesh):
    in_specs = (
        P("rows", None),
        P("centers", None),
        P("rows", None),
        P("centers", None),
        P("rows", "centers"),
    )
    out_specs = P("centers", None)

    def program(features, centers, labels, coeffs, precond):
        fit = fits(mesh.shape["rows"], mesh.shape["centers"], features, coeffs, precond)
        one = jax.shard_map(
            body if fit else plain_body, mesh=mesh, in_specs=in_specs, out_specs=out_specs, check_vma=False
        )
        return one(features, centers, labels, coeffs, precond)

    return program
```

time: 284 us -> 254 us (0.89)
  waiting for transfers between devices: 80.6 us -> 52.9 us
  local copies, waits for them, and re-layouts: 18.4 us -> 4.41 us
  starting transfers between devices: 91.5 us -> 104 us
  Pallas kernels: 85.9 us -> 89.9 us
    ppermute x78 -> x74, waiting for transfers between devices: 80.6 us -> 52.9 us  [swap(): return lax.ppermute(x, axis, [(i, i ^ mask) for i in range(size)])]
    unnamed x48 -> x8, local copies, waits for them, and re-layouts: 16.4 us -> 3.41 us
    ppermute x78 -> x74, starting transfers between devices: 91.5 us -> 104 us  [swap(): return lax.ppermute(x, axis, [(i, i ^ mask) for i in range(size)])]
    pallas_call x11 -> x21, Pallas kernels: 69.4 us -> 79.2 us  [the longest x17 78.9 us: call(): pl.pallas_call(whole, in_specs=[FAR] + [WHOLE] * n_in, out_specs=[WHOLE]...]
    pallas_call x4 -> x2, Pallas kernels: 6.96 us -> 0.14 us  [add_and_cut(): pl.pallas_call(kernel, in_specs=[WHOLE] * 2, out_specs=[WHOLE] * chips, o...]
    add x8 -> x6, other arithmetic: 3.52 us -> 0.13 us  [the longest x2 0.07 us: body(): fwd = fwd + swap(cuts[k], 'centers', 2 * k)]
  transfers between devices with their start and end apart: 78 -> 74, of which waited for: 36 -> 26; matrix products, arithmetic and copies ran while one was open for 2% -> 0% of each run, Pallas kernels for 13% -> 21%
where the time goes in v2:
time: 254 us
  starting transfers between devices  104 us (41%)
  Pallas kernels  89.9 us (35%)
  waiting for transfers between devices  52.9 us (21%)
  local copies, waits for them, and re-layouts  4.41 us (2%)
    ppermute x74, starting transfers between devices, swap(): return lax.ppermute(x, axis, [(i, i ^ mask) for i in range(size)])  104 us
    pallas_call x17, Pallas kernels, call(): pl.pallas_call(whole, in_specs=[FAR] + [WHOLE] * n_in, out_specs=[WHOLE]...  78.9 us
    ppermute x74, waiting for transfers between devices, swap(): return lax.ppermute(x, axis, [(i, i ^ mask) for i in range(size)])  52.9 us
    pallas_call x1, Pallas kernels, tile_and_logits(): pl.pallas_call(kernel, grid=(rows // size,), in_specs=[pl.BlockSpec((size...  9.78 us
  transfers between devices with their start and end apart: 74, of which 26 were waited for; matrix products, arithmetic and copies ran while one was open for 0% of the time, Pallas kernels for 21%

profile of v2, /device:TPU:0, one launch (start us, length us, event | category | flops | bytes accessed | tf_op | source)
XLA Modules:
  0.0 253.8 jit_solution(8877139113536615815)
XLA Ops:
  0.0 9.8 %tile_and_logits.1 = (f32[1024,2048]{1,0:T(8,128)}, f32[32,1024]{1,0:T(8,128)}, f32[32,1024]{1,0:T(8,128)}) custom-call(f32[1024,128]{1,0:T(8,128)} %x_ref.1, f32[2048,128]{1,0:T(8,128)} %c_ref.1, f32[64,2048]{1,0:T(8,128)} %bitcast.13), custom_call_target="tpu_custom_call" | custom-call | flops 3221225472 | bytes 8388608 | tf_op jit(solution)/shard_map/tile_and_logits/pallas_call | solution.py:240
  12.4 3.9 %collective-permute-start.3 = (f32[32,1024]{1,0:T(8,128)S(1)}, f32[32,1024]{1,0:T(8,128)S(1)}, u32[]{:S(2)}, u32[]{:S(2)}) collective-permute-start(f32[32,1024]{1,0:T(8,128)S(1)} %add.90), channel_id=1, source_target_pairs={{0,6},{1,7},{2,4},{3,5},{4,2},{5,3},{6,0},{7,1},{8,14},{9,15},{10,... | collective-permute-start | bytes 393224 | tf_op jit(solution)/shard_map/ppermute | solution.py:336
  16.9 3.3 %collective-permute-done.3 = f32[32,1024]{1,0:T(8,128)S(1)} collective-permute-done((f32[32,1024]{1,0:T(8,128)S(1)}, f32[32,1024]{1,0:T(8,128)S(1)}, u32[]{:S(2)}, u32[]{:S(2)}) %collective-permute-start.3) | collective-permute-done | bytes 131104 | tf_op jit(solution)/shard_map/ppermute | solution.py:336
  25.5 3.4 %copy-done = f32[1024,2048]{1,0:T(8,128)S(1)} copy-done((f32[1024,2048]{1,0:T(8,128)S(1)}, f32[1024,2048]{1,0:T(8,128)}, u32[]{:S(2)}) %copy-start) | copy-done | bytes 8388632
  31.1 3.7 %collective-permute-start.13 = (f32[16,1024]{1,0:T(8,128)S(1)}, f32[16,1024]{1,0:T(8,128)S(1)}, u32[]{:S(2)}, u32[]{:S(2)}) collective-permute-start(f32[16,1024]{1,0:T(8,128)S(1)} %get-tuple-element.68), channel_id=1, source_target_pairs={{0,24},{8,16},{16,8},{24,0},{1,25},{9,17},{17,9},{25,1},{2,26},{10... | collective-permute-start | bytes 196616 | tf_op jit(solution)/shard_map/ppermute | solution.py:336
  37.7 3.7 %collective-permute-start.7 = (f32[16,1024]{1,0:T(8,128)S(1)}, f32[16,1024]{1,0:T(8,128)S(1)}, u32[]{:S(2)}, u32[]{:S(2)}) collective-permute-start(f32[16,1024]{1,0:T(8,128)S(1)} %get-tuple-element.64), channel_id=1, source_target_pairs={{0,24},{8,16},{16,8},{24,0},{1,25},{9,17},{17,9},{25,1},{2,26},{10... | collective-permute-start | bytes 196616 | tf_op jit(solution)/shard_map/ppermute | solution.py:336
  43.5 2.9 %collective-permute-start.15 = (f32[16,1024]{1,0:T(8,128)S(1)}, f32[16,1024]{1,0:T(8,128)S(1)}, u32[]{:S(2)}, u32[]{:S(2)}) collective-permute-start(f32[16,1024]{1,0:T(8,128)S(1)} %add_add_fusion.4.refs_1_), channel_id=1, source_target_pairs={{0,16},{8,24},{16,0},{24,8},{1,17},{9,25},{17,1},{25,9},{2,18},{10... | collective-permute-start | bytes 196616 | tf_op jit(solution)/shard_map/ppermute | solution.py:336
  52.9 8.0 %fwda.2.refs_5_ = f32[64,4096]{1,0:T(8,128)S(1)} custom-call(f32[4096,2048]{1,0:T(8,128)} %refs_0_.23, f32[16,1024]{1,0:T(8,128)S(1)} %add_add_fusion.4.refs_1_, f32[16,1024]{1,0:T(8,128)S(1)} %collective-permute-done.14.refs_2_, f32[16,1024]{1,0:T(8,128)S(1)} %collective-permute-done.15.refs_3_, f32[16,1024]{1,0:T(8,128)S(1)} %collective-permute-done.16.refs_4_), custom_call_target="tpu_custom_call" | custom-call | flops 1610612736 | bytes 16777216 | tf_op jit(solution)/shard_map/fwda/pallas_call | solution.py:117
  61.0 4.8 %fwdb.2 = f32[64,2048]{1,0:T(8,128)S(1)} custom-call(f32[4096,2048]{1,0:T(8,128)} %refs_0_.23, f32[16,1024]{1,0:T(8,128)S(1)} %add_add_fusion.5.refs_1_, f32[16,1024]{1,0:T(8,128)S(1)} %collective-permute-done.8.refs_2_, f32[16,1024]{1,0:T(8,128)S(1)} %collective-permute-done.9.refs_3_, f32[16,1024]{1,0:T(8,128)S(1)} %collective-permute-done.10.refs_4_, ...), custom_call_target="tpu_custom_call" | custom-call | flops 805306368 | bytes 8388608 | tf_op jit(solution)/shard_map/fwdb/pallas_call | solution.py:117
  65.9 4.8 %fwdc.2.a_ref = f32[64,2048]{1,0:T(8,128)S(1)} custom-call(f32[4096,2048]{1,0:T(8,128)} %refs_0_.23, f32[16,1024]{1,0:T(8,128)S(1)} %add_add_fusion.5.refs_1_, f32[16,1024]{1,0:T(8,128)S(1)} %collective-permute-done.8.refs_2_, f32[16,1024]{1,0:T(8,128)S(1)} %collective-permute-done.9.refs_3_, f32[16,1024]{1,0:T(8,128)S(1)} %collective-permute-done.10.refs_4_, ...), custom_call_target="tpu_custom_call" | custom-call | flops 805306368 | bytes 8388608 | tf_op jit(solution)/shard_map/fwdc/pallas_call | solution.py:117
  74.3 3.7 %collective-permute-done.20 = f32[16,2048]{1,0:T(8,128)S(1)} collective-permute-done((f32[16,2048]{1,0:T(8,128)S(1)}, f32[16,2048]{1,0:T(8,128)S(1)}, u32[]{:S(2)}, u32[]{:S(2)}) %collective-permute-start.20) | collective-permute-done | bytes 131104 | tf_op jit(solution)/shard_map/ppermute | solution.py:336
  84.1 3.8 %collective-permute-done.23.refs_4_ = f32[16,2048]{1,0:T(8,128)S(1)} collective-permute-done((f32[16,2048]{1,0:T(8,128)S(1)}, f32[16,2048]{1,0:T(8,128)S(1)}, u32[]{:S(2)}, u32[]{:S(2)}) %collective-permute-start.23) | collective-permute-done | bytes 131104 | tf_op jit(solution)/shard_map/ppermute | solution.py:336
  90.8 4.4 %backa.2 = (f32[64,1024]{1,0:T(8,128)S(1)}, f32[8,128]{1,0:T(8,128)S(1)}) custom-call(f32[4096,2048]{1,0:T(8,128)} %refs_0_.23, f32[16,2048]{1,0:T(8,128)S(1)} %add_add_fusion.1.refs_1_, f32[16,2048]{1,0:T(8,128)S(1)} %collective-permute-done.21.refs_2_, f32[16,2048]{1,0:T(8,128)S(1)} %collective-permute-done.22.refs_3_, ...), custom_call_target="tpu_custom_call" | custom-call | flops 805306368 | bytes 8388608 | tf_op jit(solution)/shard_map/backa/pallas_call | solution.py:117
  95.2 4.5 %backb.2 = (f32[16,1152]{1,0:T(8,128)S(1)}, f32[16,1152]{1,0:T(8,128)S(1)}, f32[16,1152]{1,0:T(8,128)S(1)}, f32[16,1152]{1,0:T(8,128)S(1)}) custom-call(f32[4096,2048]{1,0:T(8,128)} %refs_0_.23, f32[16,2048]{1,0:T(8,128)S(1)} %get-tuple-element.118.refs_1_.refs_5_, f32[16,2048]{1,0:T(8,128)S(1)} %get-tuple-element.117.refs_2_.refs_6_, ...), custom_call_target="tpu_custom_call" | custom-call | flops 805306368 | bytes 8388608 | tf_op jit(solution)/shard_map/backb/pallas_call | solution.py:117
  105.0 7.0 %backc.2 = (f32[16,1024]{1,0:T(8,128)S(1)}, f32[16,1024]{1,0:T(8,128)S(1)}, f32[16,1024]{1,0:T(8,128)S(1)}, f32[16,1024]{1,0:T(8,128)S(1)}) custom-call(f32[4096,2048]{1,0:T(8,128)} %refs_0_.23, f32[16,2048]{1,0:T(8,128)S(1)} %add_add_fusion.1.refs_1_, f32[16,2048]{1,0:T(8,128)S(1)} %collective-permute-done.21.refs_2_, ...), custom_call_target="tpu_custom_call" | custom-call | flops 1610612736 | bytes 16777216 | tf_op jit(solution)/shard_map/backc/pallas_call | solution.py:117
  116.6 3.0 %collective-permute-start.29 = (f32[16,1024]{1,0:T(8,128)S(1)}, f32[16,1024]{1,0:T(8,128)S(1)}, u32[]{:S(2)}, u32[]{:S(2)}) collective-permute-start(f32[16,1024]{1,0:T(8,128)S(1)} %get-tuple-element.79.refs_1_.refs_4_), channel_id=1, source_target_pairs={{0,16},{8,24},{16,0},{24,8},{1,17},{9,25},{17,1},{25,9},{2,18},{10... | collective-permute-start | bytes 196616 | tf_op jit(solution)/shard_map/ppermute | solution.py:336
  121.9 4.4 %collective-permute-start.34 = (f32[16,1024]{1,0:T(8,128)S(1)}, f32[16,1024]{1,0:T(8,128)S(1)}, u32[]{:S(2)}, u32[]{:S(2)}) collective-permute-start(f32[16,1024]{1,0:T(8,128)S(1)} %update.5.refs_5_.refs_4_), channel_id=1, source_target_pairs={{0,8},{8,0},{16,24},{24,16},{1,9},{9,1},{17,25},{25,17},{2,10},{10... | collective-permute-start | bytes 196616 | tf_op jit(solution)/shard_map/ppermute | solution.py:336
  131.4 3.1 %collective-permute-done.36.refs_8_ = f32[16,1024]{1,0:T(8,128)S(1)} collective-permute-done((f32[16,1024]{1,0:T(8,128)S(1)}, f32[16,1024]{1,0:T(8,128)S(1)}, u32[]{:S(2)}, u32[]{:S(2)}) %collective-permute-start.36) | collective-permute-done | bytes 65568 | tf_op jit(solution)/shard_map/ppermute | solution.py:336
  134.6 3.6 %logits.1 = (f32[32,1024]{1,0:T(8,128)S(1)}, f32[32,1024]{1,0:T(8,128)S(1)}) custom-call(f32[1024,2048]{1,0:T(8,128)S(1)} %bitcast.12, f32[16,1024]{1,0:T(8,128)S(1)} %get-tuple-element.79.refs_1_.refs_4_, f32[16,1024]{1,0:T(8,128)S(1)} %collective-permute-done.28.refs_2_, f32[16,1024]{1,0:T(8,128)S(1)} %collective-permute-done.29.refs_3_, ...), custom_call_target="tpu_custom_call" | custom-call | flops 805306368 | bytes 8388608 | tf_op jit(solution)/shard_map/logits/pallas_call | solution.py:117
  143.2 3.8 %collective-permute-done.40 = f32[32,1024]{1,0:T(8,128)S(1)} collective-permute-done((f32[32,1024]{1,0:T(8,128)S(1)}, f32[32,1024]{1,0:T(8,128)S(1)}, u32[]{:S(2)}, u32[]{:S(2)}) %collective-permute-start.40) | collective-permute-done | bytes 131104 | tf_op jit(solution)/shard_map/ppermute | solution.py:336
  160.8 2.9 %collective-permute-start.42 = (f32[16,1024]{1,0:T(8,128)S(1)}, f32[16,1024]{1,0:T(8,128)S(1)}, u32[]{:S(2)}, u32[]{:S(2)}) collective-permute-start(f32[16,1024]{1,0:T(8,128)S(1)} %get-tuple-element.88), channel_id=1, source_target_pairs={{0,8},{8,0},{16,24},{24,16},{1,9},{9,1},{17,25},{25,17},{2,10},{10... | collective-permute-start | bytes 196616 | tf_op jit(solution)/shard_map/ppermute | solution.py:336
  173.2 8.0 %fwda.3.refs_5_ = f32[64,4096]{1,0:T(8,128)S(1)} custom-call(f32[4096,2048]{1,0:T(8,128)} %refs_0_.23, f32[16,1024]{1,0:T(8,128)S(1)} %add_add_fusion.2.refs_1_, f32[16,1024]{1,0:T(8,128)S(1)} %collective-permute-done.51.refs_2_, f32[16,1024]{1,0:T(8,128)S(1)} %collective-permute-done.52.refs_3_, f32[16,1024]{1,0:T(8,128)S(1)} %collective-permute-done.53.refs_4_), custom_call_target="tpu_custom_call" | custom-call | flops 1610612736 | bytes 16777216 | tf_op jit(solution)/shard_map/fwda/pallas_call | solution.py:117
  181.2 4.8 %fwdb.3 = f32[64,2048]{1,0:T(8,128)S(1)} custom-call(f32[4096,2048]{1,0:T(8,128)} %refs_0_.23, f32[16,1024]{1,0:T(8,128)S(1)} %add_add_fusion.3.refs_1_, f32[16,1024]{1,0:T(8,128)S(1)} %collective-permute-done.45.refs_2_, f32[16,1024]{1,0:T(8,128)S(1)} %collective-permute-done.46.refs_3_, f32[16,1024]{1,0:T(8,128)S(1)} %collective-permute-done.47.refs_4_, ...), custom_call_target="tpu_custom_call" | custom-call | flops 805306368 | bytes 8388608 | tf_op jit(solution)/shard_map/fwdb/pallas_call | solution.py:117
  186.1 4.8 %fwdc.3.a_ref = f32[64,2048]{1,0:T(8,128)S(1)} custom-call(f32[4096,2048]{1,0:T(8,128)} %refs_0_.23, f32[16,1024]{1,0:T(8,128)S(1)} %add_add_fusion.3.refs_1_, f32[16,1024]{1,0:T(8,128)S(1)} %collective-permute-done.45.refs_2_, f32[16,1024]{1,0:T(8,128)S(1)} %collective-permute-done.46.refs_3_, f32[16,1024]{1,0:T(8,128)S(1)} %collective-permute-done.47.refs_4_, ...), custom_call_target="tpu_custom_call" | custom-call | flops 805306368 | bytes 8388608 | tf_op jit(solution)/shard_map/fwdc/pallas_call | solution.py:117
  194.6 3.7 %collective-permute-done.57 = f32[16,2048]{1,0:T(8,128)S(1)} collective-permute-done((f32[16,2048]{1,0:T(8,128)S(1)}, f32[16,2048]{1,0:T(8,128)S(1)}, u32[]{:S(2)}, u32[]{:S(2)}) %collective-permute-start.57) | collective-permute-done | bytes 131104 | tf_op jit(solution)/shard_map/ppermute | solution.py:336
  204.3 3.8 %collective-permute-done.60.refs_4_ = f32[16,2048]{1,0:T(8,128)S(1)} collective-permute-done((f32[16,2048]{1,0:T(8,128)S(1)}, f32[16,2048]{1,0:T(8,128)S(1)}, u32[]{:S(2)}, u32[]{:S(2)}) %collective-permute-start.60) | collective-permute-done | bytes 131104 | tf_op jit(solution)/shard_map/ppermute | solution.py:336
  210.1 4.4 %backa.3 = (f32[64,1024]{1,0:T(8,128)S(1)}, f32[8,128]{1,0:T(8,128)S(1)}) custom-call(f32[4096,2048]{1,0:T(8,128)} %refs_0_.23, f32[16,2048]{1,0:T(8,128)S(1)} %add_add_fusion.refs_1_, f32[16,2048]{1,0:T(8,128)S(1)} %collective-permute-done.58.refs_2_, f32[16,2048]{1,0:T(8,128)S(1)} %collective-permute-done.59.refs_3_, ...), custom_call_target="tpu_custom_call" | custom-call | flops 805306368 | bytes 8388608 | tf_op jit(solution)/shard_map/backa/pallas_call | solution.py:117
  214.5 4.3 %backb.3 = (f32[16,1152]{1,0:T(8,128)S(1)}, f32[16,1152]{1,0:T(8,128)S(1)}, f32[16,1152]{1,0:T(8,128)S(1)}, f32[16,1152]{1,0:T(8,128)S(1)}) custom-call(f32[4096,2048]{1,0:T(8,128)} %refs_0_.23, f32[16,2048]{1,0:T(8,128)S(1)} %get-tuple-element.114.refs_1_.refs_5_, f32[16,2048]{1,0:T(8,128)S(1)} %get-tuple-element.113.refs_2_.refs_6_, ...), custom_call_target="tpu_custom_call" | custom-call | flops 805306368 | bytes 8388608 | tf_op jit(solution)/shard_map/backb/pallas_call | solution.py:117
  218.9 3.0 %collective-permute-start.62 = (f32[16,1152]{1,0:T(8,128)S(1)}, f32[16,1152]{1,0:T(8,128)S(1)}, u32[]{:S(2)}, u32[]{:S(2)}) collective-permute-start(f32[16,1152]{1,0:T(8,128)S(1)} %get-tuple-element.102), channel_id=1, source_target_pairs={{0,8},{8,0},{16,24},{24,16},{1,9},{9,1},{17,25},{25,17},{2,10},{10... | collective-permute-start | bytes 221192 | tf_op jit(solution)/shard_map/ppermute | solution.py:336
  224.3 6.8 %backc.3 = (f32[16,1024]{1,0:T(8,128)S(1)}, f32[16,1024]{1,0:T(8,128)S(1)}, f32[16,1024]{1,0:T(8,128)S(1)}, f32[16,1024]{1,0:T(8,128)S(1)}) custom-call(f32[4096,2048]{1,0:T(8,128)} %refs_0_.23, f32[16,2048]{1,0:T(8,128)S(1)} %add_add_fusion.refs_1_, f32[16,2048]{1,0:T(8,128)S(1)} %collective-permute-done.58.refs_2_, ...), custom_call_target="tpu_custom_call" | custom-call | flops 1610612736 | bytes 16777216 | tf_op jit(solution)/shard_map/backc/pallas_call | solution.py:117
  241.1 5.5 %collective-permute-start.71 = (f32[16,1024]{1,0:T(8,128)S(1)}, f32[16,1024]{1,0:T(8,128)S(1)}, u32[]{:S(2)}, u32[]{:S(2)}) collective-permute-start(f32[16,1024]{1,0:T(8,128)S(1)} %update.7.refs_4_), channel_id=1, source_target_pairs={{0,8},{8,0},{16,24},{24,16},{1,9},{9,1},{17,25},{25,17},{2,10},{10... | collective-permute-start | bytes 196616 | tf_op jit(solution)/shard_map/ppermute | solution.py:336
  249.1 2.9 %collective-permute-done.72.refs_6_ = f32[16,1024]{1,0:T(8,128)S(1)} collective-permute-done((f32[16,1024]{1,0:T(8,128)S(1)}, f32[16,1024]{1,0:T(8,128)S(1)}, u32[]{:S(2)}, u32[]{:S(2)}) %collective-permute-start.72) | collective-permute-done | bytes 65568 | tf_op jit(solution)/shard_map/ppermute | solution.py:336
  (166 shorter events, 108.9 us)
Async XLA Ops:
  31.1 10.3 %collective-permute-start.13 = (f32[16,1024]{1,0:T(8,128)S(1)}, f32[16,1024]{1,0:T(8,128)S(1)}, u32[]{:S(2)}, u32[]{:S(2)}) collective-permute-start(f32[16,1024]{1,0:T(8,128)S(1)} %get-tuple-element.68), channel_id=1, source_target_pairs={{0,24},{8,16},{16,8},{24,0},{1,25},{9,17},{17,9},{25,1},{2,26},{10... | collective-permute-start | bytes 196616 | tf_op jit(solution)/shard_map/ppermute | solution.py:336
  37.7 8.7 %collective-permute-start.7 = (f32[16,1024]{1,0:T(8,128)S(1)}, f32[16,1024]{1,0:T(8,128)S(1)}, u32[]{:S(2)}, u32[]{:S(2)}) collective-permute-start(f32[16,1024]{1,0:T(8,128)S(1)} %get-tuple-element.64), channel_id=1, source_target_pairs={{0,24},{8,16},{16,8},{24,0},{1,25},{9,17},{17,9},{25,1},{2,26},{10... | collective-permute-start | bytes 196616 | tf_op jit(solution)/shard_map/ppermute | solution.py:336
  42.2 8.7 %collective-permute-start.14 = (f32[16,1024]{1,0:T(8,128)S(1)}, f32[16,1024]{1,0:T(8,128)S(1)}, u32[]{:S(2)}, u32[]{:S(2)}) collective-permute-start(f32[16,1024]{1,0:T(8,128)S(1)} %add_add_fusion.4.refs_1_), channel_id=1, source_target_pairs={{0,8},{8,0},{16,24},{24,16},{1,9},{9,1},{17,25},{25,17},{2,10},{10... | collective-permute-start | bytes 196616 | tf_op jit(solution)/shard_map/ppermute | solution.py:336
  43.5 9.4 %collective-permute-start.15 = (f32[16,1024]{1,0:T(8,128)S(1)}, f32[16,1024]{1,0:T(8,128)S(1)}, u32[]{:S(2)}, u32[]{:S(2)}) collective-permute-start(f32[16,1024]{1,0:T(8,128)S(1)} %add_add_fusion.4.refs_1_), channel_id=1, source_target_pairs={{0,16},{8,24},{16,0},{24,8},{1,17},{9,25},{17,1},{25,9},{2,18},{10... | collective-permute-start | bytes 196616 | tf_op jit(solution)/shard_map/ppermute | solution.py:336
  48.3 12.6 %collective-permute-start.8 = (f32[16,1024]{1,0:T(8,128)S(1)}, f32[16,1024]{1,0:T(8,128)S(1)}, u32[]{:S(2)}, u32[]{:S(2)}) collective-permute-start(f32[16,1024]{1,0:T(8,128)S(1)} %add_add_fusion.5.refs_1_), channel_id=1, source_target_pairs={{0,8},{8,0},{16,24},{24,16},{1,9},{9,1},{17,25},{25,17},{2,10},{10... | collective-permute-start | bytes 196616 | tf_op jit(solution)/shard_map/ppermute | solution.py:336
  49.3 11.6 %collective-permute-start.9 = (f32[16,1024]{1,0:T(8,128)S(1)}, f32[16,1024]{1,0:T(8,128)S(1)}, u32[]{:S(2)}, u32[]{:S(2)}) collective-permute-start(f32[16,1024]{1,0:T(8,128)S(1)} %add_add_fusion.5.refs_1_), channel_id=1, source_target_pairs={{0,16},{8,24},{16,0},{24,8},{1,17},{9,25},{17,1},{25,9},{2,18},{10... | collective-permute-start | bytes 196616 | tf_op jit(solution)/shard_map/ppermute | solution.py:336
  50.9 10.0 %collective-permute-start.10 = (f32[16,1024]{1,0:T(8,128)S(1)}, f32[16,1024]{1,0:T(8,128)S(1)}, u32[]{:S(2)}, u32[]{:S(2)}) collective-permute-start(f32[16,1024]{1,0:T(8,128)S(1)} %add_add_fusion.5.refs_1_), channel_id=1, source_target_pairs={{0,24},{8,16},{16,8},{24,0},{1,25},{9,17},{17,9},{25,1},{2,26},{10... | collective-permute-start | bytes 196616 | tf_op jit(solution)/shard_map/ppermute | solution.py:336
  72.5 7.9 %collective-permute-start.19 = (f32[16,2048]{1,0:T(8,128)S(1)}, f32[16,2048]{1,0:T(8,128)S(1)}, u32[]{:S(2)}, u32[]{:S(2)}) collective-permute-start(f32[16,2048]{1,0:T(8,128)S(1)} %get-tuple-element.71), channel_id=1, source_target_pairs={{0,4},{1,5},{2,6},{3,7},{4,0},{5,1},{6,2},{7,3},{8,12},{9,13},{10,... | collective-permute-start | bytes 393224 | tf_op jit(solution)/shard_map/ppermute | solution.py:336
  99.7 15.3 %collective-permute-start.25 = (f32[16,1152]{1,0:T(8,128)S(1)}, f32[16,1152]{1,0:T(8,128)S(1)}, u32[]{:S(2)}, u32[]{:S(2)}) collective-permute-start(f32[16,1152]{1,0:T(8,128)S(1)} %get-tuple-element.76), channel_id=1, source_target_pairs={{0,8},{8,0},{16,24},{24,16},{1,9},{9,1},{17,25},{25,17},{2,10},{10... | collective-permute-start | bytes 221192 | tf_op jit(solution)/shard_map/ppermute | solution.py:336
  101.8 14.6 %collective-permute-start.26 = (f32[16,1152]{1,0:T(8,128)S(1)}, f32[16,1152]{1,0:T(8,128)S(1)}, u32[]{:S(2)}, u32[]{:S(2)}) collective-permute-start(f32[16,1152]{1,0:T(8,128)S(1)} %get-tuple-element.77), channel_id=1, source_target_pairs={{0,16},{8,24},{16,0},{24,8},{1,17},{9,25},{17,1},{25,9},{2,18},{10... | collective-permute-start | bytes 221192 | tf_op jit(solution)/shard_map/ppermute | solution.py:336
  103.6 12.8 %collective-permute-start.27 = (f32[16,1152]{1,0:T(8,128)S(1)}, f32[16,1152]{1,0:T(8,128)S(1)}, u32[]{:S(2)}, u32[]{:S(2)}) collective-permute-start(f32[16,1152]{1,0:T(8,128)S(1)} %get-tuple-element.78), channel_id=1, source_target_pairs={{0,24},{8,16},{16,8},{24,0},{1,25},{9,17},{17,9},{25,1},{2,26},{10... | collective-permute-start | bytes 221192 | tf_op jit(solution)/shard_map/ppermute | solution.py:336
  112.7 8.2 %collective-permute-start.32 = (f32[16,1024]{1,0:T(8,128)S(1)}, f32[16,1024]{1,0:T(8,128)S(1)}, u32[]{:S(2)}, u32[]{:S(2)}) collective-permute-start(f32[16,1024]{1,0:T(8,128)S(1)} %get-tuple-element.82), channel_id=1, source_target_pairs={{0,16},{8,24},{16,0},{24,8},{1,17},{9,25},{17,1},{25,9},{2,18},{10... | collective-permute-start | bytes 196616 | tf_op jit(solution)/shard_map/ppermute | solution.py:336
  116.5 11.9 %collective-permute-start.28 = (f32[16,1024]{1,0:T(8,128)S(1)}, f32[16,1024]{1,0:T(8,128)S(1)}, u32[]{:S(2)}, u32[]{:S(2)}) collective-permute-start(f32[16,1024]{1,0:T(8,128)S(1)} %get-tuple-element.79.refs_1_.refs_4_), channel_id=1, source_target_pairs={{0,8},{8,0},{16,24},{24,16},{1,9},{9,1},{17,25},{25,17},{2,10},{10... | collective-permute-start | bytes 196616 | tf_op jit(solution)/shard_map/ppermute | solution.py:336
  116.6 13.3 %collective-permute-start.29 = (f32[16,1024]{1,0:T(8,128)S(1)}, f32[16,1024]{1,0:T(8,128)S(1)}, u32[]{:S(2)}, u32[]{:S(2)}) collective-permute-start(f32[16,1024]{1,0:T(8,128)S(1)} %get-tuple-element.79.refs_1_.refs_4_), channel_id=1, source_target_pairs={{0,16},{8,24},{16,0},{24,8},{1,17},{9,25},{17,1},{25,9},{2,18},{10... | collective-permute-start | bytes 196616 | tf_op jit(solution)/shard_map/ppermute | solution.py:336
  119.5 10.3 %collective-permute-start.30 = (f32[16,1024]{1,0:T(8,128)S(1)}, f32[16,1024]{1,0:T(8,128)S(1)}, u32[]{:S(2)}, u32[]{:S(2)}) collective-permute-start(f32[16,1024]{1,0:T(8,128)S(1)} %get-tuple-element.79.refs_1_.refs_4_), channel_id=1, source_target_pairs={{0,24},{8,16},{16,8},{24,0},{1,25},{9,17},{17,9},{25,1},{2,26},{10... | collective-permute-start | bytes 196616 | tf_op jit(solution)/shard_map/ppermute | solution.py:336
  152.7 8.2 %collective-permute-start.50 = (f32[16,1024]{1,0:T(8,128)S(1)}, f32[16,1024]{1,0:T(8,128)S(1)}, u32[]{:S(2)}, u32[]{:S(2)}) collective-permute-start(f32[16,1024]{1,0:T(8,128)S(1)} %get-tuple-element.94), channel_id=1, source_target_pairs={{0,24},{8,16},{16,8},{24,0},{1,25},{9,17},{17,9},{25,1},{2,26},{10... | collective-permute-start | bytes 196616 | tf_op jit(solution)/shard_map/ppermute | solution.py:336
  154.1 9.6 %collective-permute-start.49 = (f32[16,1024]{1,0:T(8,128)S(1)}, f32[16,1024]{1,0:T(8,128)S(1)}, u32[]{:S(2)}, u32[]{:S(2)}) collective-permute-start(f32[16,1024]{1,0:T(8,128)S(1)} %get-tuple-element.93), channel_id=1, source_target_pairs={{0,16},{8,24},{16,0},{24,8},{1,17},{9,25},{17,1},{25,9},{2,18},{10... | collective-permute-start | bytes 196616 | tf_op jit(solution)/shard_map/ppermute | solution.py:336
  155.0 8.8 %collective-permute-start.48 = (f32[16,1024]{1,0:T(8,128)S(1)}, f32[16,1024]{1,0:T(8,128)S(1)}, u32[]{:S(2)}, u32[]{:S(2)}) collective-permute-start(f32[16,1024]{1,0:T(8,128)S(1)} %get-tuple-element.92), channel_id=1, source_target_pairs={{0,8},{8,0},{16,24},{24,16},{1,9},{9,1},{17,25},{25,17},{2,10},{10... | collective-permute-start | bytes 196616 | tf_op jit(solution)/shard_map/ppermute | solution.py:336
  160.8 7.9 %collective-permute-start.43 = (f32[16,1024]{1,0:T(8,128)S(1)}, f32[16,1024]{1,0:T(8,128)S(1)}, u32[]{:S(2)}, u32[]{:S(2)}) collective-permute-start(f32[16,1024]{1,0:T(8,128)S(1)} %get-tuple-element.89), channel_id=1, source_target_pairs={{0,16},{8,24},{16,0},{24,8},{1,17},{9,25},{17,1},{25,9},{2,18},{10... | collective-permute-start | bytes 196616 | tf_op jit(solution)/shard_map/ppermute | solution.py:336
  163.9 9.3 %collective-permute-start.52 = (f32[16,1024]{1,0:T(8,128)S(1)}, f32[16,1024]{1,0:T(8,128)S(1)}, u32[]{:S(2)}, u32[]{:S(2)}) collective-permute-start(f32[16,1024]{1,0:T(8,128)S(1)} %add_add_fusion.2.refs_1_), channel_id=1, source_target_pairs={{0,16},{8,24},{16,0},{24,8},{1,17},{9,25},{17,1},{25,9},{2,18},{10... | collective-permute-start | bytes 196616 | tf_op jit(solution)/shard_map/ppermute | solution.py:336
  168.7 12.5 %collective-permute-start.45 = (f32[16,1024]{1,0:T(8,128)S(1)}, f32[16,1024]{1,0:T(8,128)S(1)}, u32[]{:S(2)}, u32[]{:S(2)}) collective-permute-start(f32[16,1024]{1,0:T(8,128)S(1)} %add_add_fusion.3.refs_1_), channel_id=1, source_target_pairs={{0,8},{8,0},{16,24},{24,16},{1,9},{9,1},{17,25},{25,17},{2,10},{10... | collective-permute-start | bytes 196616 | tf_op jit(solution)/shard_map/ppermute | solution.py:336
  168.8 12.4 %collective-permute-start.46 = (f32[16,1024]{1,0:T(8,128)S(1)}, f32[16,1024]{1,0:T(8,128)S(1)}, u32[]{:S(2)}, u32[]{:S(2)}) collective-permute-start(f32[16,1024]{1,0:T(8,128)S(1)} %add_add_fusion.3.refs_1_), channel_id=1, source_target_pairs={{0,16},{8,24},{16,0},{24,8},{1,17},{9,25},{17,1},{25,9},{2,18},{10... | collective-permute-start | bytes 196616 | tf_op jit(solution)/shard_map/ppermute | solution.py:336
  171.4 9.9 %collective-permute-start.47 = (f32[16,1024]{1,0:T(8,128)S(1)}, f32[16,1024]{1,0:T(8,128)S(1)}, u32[]{:S(2)}, u32[]{:S(2)}) collective-permute-start(f32[16,1024]{1,0:T(8,128)S(1)} %add_add_fusion.3.refs_1_), channel_id=1, source_target_pairs={{0,24},{8,16},{16,8},{24,0},{1,25},{9,17},{17,9},{25,1},{2,26},{10... | collective-permute-start | bytes 196616 | tf_op jit(solution)/shard_map/ppermute | solution.py:336
  192.8 7.9 %collective-permute-start.56 = (f32[16,2048]{1,0:T(8,128)S(1)}, f32[16,2048]{1,0:T(8,128)S(1)}, u32[]{:S(2)}, u32[]{:S(2)}) collective-permute-start(f32[16,2048]{1,0:T(8,128)S(1)} %get-tuple-element.97), channel_id=1, source_target_pairs={{0,4},{1,5},{2,6},{3,7},{4,0},{5,1},{6,2},{7,3},{8,12},{9,13},{10,... | collective-permute-start | bytes 393224 | tf_op jit(solution)/shard_map/ppermute | solution.py:336
  218.9 14.4 %collective-permute-start.62 = (f32[16,1152]{1,0:T(8,128)S(1)}, f32[16,1152]{1,0:T(8,128)S(1)}, u32[]{:S(2)}, u32[]{:S(2)}) collective-permute-start(f32[16,1152]{1,0:T(8,128)S(1)} %get-tuple-element.102), channel_id=1, source_target_pairs={{0,8},{8,0},{16,24},{24,16},{1,9},{9,1},{17,25},{25,17},{2,10},{10... | collective-permute-start | bytes 221192 | tf_op jit(solution)/shard_map/ppermute | solution.py:336
  221.9 13.7 %collective-permute-start.63 = (f32[16,1152]{1,0:T(8,128)S(1)}, f32[16,1152]{1,0:T(8,128)S(1)}, u32[]{:S(2)}, u32[]{:S(2)}) collective-permute-start(f32[16,1152]{1,0:T(8,128)S(1)} %get-tuple-element.103), channel_id=1, source_target_pairs={{0,16},{8,24},{16,0},{24,8},{1,17},{9,25},{17,1},{25,9},{2,18},{10... | collective-permute-start | bytes 221192 | tf_op jit(solution)/shard_map/ppermute | solution.py:336
  222.0 13.5 %collective-permute-start.64 = (f32[16,1152]{1,0:T(8,128)S(1)}, f32[16,1152]{1,0:T(8,128)S(1)}, u32[]{:S(2)}, u32[]{:S(2)}) collective-permute-start(f32[16,1152]{1,0:T(8,128)S(1)} %get-tuple-element.104), channel_id=1, source_target_pairs={{0,24},{8,16},{16,8},{24,0},{1,25},{9,17},{17,9},{25,1},{2,26},{10... | collective-permute-start | bytes 221192 | tf_op jit(solution)/shard_map/ppermute | solution.py:336
  232.2 8.8 %collective-permute-start.69 = (f32[16,1024]{1,0:T(8,128)S(1)}, f32[16,1024]{1,0:T(8,128)S(1)}, u32[]{:S(2)}, u32[]{:S(2)}) collective-permute-start(f32[16,1024]{1,0:T(8,128)S(1)} %get-tuple-element.108), channel_id=1, source_target_pairs={{0,16},{8,24},{16,0},{24,8},{1,17},{9,25},{17,1},{25,9},{2,18},{10... | collective-permute-start | bytes 196616 | tf_op jit(solution)/shard_map/ppermute | solution.py:336
  235.6 11.1 %collective-permute-start.65 = (f32[16,1024]{1,0:T(8,128)S(1)}, f32[16,1024]{1,0:T(8,128)S(1)}, u32[]{:S(2)}, u32[]{:S(2)}) collective-permute-start(f32[16,1024]{1,0:T(8,128)S(1)} %get-tuple-element.105.refs_0_), channel_id=1, source_target_pairs={{0,8},{8,0},{16,24},{24,16},{1,9},{9,1},{17,25},{25,17},{2,10},{10... | collective-permute-start | bytes 196616 | tf_op jit(solution)/shard_map/ppermute | solution.py:336
  235.8 13.2 %collective-permute-start.66 = (f32[16,1024]{1,0:T(8,128)S(1)}, f32[16,1024]{1,0:T(8,128)S(1)}, u32[]{:S(2)}, u32[]{:S(2)}) collective-permute-start(f32[16,1024]{1,0:T(8,128)S(1)} %get-tuple-element.105.refs_0_), channel_id=1, source_target_pairs={{0,16},{8,24},{16,0},{24,8},{1,17},{9,25},{17,1},{25,9},{2,18},{10... | collective-permute-start | bytes 196616 | tf_op jit(solution)/shard_map/ppermute | solution.py:336
  237.8 11.2 %collective-permute-start.67 = (f32[16,1024]{1,0:T(8,128)S(1)}, f32[16,1024]{1,0:T(8,128)S(1)}, u32[]{:S(2)}, u32[]{:S(2)}) collective-permute-start(f32[16,1024]{1,0:T(8,128)S(1)} %get-tuple-element.105.refs_0_), channel_id=1, source_target_pairs={{0,24},{8,16},{16,8},{24,0},{1,25},{9,17},{17,9},{25,1},{2,26},{10... | collective-permute-start | bytes 196616 | tf_op jit(solution)/shard_map/ppermute | solution.py:336
  241.1 8.0 %collective-permute-start.71 = (f32[16,1024]{1,0:T(8,128)S(1)}, f32[16,1024]{1,0:T(8,128)S(1)}, u32[]{:S(2)}, u32[]{:S(2)}) collective-permute-start(f32[16,1024]{1,0:T(8,128)S(1)} %update.7.refs_4_), channel_id=1, source_target_pairs={{0,8},{8,0},{16,24},{24,16},{1,9},{9,1},{17,25},{25,17},{2,10},{10... | collective-permute-start | bytes 196616 | tf_op jit(solution)/shard_map/ppermute | solution.py:336
  (46 other events, 389.1 us)

commit v3 on v2

--- a/solution.py
+++ b/solution.py
@@ -18,11 +18,11 @@
 NT = (((1,), (1,)), ((), ()))
 WHOLE = pl.BlockSpec(memory_space=pltpu.VMEM)
 FAR = pl.BlockSpec(memory_space=pltpu.HBM)
-VMEM_LIMIT = 26 << 20
-TILE_LIMIT = 62 << 20
-NEAR_LIMIT = 26 << 20
-SMALL_LIMIT = 8 << 20
-IN_FLIGHT = 12 << 20
+VMEM_LIMIT = 13 << 20
+TILE_LIMIT = 30 << 20
+NEAR_LIMIT = 13 << 20
+SMALL_LIMIT = 6 << 20
+IN_FLIGHT = 6 << 20
 
 
 def dot(a, b, dims):
@@ -50,6 +50,8 @@
 
 
 def rows_at(start, count):
+    if isinstance(start, int):
+        return pl.ds(start, count)
     return pl.ds(pl.multiple_of(start, count), count)
 
 
@@ -104,20 +106,45 @@
     lax.fori_loop(0, blocks, one, 0)
 
 
-def call(kernel, weights, others, outs, scratch, count, size, n_lanes, out, name, limit):
-    n_in, n_out, n_scratch = len(others), len(outs), len(scratch)
+def stream_near(sources, size, use):
+    for ref, first, count, at in sources:
+
+        def one(i, carry, ref=ref, first=first, at=at):
+            use(pl.ds(pl.multiple_of(at + i * size, size), size), ref[first + i])
+            return carry
+
+        lax.fori_loop(0, count, one, 0)
+
+
+def call(kernel, weights, others, outs, scratch, count, size, n_lanes, out, name, limit, near=False, keep=False):
+    weights = list(weights) if near else [weights]
+    n_weights, n_in, n_out, n_scratch = len(weights), len(others), len(outs), len(scratch)
 
     def whole(*refs):
-        ins, rest = refs[1 : 1 + n_in], refs[1 + n_in :]
-        held, sems = rest[n_out + n_scratch :]
-        kernel(refs[0], ins, rest[:n_out], rest[n_out : n_out + n_scratch], held, sems)
+        ins, rest = refs[n_weights : n_weights + n_in], refs[n_weights + n_in :]
+        if near:
+            held = sems = None
+        elif keep:
+            held, sems = rest[n_out], rest[-1]
+        else:
+            held, sems = rest[n_out + n_scratch :]
+        first = n_out + (1 if keep else 0)
+        kernel(refs[:n_weights], ins, rest[:n_out], rest[first : first + n_scratch], held, sems)
 
     slots = max(2, min(count // size, IN_FLIGHT // (4 * size * n_lanes)))
-    scratch = list(scratch) + [pltpu.VMEM((slots, size, n_lanes), f32), pltpu.SemaphoreType.DMA((slots,))]
+    scratch = list(scratch)
+    outs = list(outs)
+    if keep:
+        slots = count // size
+        outs.append((slots, size, n_lanes))
+    elif not near:
+        scratch.append(pltpu.VMEM((slots, size, n_lanes), f32))
+    if not near:
+        scratch.append(pltpu.SemaphoreType.DMA((slots,)))
     return pl.pallas_call(
         whole,
-        in_specs=[FAR] + [WHOLE] * n_in,
-        out_specs=[WHOLE] * n_out,
+        in_specs=[WHOLE if near else FAR] * n_weights + [WHOLE] * n_in,
+        out_specs=[WHOLE] * len(outs),
         out_shape=[jax.ShapeDtypeStruct(shape, f32) for shape in outs],
         scratch_shapes=scratch,
         compiler_params=pltpu.CompilerParams(vmem_limit_bytes=limit),
@@ -125,10 +152,10 @@
             flops=6 * out * count * n_lanes, bytes_accessed=4 * count * n_lanes, transcendentals=0
         ),
         name=name,
-    )(weights, *others)
-
-
-def down(weights, pieces, places, out, first, count, lanes, name, chunks=0, before=None, squares=None, limit=VMEM_LIMIT):
+    )(*weights, *others)
+
+
+def down(weights, pieces, places, out, first, count, lanes, name, chunks=0, before=None, squares=None, limit=VMEM_LIMIT, near=None):
     size = block_of(count, 512)
     n_lanes = lanes.stop - lanes.start
     n_pieces = len(pieces)
@@ -150,7 +177,10 @@
 
         total[...] = jnp.zeros_like(total) if before is None else ins[n_pieces][...]
         stage(ins[:n_pieces], places, full, parts)
-        stream(w_ref, held, sems, first, count, size, lanes, use)
+        if near is None:
+            stream(w_ref[0], held, sems, first, count, size, lanes, use)
+        else:
+            stream_near([(ref, *rest) for ref, rest in zip(w_ref, near(size))], size, use)
         if not chunks:
             out_refs[0][...] = total[...]
         for k in range(chunks):
@@ -164,12 +194,13 @@
                 out_refs[k][:, n_lanes : n_lanes + extra] = jnp.full((share, extra), sum_sq, f32)
 
     scratch = [pltpu.VMEM((out, count), f32), pltpu.VMEM((2 * out, count), bf16), pltpu.VMEM((out, n_lanes), f32)]
-    return call(kernel, weights, others, outs, scratch, count, size, n_lanes, out, name, limit)
-
-
-def across(weights, pieces, places, out, first, count, lanes, name, before=None, halves=False, limit=VMEM_LIMIT):
+    return call(kernel, weights, others, outs, scratch, count, size, n_lanes, out, name, limit, near is not None)
+
+
+def across(weights, pieces, places, out, first, count, lanes, name, before=None, halves=False, limit=VMEM_LIMIT, near=False, keep=False):
     width = lanes.stop - lanes.start
     size = block_of(count, 512)
+    weights = [weights] if near else weights
     half = out // 2
     n_pieces = len(pieces)
     outs = [(half, count)] * 2 if halves else [(out, count)]
@@ -188,7 +219,10 @@
             total[:, at] = sums
 
         stage(ins[:n_pieces], places, full, parts)
-        stream(w_ref, held, sems, first, count, size, lanes, use)
+        if near:
+            stream_near([(w_ref[0], 0, count // size, 0)], size, use)
+        else:
+            stream(w_ref[0], held, sems, first, count, size, lanes, use)
         if halves:
             core = core_of()
             out_refs[0][...] = total[rows_at((1 - core) * half, half), :]
@@ -196,7 +230,7 @@
 
     scratch = [pltpu.VMEM((out, width), f32), pltpu.VMEM((2 * out, width), bf16)]
     scratch += [pltpu.VMEM((out, count), f32)] if halves else []
-    return call(kernel, weights, others, outs, scratch, count, size, width, out, name, limit)
+    return call(kernel, weights, others, outs, scratch, count, size, width, out, name, limit, near, keep)
 
 
 def tile_and_logits(features, centers, coeffs):
@@ -289,6 +323,49 @@
     )(first, second)
 
 
+def small(kernel, others, outs, name):
+    return pl.pallas_call(
+        kernel,
+        in_specs=[WHOLE] * len(others),
+        out_specs=[WHOLE] * len(outs),
+        out_shape=[jax.ShapeDtypeStruct(shape, f32) for shape in outs],
+        compiler_params=pltpu.CompilerParams(vmem_limit_bytes=SMALL_LIMIT),
+        name=name,
+    )(*others)
+
+
+def add_up(terms, name):
+    def kernel(*refs):
+        total = refs[0][...]
+        for ref in refs[1:-1]:
+            total = total + ref[...]
+        refs[-1][...] = total
+
+    return small(kernel, terms, [terms[0].shape], name)[0]
+
+
+def residuals(logits, labels, rows_total):
+    half = logits[0].shape[0]
+
+    def kernel(*refs):
+        total = refs[0][...]
+        for ref in refs[1:-2]:
+            total = total + ref[...]
+        targets = refs[-2][rows_at(core_of() * half, half), :].astype(f32)
+        refs[-1][...] = (jax.nn.sigmoid(total) - targets) / rows_total
+
+    return small(kernel, [*logits, labels], [logits[0].shape], "resid")[0]
+
+
+def rank_share(a, share, lanes):
+    def kernel(a_ref, *outs):
+        at = rows_at(lax.axis_index("rows") * share, share)
+        for out, cut in zip(outs, lanes):
+            out[...] = a_ref[at, cut]
+
+    return small(kernel, [a], [(share, cut.stop - cut.start) for cut in lanes], "share")
+
+
 def update(cuts, a, elements, scale=None):
     rows, count = a.shape
     n_cuts = len(cuts)
@@ -352,12 +429,8 @@
     left, right = slice(0, cols), slice(cols, count)
     every = slice(None)
 
-    rank = lax.axis_index("rows")
-    core = core_of()
-    targets = lax.dynamic_slice_in_dim(labels.T, core * half, half, 0).astype(f32)
     a = coeffs.T
-    a_share = lax.dynamic_slice_in_dim(a, rank * share, share, 0)
-    a_halves = [a_share[:, left], a_share[:, right]]
+    a_halves = rank_share(a, share, (left, right))
 
     def core_places():
         me = core_of()
@@ -374,8 +447,11 @@
 
     def chip_places_both():
         me = core_of()
-        lanes = [pl.ds(pl.multiple_of(who * row_half, row_half), row_half) for who in (me, 1 - me)]
-        return [(at, both) for both in lanes for at, _ in chip_places()]
+        own, other = [pl.ds(pl.multiple_of(who * row_half, row_half), row_half) for who in (me, 1 - me)]
+        return [(at, own) for at, _ in chip_places()] + [(0, other)]
+
+    def whole_place():
+        return [(0, every)]
 
     def my_rows():
         return core_of() * row_half
@@ -385,12 +461,6 @@
 
     def to_rank(cuts):
         return [cuts[0]] + [swap(cuts[k], "rows", k) for k in range(1, depth_ranks)]
-
-    def sum_of(cuts):
-        total = cuts[0]
-        for cut in cuts[1:]:
-            total = total + cut
-        return total
 
     def all_rows(x):
         return [x] + [swap(x, "rows", k) for k in range(1, depth_ranks)]
@@ -403,31 +473,51 @@
             theirs, mine = across(
                 tile, a_pieces, rank_places_both, out, 0, rows_here, slice(0, count), "logits", halves=True, limit=NEAR_LIMIT
             )
-        logits = mine + swap(theirs, "centers", 1)
-        full = logits
-        for k in range(1, chips):
-            full = full + swap(logits, "centers", 2 * k)
-        resid = (jax.nn.sigmoid(full) - targets) / rows_total
+        logits = add_up([mine, swap(theirs, "centers", 1)], "chip_logits")
+        logits = [logits] + [swap(logits, "centers", 2 * k) for k in range(1, chips)]
+        resid = residuals(logits, labels.T, rows_total)
         resids = [resid, swap(resid, "centers", 1)]
         grads = []
         for lanes, name in ((left, "grada"), (right, "gradb")):
             cuts = down(tile, resids, core_places, out, 0, rows_here, lanes, name, chunks=depth_ranks, limit=NEAR_LIMIT)
-            grads.append(all_rows(sum_of(to_rank(cuts))))
-        (begun,) = across(precond, grads[0], rank_places, out, 0, p_rows, left, "fwda")
-        (theirs,) = across(precond, grads[1], rank_places, out, other_rows, row_half, right, "fwdb", before=begun)
-        (mine,) = across(precond, grads[1], rank_places, out, my_rows, row_half, right, "fwdc", before=begun)
+            grads.append(all_rows(add_up(to_rank(cuts), "grad_sum")))
+        places = rank_places
+        if step == 0:
+            begun, near_left = across(precond, grads[0], places, out, 0, p_rows, left, "fwda", keep=True)
+            theirs, near_other = across(
+                precond, grads[1], places, out, other_rows, row_half, right, "fwdb", before=begun, keep=True
+            )
+            mine, near_mine = across(
+                precond, grads[1], places, out, my_rows, row_half, right, "fwdc", before=begun, keep=True
+            )
+        else:
+            (begun,) = across(near_left, grads[0], places, out, 0, p_rows, left, "fwda", near=True)
+            (theirs,) = across(
+                near_other, grads[1], places, out, other_rows, row_half, right, "fwdb", before=begun, near=True
+            )
+            (mine,) = across(
+                near_mine, grads[1], places, out, my_rows, row_half, right, "fwdc", before=begun, near=True
+            )
         cuts = add_and_cut(mine, swap(theirs, "centers", 1), chips, "cut")
-        fwd = cuts[0]
-        for k in range(1, chips):
-            fwd = fwd + swap(cuts[k], "centers", 2 * k)
+        fwd = add_up([cuts[0]] + [swap(cuts[k], "centers", 2 * k) for k in range(1, chips)], "fwd_sum")
         fwds = [fwd] + [swap(fwd, "centers", 2 * k) for k in range(1, chips)]
-        others = swap(jnp.concatenate(fwds, axis=0), "centers", 1)
-        others = [others[k * part : (k + 1) * part] for k in range(chips)]
-        begun, squares = down(precond, fwds, chip_places, out, my_rows, row_half, left, "backa", squares="sum")
+        others = [swap(assemble(fwds, chip_places, (out, row_half), "fwd_mine"), "centers", 1)]
+        begun, squares = down(
+            [near_left],
+            fwds,
+            chip_places,
+            out,
+            my_rows,
+            row_half,
+            left,
+            "backa",
+            squares="sum",
+            near=lambda size: [(my_rows() // size, row_half // size, 0)],
+        )
         cuts = down(
-            precond,
+            [near_left],
             others,
-            chip_places,
+            whole_place,
             out,
             other_rows,
             row_half,
@@ -436,10 +526,20 @@
             chunks=depth_ranks,
             before=begun,
             squares=squares,
+            near=lambda size: [(other_rows() // size, row_half // size, 0)],
         )
         first, scale = update(to_rank(cuts), a_halves[0], center_total * out)
         cuts = down(
-            precond, fwds + others, chip_places_both, out, 0, p_rows, right, "backc", chunks=depth_ranks
+            [near_mine, near_other],
+            fwds + others,
+            chip_places_both,
+            out,
+            0,
+            p_rows,
+            right,
+            "backc",
+            chunks=depth_ranks,
+            near=lambda size: [(0, row_half // size, my_rows()), (0, row_half // size, other_rows())],
         )
         (second,) = update(to_rank(cuts), a_halves[1], center_total * out, scale)
         a_halves = [first, second]

time: 254 us -> 233 us (0.917)
  Pallas kernels: 89.9 us -> 71.3 us
  starting transfers between devices: 104 us -> 108 us
  waiting for transfers between devices: 52.9 us -> 50.3 us
    pallas_call x17 -> x28, Pallas kernels: 78.9 us -> 62.4 us  [the longest x17 62.1 us: call(): pl.pallas_call(whole, in_specs=[WHOLE if near else FAR] * n_weights + [WH...]
    ppermute x74, starting transfers between devices: 104 us -> 108 us  [swap(): return lax.ppermute(x, axis, [(i, i ^ mask) for i in range(size)])]
    ppermute x74, waiting for transfers between devices: 52.9 us -> 50.3 us  [swap(): return lax.ppermute(x, axis, [(i, i ^ mask) for i in range(size)])]
  transfers between devices with their start and end apart: 74 -> 74, of which waited for: 26 -> 24; matrix products, arithmetic and copies ran while one was open for 0% -> 0% of each run, Pallas kernels for 21% -> 18%
where the time goes in v3:
time: 233 us
  starting transfers between devices  108 us (46%)
  Pallas kernels  71.3 us (31%)
  waiting for transfers between devices  50.3 us (22%)
  local copies, waits for them, and re-layouts  3.37 us (1%)
    ppermute x74, starting transfers between devices, swap(): return lax.ppermute(x, axis, [(i, i ^ mask) for i in range(size)])  108 us
    pallas_call x17, Pallas kernels, call(): pl.pallas_call(whole, in_specs=[WHOLE if near else FAR] * n_weights + [WH...  62.1 us
    ppermute x74, waiting for transfers between devices, swap(): return lax.ppermute(x, axis, [(i, i ^ mask) for i in range(size)])  50.3 us
    pallas_call x1, Pallas kernels, tile_and_logits(): pl.pallas_call(kernel, grid=(rows // size,), in_specs=[pl.BlockSpec((size...  7.57 us
  transfers between devices with their start and end apart: 74, of which 24 were waited for; matrix products, arithmetic and copies ran while one was open for 0% of the time, Pallas kernels for 18%

profile of v3, /device:TPU:0, one launch (start us, length us, event | category | flops | bytes accessed | tf_op | source)
XLA Modules:
  0.0 233.3 jit_solution(355742383398919910)
XLA Ops:
  3.4 7.6 %tile_and_logits.1 = (f32[1024,2048]{1,0:T(8,128)S(1)}, f32[32,1024]{1,0:T(8,128)S(1)}, f32[32,1024]{1,0:T(8,128)S(1)}) custom-call(f32[1024,128]{1,0:T(8,128)S(1)} %copy-done.5, f32[2048,128]{1,0:T(8,128)S(1)} %copy-done.4, f32[64,2048]{1,0:T(8,128)S(1)} %bitcast.7), custom_call_target="tpu_custom_call" | custom-call | flops 3221225472 | bytes 8388608 | tf_op jit(solution)/shard_map/tile_and_logits/pallas_call | solution.py:274
  12.5 2.9 %collective-permute-start.1 = (f32[32,1024]{1,0:T(8,128)S(1)}, f32[32,1024]{1,0:T(8,128)S(1)}, u32[]{:S(2)}, u32[]{:S(2)}) collective-permute-start(f32[32,1024]{1,0:T(8,128)S(1)} %chip_logits.2.refs_0_), channel_id=1, source_target_pairs={{0,2},{1,3},{2,0},{3,1},{4,6},{5,7},{6,4},{7,5},{8,10},{9,11},{10,... | collective-permute-start | bytes 393224 | tf_op jit(solution)/shard_map/ppermute | solution.py:413
  19.3 4.2 %collective-permute-done.2.refs_2_ = f32[32,1024]{1,0:T(8,128)S(1)} collective-permute-done((f32[32,1024]{1,0:T(8,128)S(1)}, f32[32,1024]{1,0:T(8,128)S(1)}, u32[]{:S(2)}, u32[]{:S(2)}) %collective-permute-start.2) | collective-permute-done | bytes 131104 | tf_op jit(solution)/shard_map/ppermute | solution.py:413
  28.7 2.6 %collective-permute-start.6 = (f32[16,1024]{1,0:T(8,128)S(1)}, f32[16,1024]{1,0:T(8,128)S(1)}, u32[]{:S(2)}, u32[]{:S(2)}) collective-permute-start(f32[16,1024]{1,0:T(8,128)S(1)} %get-tuple-element.71), channel_id=1, source_target_pairs={{0,16},{8,24},{16,0},{24,8},{1,17},{9,25},{17,1},{25,9},{2,18},{10... | collective-permute-start | bytes 196616 | tf_op jit(solution)/shard_map/ppermute | solution.py:413
  34.5 3.5 %collective-permute-start.12 = (f32[16,1024]{1,0:T(8,128)S(1)}, f32[16,1024]{1,0:T(8,128)S(1)}, u32[]{:S(2)}, u32[]{:S(2)}) collective-permute-start(f32[16,1024]{1,0:T(8,128)S(1)} %get-tuple-element.76), channel_id=1, source_target_pairs={{0,16},{8,24},{16,0},{24,8},{1,17},{9,25},{17,1},{25,9},{2,18},{10... | collective-permute-start | bytes 196616 | tf_op jit(solution)/shard_map/ppermute | solution.py:413
  38.6 3.8 %collective-permute-start.9 = (f32[16,1024]{1,0:T(8,128)S(1)}, f32[16,1024]{1,0:T(8,128)S(1)}, u32[]{:S(2)}, u32[]{:S(2)}) collective-permute-start(f32[16,1024]{1,0:T(8,128)S(1)} %grad_sum.4.refs_1_), channel_id=1, source_target_pairs={{0,16},{8,24},{16,0},{24,8},{1,17},{9,25},{17,1},{25,9},{2,18},{10... | collective-permute-start | bytes 196616 | tf_op jit(solution)/shard_map/ppermute | solution.py:413
  44.1 2.9 %collective-permute-start.14 = (f32[16,1024]{1,0:T(8,128)S(1)}, f32[16,1024]{1,0:T(8,128)S(1)}, u32[]{:S(2)}, u32[]{:S(2)}) collective-permute-start(f32[16,1024]{1,0:T(8,128)S(1)} %grad_sum.5.refs_1_), channel_id=1, source_target_pairs={{0,8},{8,0},{16,24},{24,16},{1,9},{9,1},{17,25},{25,17},{2,10},{10... | collective-permute-start | bytes 196616 | tf_op jit(solution)/shard_map/ppermute | solution.py:413
  47.0 3.2 %collective-permute-start.15 = (f32[16,1024]{1,0:T(8,128)S(1)}, f32[16,1024]{1,0:T(8,128)S(1)}, u32[]{:S(2)}, u32[]{:S(2)}) collective-permute-start(f32[16,1024]{1,0:T(8,128)S(1)} %grad_sum.5.refs_1_), channel_id=1, source_target_pairs={{0,16},{8,24},{16,0},{24,8},{1,17},{9,25},{17,1},{25,9},{2,18},{10... | collective-permute-start | bytes 196616 | tf_op jit(solution)/shard_map/ppermute | solution.py:413
  51.6 8.0 %fwda.2 = (f32[64,4096]{1,0:T(8,128)S(1)}, f32[8,512,1024]{2,1,0:T(8,128)S(1)}) custom-call(f32[4096,2048]{1,0:T(8,128)} %refs_0_.5, f32[16,1024]{1,0:T(8,128)S(1)} %grad_sum.4.refs_1_, f32[16,1024]{1,0:T(8,128)S(1)} %collective-permute-done.8.refs_2_, f32[16,1024]{1,0:T(8,128)S(1)} %collective-permute-done.9.refs_3_, ...), custom_call_target="tpu_custom_call" | custom-call | flops 1610612736 | bytes 16777216 | tf_op jit(solution)/shard_map/fwda/pallas_call | solution.py:144
  59.6 4.8 %fwdb.2 = (f32[64,2048]{1,0:T(8,128)S(1)}, f32[4,512,1024]{2,1,0:T(8,128)S(1)}) custom-call(f32[4096,2048]{1,0:T(8,128)} %refs_0_.5, f32[16,1024]{1,0:T(8,128)S(1)} %grad_sum.5.refs_1_, f32[16,1024]{1,0:T(8,128)S(1)} %collective-permute-done.14.refs_2_, f32[16,1024]{1,0:T(8,128)S(1)} %collective-permute-done.15.refs_3_, ...), custom_call_target="tpu_custom_call" | custom-call | flops 805306368 | bytes 8388608 | tf_op jit(solution)/shard_map/fwdb/pallas_call | solution.py:144
  64.6 4.9 %fwdc.2 = (f32[64,2048]{1,0:T(8,128)S(1)}, f32[4,512,1024]{2,1,0:T(8,128)S(1)}) custom-call(f32[4096,2048]{1,0:T(8,128)} %refs_0_.5, f32[16,1024]{1,0:T(8,128)S(1)} %grad_sum.5.refs_1_, f32[16,1024]{1,0:T(8,128)S(1)} %collective-permute-done.14.refs_2_, f32[16,1024]{1,0:T(8,128)S(1)} %collective-permute-done.15.refs_3_, ...), custom_call_target="tpu_custom_call" | custom-call | flops 805306368 | bytes 8388608 | tf_op jit(solution)/shard_map/fwdc/pallas_call | solution.py:144
  73.1 2.8 %collective-permute-done.18.refs_1_ = f32[16,2048]{1,0:T(8,128)S(1)} collective-permute-done((f32[16,2048]{1,0:T(8,128)S(1)}, f32[16,2048]{1,0:T(8,128)S(1)}, u32[]{:S(2)}, u32[]{:S(2)}) %collective-permute-start.18) | collective-permute-done | bytes 131104 | tf_op jit(solution)/shard_map/ppermute | solution.py:413
  82.8 2.9 %collective-permute-done.21.refs_1_.refs_2_.refs_3_ = f32[16,2048]{1,0:T(8,128)S(1)} collective-permute-done((f32[16,2048]{1,0:T(8,128)S(1)}, f32[16,2048]{1,0:T(8,128)S(1)}, u32[]{:S(2)}, u32[]{:S(2)}) %collective-permute-start.21) | collective-permute-done | bytes 131104 | tf_op jit(solution)/shard_map/ppermute | solution.py:413
  97.6 4.7 %backc.2 = (f32[16,1024]{1,0:T(8,128)S(1)}, f32[16,1024]{1,0:T(8,128)S(1)}, f32[16,1024]{1,0:T(8,128)S(1)}, f32[16,1024]{1,0:T(8,128)S(1)}) custom-call(f32[4,512,1024]{2,1,0:T(8,128)S(1)} %get-tuple-element.79.refs_0_, f32[4,512,1024]{2,1,0:T(8,128)S(1)} %get-tuple-element.94.refs_1_.refs_0_, f32[16,2048]{1,0:T(8,128)S(1)} %fwd_sum.2.refs_0_.refs_1_.refs_2_, ...), custom_call_target="tpu_custom_call" | custom-call | flops 1610612736 | bytes 16777216 | tf_op jit(solution)/shard_map/backc/pallas_call | solution.py:144
  102.3 3.0 %collective-permute-start.32 = (f32[16,1024]{1,0:T(8,128)S(1)}, f32[16,1024]{1,0:T(8,128)S(1)}, u32[]{:S(2)}, u32[]{:S(2)}) collective-permute-start(f32[16,1024]{1,0:T(8,128)S(1)} %get-tuple-element.97), channel_id=1, source_target_pairs={{0,16},{8,24},{16,0},{24,8},{1,17},{9,25},{17,1},{25,9},{2,18},{10... | collective-permute-start | bytes 196616 | tf_op jit(solution)/shard_map/ppermute | solution.py:413
  106.9 3.0 %collective-permute-start.29 = (f32[16,1024]{1,0:T(8,128)S(1)}, f32[16,1024]{1,0:T(8,128)S(1)}, u32[]{:S(2)}, u32[]{:S(2)}) collective-permute-start(f32[16,1024]{1,0:T(8,128)S(1)} %get-tuple-element.93.refs_1_.refs_4_), channel_id=1, source_target_pairs={{0,16},{8,24},{16,0},{24,8},{1,17},{9,25},{17,1},{25,9},{2,18},{10... | collective-permute-start | bytes 196616 | tf_op jit(solution)/shard_map/ppermute | solution.py:413
  111.9 3.2 %collective-permute-start.34 = (f32[16,1024]{1,0:T(8,128)S(1)}, f32[16,1024]{1,0:T(8,128)S(1)}, u32[]{:S(2)}, u32[]{:S(2)}) collective-permute-start(f32[16,1024]{1,0:T(8,128)S(1)} %update.5.refs_5_.refs_4_), channel_id=1, source_target_pairs={{0,8},{8,0},{16,24},{24,16},{1,9},{9,1},{17,25},{25,17},{2,10},{10... | collective-permute-start | bytes 196616 | tf_op jit(solution)/shard_map/ppermute | solution.py:413
  115.2 2.9 %collective-permute-start.35 = (f32[16,1024]{1,0:T(8,128)S(1)}, f32[16,1024]{1,0:T(8,128)S(1)}, u32[]{:S(2)}, u32[]{:S(2)}) collective-permute-start(f32[16,1024]{1,0:T(8,128)S(1)} %update.5.refs_5_.refs_4_), channel_id=1, source_target_pairs={{0,16},{8,24},{16,0},{24,8},{1,17},{9,25},{17,1},{25,9},{2,18},{10... | collective-permute-start | bytes 196616 | tf_op jit(solution)/shard_map/ppermute | solution.py:413
  120.8 3.5 %collective-permute-done.36.refs_8_ = f32[16,1024]{1,0:T(8,128)S(1)} collective-permute-done((f32[16,1024]{1,0:T(8,128)S(1)}, f32[16,1024]{1,0:T(8,128)S(1)}, u32[]{:S(2)}, u32[]{:S(2)}) %collective-permute-start.36) | collective-permute-done | bytes 65568 | tf_op jit(solution)/shard_map/ppermute | solution.py:413
  124.2 3.6 %logits.1 = (f32[32,1024]{1,0:T(8,128)S(1)}, f32[32,1024]{1,0:T(8,128)S(1)}) custom-call(f32[1024,2048]{1,0:T(8,128)S(1)} %get-tuple-element.66.refs_0_, f32[16,1024]{1,0:T(8,128)S(1)} %get-tuple-element.93.refs_1_.refs_4_, f32[16,1024]{1,0:T(8,128)S(1)} %collective-permute-done.28.refs_2_, f32[16,1024]{1,0:T(8,128)S(1)} %collective-permute-done.29.refs_3_, ...), custom_call_target="tpu_custom_call" | custom-call | flops 805306368 | bytes 8388608 | tf_op jit(solution)/shard_map/logits/pallas_call | solution.py:144
  132.9 2.9 %collective-permute-done.38.refs_1_ = f32[32,1024]{1,0:T(8,128)S(1)} collective-permute-done((f32[32,1024]{1,0:T(8,128)S(1)}, f32[32,1024]{1,0:T(8,128)S(1)}, u32[]{:S(2)}, u32[]{:S(2)}) %collective-permute-start.38) | collective-permute-done | bytes 131104 | tf_op jit(solution)/shard_map/ppermute | solution.py:413
  135.7 2.8 %collective-permute-done.39.refs_2_ = f32[32,1024]{1,0:T(8,128)S(1)} collective-permute-done((f32[32,1024]{1,0:T(8,128)S(1)}, f32[32,1024]{1,0:T(8,128)S(1)}, u32[]{:S(2)}, u32[]{:S(2)}) %collective-permute-start.39) | collective-permute-done | bytes 131104 | tf_op jit(solution)/shard_map/ppermute | solution.py:413
  158.0 5.5 %collective-permute-start.45 = (f32[16,1024]{1,0:T(8,128)S(1)}, f32[16,1024]{1,0:T(8,128)S(1)}, u32[]{:S(2)}, u32[]{:S(2)}) collective-permute-start(f32[16,1024]{1,0:T(8,128)S(1)} %grad_sum.6.refs_1_), channel_id=1, source_target_pairs={{0,8},{8,0},{16,24},{24,16},{1,9},{9,1},{17,25},{25,17},{2,10},{10... | collective-permute-start | bytes 196616 | tf_op jit(solution)/shard_map/ppermute | solution.py:413
  166.0 6.4 %fwda.3.refs_5_ = f32[64,4096]{1,0:T(8,128)S(1)} custom-call(f32[8,512,1024]{2,1,0:T(8,128)S(1)} %get-tuple-element.73.refs_0_, f32[16,1024]{1,0:T(8,128)S(1)} %grad_sum.7.refs_1_, f32[16,1024]{1,0:T(8,128)S(1)} %collective-permute-done.51.refs_2_, f32[16,1024]{1,0:T(8,128)S(1)} %collective-permute-done.52.refs_3_, ...), custom_call_target="tpu_custom_call" | custom-call | flops 1610612736 | bytes 16777216 | tf_op jit(solution)/shard_map/fwda/pallas_call | solution.py:144
  172.4 3.2 %fwdb.3 = f32[64,2048]{1,0:T(8,128)S(1)} custom-call(f32[4,512,1024]{2,1,0:T(8,128)S(1)} %get-tuple-element.94.refs_1_.refs_0_, f32[16,1024]{1,0:T(8,128)S(1)} %grad_sum.6.refs_1_, f32[16,1024]{1,0:T(8,128)S(1)} %collective-permute-done.45.refs_2_, f32[16,1024]{1,0:T(8,128)S(1)} %collective-permute-done.46.refs_3_, ...), custom_call_target="tpu_custom_call" | custom-call | flops 805306368 | bytes 8388608 | tf_op jit(solution)/shard_map/fwdb/pallas_call | solution.py:144
  175.7 3.2 %fwdc.3.a_ref = f32[64,2048]{1,0:T(8,128)S(1)} custom-call(f32[4,512,1024]{2,1,0:T(8,128)S(1)} %bitcast.4, f32[16,1024]{1,0:T(8,128)S(1)} %grad_sum.6.refs_1_, f32[16,1024]{1,0:T(8,128)S(1)} %collective-permute-done.45.refs_2_, f32[16,1024]{1,0:T(8,128)S(1)} %collective-permute-done.46.refs_3_, f32[16,1024]{1,0:T(8,128)S(1)} %collective-permute-done.47.refs_4_, ...), custom_call_target="tpu_custom_call" | custom-call | flops 805306368 | bytes 8388608 | tf_op jit(solution)/shard_map/fwdc/pallas_call | solution.py:144
  182.6 2.8 %collective-permute-done.55.refs_1_ = f32[16,2048]{1,0:T(8,128)S(1)} collective-permute-done((f32[16,2048]{1,0:T(8,128)S(1)}, f32[16,2048]{1,0:T(8,128)S(1)}, u32[]{:S(2)}, u32[]{:S(2)}) %collective-permute-start.55) | collective-permute-done | bytes 131104 | tf_op jit(solution)/shard_map/ppermute | solution.py:413
  185.4 3.1 %collective-permute-done.56.refs_2_ = f32[16,2048]{1,0:T(8,128)S(1)} collective-permute-done((f32[16,2048]{1,0:T(8,128)S(1)}, f32[16,2048]{1,0:T(8,128)S(1)}, u32[]{:S(2)}, u32[]{:S(2)}) %collective-permute-start.56) | collective-permute-done | bytes 131104 | tf_op jit(solution)/shard_map/ppermute | solution.py:413
  194.4 2.9 %collective-permute-done.59.refs_2_.refs_3_.refs_4_ = f32[16,2048]{1,0:T(8,128)S(1)} collective-permute-done((f32[16,2048]{1,0:T(8,128)S(1)}, f32[16,2048]{1,0:T(8,128)S(1)}, u32[]{:S(2)}, u32[]{:S(2)}) %collective-permute-start.59) | collective-permute-done | bytes 131104 | tf_op jit(solution)/shard_map/ppermute | solution.py:413
  206.9 4.5 %backc.3 = (f32[16,1024]{1,0:T(8,128)S(1)}, f32[16,1024]{1,0:T(8,128)S(1)}, f32[16,1024]{1,0:T(8,128)S(1)}, f32[16,1024]{1,0:T(8,128)S(1)}) custom-call(f32[4,512,1024]{2,1,0:T(8,128)S(1)} %bitcast.4, f32[4,512,1024]{2,1,0:T(8,128)S(1)} %get-tuple-element.94.refs_1_.refs_0_, f32[16,2048]{1,0:T(8,128)S(1)} %fwd_sum.3.refs_0_.refs_1_.refs_2_, ...), custom_call_target="tpu_custom_call" | custom-call | flops 1610612736 | bytes 16777216 | tf_op jit(solution)/shard_map/backc/pallas_call | solution.py:144
  220.5 5.7 %collective-permute-start.71 = (f32[16,1024]{1,0:T(8,128)S(1)}, f32[16,1024]{1,0:T(8,128)S(1)}, u32[]{:S(2)}, u32[]{:S(2)}) collective-permute-start(f32[16,1024]{1,0:T(8,128)S(1)} %update.7.refs_4_), channel_id=1, source_target_pairs={{0,8},{8,0},{16,24},{24,16},{1,9},{9,1},{17,25},{25,17},{2,10},{10... | collective-permute-start | bytes 196616 | tf_op jit(solution)/shard_map/ppermute | solution.py:413
  228.7 2.9 %collective-permute-done.72.refs_6_ = f32[16,1024]{1,0:T(8,128)S(1)} collective-permute-done((f32[16,1024]{1,0:T(8,128)S(1)}, f32[16,1024]{1,0:T(8,128)S(1)}, u32[]{:S(2)}, u32[]{:S(2)}) %collective-permute-start.72) | collective-permute-done | bytes 65568 | tf_op jit(solution)/shard_map/ppermute | solution.py:413
  (171 shorter events, 108.7 us)
Async XLA Ops:
  27.1 10.9 %collective-permute-start.5 = (f32[16,1024]{1,0:T(8,128)S(1)}, f32[16,1024]{1,0:T(8,128)S(1)}, u32[]{:S(2)}, u32[]{:S(2)}) collective-permute-start(f32[16,1024]{1,0:T(8,128)S(1)} %get-tuple-element.70), channel_id=1, source_target_pairs={{0,8},{8,0},{16,24},{24,16},{1,9},{9,1},{17,25},{25,17},{2,10},{10... | collective-permute-start | bytes 196616 | tf_op jit(solution)/shard_map/ppermute | solution.py:413
  28.7 9.5 %collective-permute-start.6 = (f32[16,1024]{1,0:T(8,128)S(1)}, f32[16,1024]{1,0:T(8,128)S(1)}, u32[]{:S(2)}, u32[]{:S(2)}) collective-permute-start(f32[16,1024]{1,0:T(8,128)S(1)} %get-tuple-element.71), channel_id=1, source_target_pairs={{0,16},{8,24},{16,0},{24,8},{1,17},{9,25},{17,1},{25,9},{2,18},{10... | collective-permute-start | bytes 196616 | tf_op jit(solution)/shard_map/ppermute | solution.py:413
  33.7 8.7 %collective-permute-start.11 = (f32[16,1024]{1,0:T(8,128)S(1)}, f32[16,1024]{1,0:T(8,128)S(1)}, u32[]{:S(2)}, u32[]{:S(2)}) collective-permute-start(f32[16,1024]{1,0:T(8,128)S(1)} %get-tuple-element.75), channel_id=1, source_target_pairs={{0,8},{8,0},{16,24},{24,16},{1,9},{9,1},{17,25},{25,17},{2,10},{10... | collective-permute-start | bytes 196616 | tf_op jit(solution)/shard_map/ppermute | solution.py:413
  38.2 12.0 %collective-permute-start.8 = (f32[16,1024]{1,0:T(8,128)S(1)}, f32[16,1024]{1,0:T(8,128)S(1)}, u32[]{:S(2)}, u32[]{:S(2)}) collective-permute-start(f32[16,1024]{1,0:T(8,128)S(1)} %grad_sum.4.refs_1_), channel_id=1, source_target_pairs={{0,8},{8,0},{16,24},{24,16},{1,9},{9,1},{17,25},{25,17},{2,10},{10... | collective-permute-start | bytes 196616 | tf_op jit(solution)/shard_map/ppermute | solution.py:413
  38.6 12.9 %collective-permute-start.9 = (f32[16,1024]{1,0:T(8,128)S(1)}, f32[16,1024]{1,0:T(8,128)S(1)}, u32[]{:S(2)}, u32[]{:S(2)}) collective-permute-start(f32[16,1024]{1,0:T(8,128)S(1)} %grad_sum.4.refs_1_), channel_id=1, source_target_pairs={{0,16},{8,24},{16,0},{24,8},{1,17},{9,25},{17,1},{25,9},{2,18},{10... | collective-permute-start | bytes 196616 | tf_op jit(solution)/shard_map/ppermute | solution.py:413
  42.5 9.1 %collective-permute-start.10 = (f32[16,1024]{1,0:T(8,128)S(1)}, f32[16,1024]{1,0:T(8,128)S(1)}, u32[]{:S(2)}, u32[]{:S(2)}) collective-permute-start(f32[16,1024]{1,0:T(8,128)S(1)} %grad_sum.4.refs_1_), channel_id=1, source_target_pairs={{0,24},{8,16},{16,8},{24,0},{1,25},{9,17},{17,9},{25,1},{2,26},{10... | collective-permute-start | bytes 196616 | tf_op jit(solution)/shard_map/ppermute | solution.py:413
  44.1 15.5 %collective-permute-start.14 = (f32[16,1024]{1,0:T(8,128)S(1)}, f32[16,1024]{1,0:T(8,128)S(1)}, u32[]{:S(2)}, u32[]{:S(2)}) collective-permute-start(f32[16,1024]{1,0:T(8,128)S(1)} %grad_sum.5.refs_1_), channel_id=1, source_target_pairs={{0,8},{8,0},{16,24},{24,16},{1,9},{9,1},{17,25},{25,17},{2,10},{10... | collective-permute-start | bytes 196616 | tf_op jit(solution)/shard_map/ppermute | solution.py:413
  47.0 12.6 %collective-permute-start.15 = (f32[16,1024]{1,0:T(8,128)S(1)}, f32[16,1024]{1,0:T(8,128)S(1)}, u32[]{:S(2)}, u32[]{:S(2)}) collective-permute-start(f32[16,1024]{1,0:T(8,128)S(1)} %grad_sum.5.refs_1_), channel_id=1, source_target_pairs={{0,16},{8,24},{16,0},{24,8},{1,17},{9,25},{17,1},{25,9},{2,18},{10... | collective-permute-start | bytes 196616 | tf_op jit(solution)/shard_map/ppermute | solution.py:413
  50.2 9.4 %collective-permute-start.16 = (f32[16,1024]{1,0:T(8,128)S(1)}, f32[16,1024]{1,0:T(8,128)S(1)}, u32[]{:S(2)}, u32[]{:S(2)}) collective-permute-start(f32[16,1024]{1,0:T(8,128)S(1)} %grad_sum.5.refs_1_), channel_id=1, source_target_pairs={{0,24},{8,16},{16,8},{24,0},{1,25},{9,17},{17,9},{25,1},{2,26},{10... | collective-permute-start | bytes 196616 | tf_op jit(solution)/shard_map/ppermute | solution.py:413
  93.1 12.2 %collective-permute-start.25 = (f32[16,1152]{1,0:T(8,128)S(1)}, f32[16,1152]{1,0:T(8,128)S(1)}, u32[]{:S(2)}, u32[]{:S(2)}) collective-permute-start(f32[16,1152]{1,0:T(8,128)S(1)} %get-tuple-element.89), channel_id=1, source_target_pairs={{0,8},{8,0},{16,24},{24,16},{1,9},{9,1},{17,25},{25,17},{2,10},{10... | collective-permute-start | bytes 221192 | tf_op jit(solution)/shard_map/ppermute | solution.py:413
  93.7 13.0 %collective-permute-start.26 = (f32[16,1152]{1,0:T(8,128)S(1)}, f32[16,1152]{1,0:T(8,128)S(1)}, u32[]{:S(2)}, u32[]{:S(2)}) collective-permute-start(f32[16,1152]{1,0:T(8,128)S(1)} %get-tuple-element.90), channel_id=1, source_target_pairs={{0,16},{8,24},{16,0},{24,8},{1,17},{9,25},{17,1},{25,9},{2,18},{10... | collective-permute-start | bytes 221192 | tf_op jit(solution)/shard_map/ppermute | solution.py:413
  96.2 10.6 %collective-permute-start.27 = (f32[16,1152]{1,0:T(8,128)S(1)}, f32[16,1152]{1,0:T(8,128)S(1)}, u32[]{:S(2)}, u32[]{:S(2)}) collective-permute-start(f32[16,1152]{1,0:T(8,128)S(1)} %get-tuple-element.91), channel_id=1, source_target_pairs={{0,24},{8,16},{16,8},{24,0},{1,25},{9,17},{17,9},{25,1},{2,26},{10... | collective-permute-start | bytes 221192 | tf_op jit(solution)/shard_map/ppermute | solution.py:413
  102.3 8.9 %collective-permute-start.32 = (f32[16,1024]{1,0:T(8,128)S(1)}, f32[16,1024]{1,0:T(8,128)S(1)}, u32[]{:S(2)}, u32[]{:S(2)}) collective-permute-start(f32[16,1024]{1,0:T(8,128)S(1)} %get-tuple-element.97), channel_id=1, source_target_pairs={{0,16},{8,24},{16,0},{24,8},{1,17},{9,25},{17,1},{25,9},{2,18},{10... | collective-permute-start | bytes 196616 | tf_op jit(solution)/shard_map/ppermute | solution.py:413
  106.8 11.3 %collective-permute-start.28 = (f32[16,1024]{1,0:T(8,128)S(1)}, f32[16,1024]{1,0:T(8,128)S(1)}, u32[]{:S(2)}, u32[]{:S(2)}) collective-permute-start(f32[16,1024]{1,0:T(8,128)S(1)} %get-tuple-element.93.refs_1_.refs_4_), channel_id=1, source_target_pairs={{0,8},{8,0},{16,24},{24,16},{1,9},{9,1},{17,25},{25,17},{2,10},{10... | collective-permute-start | bytes 196616 | tf_op jit(solution)/shard_map/ppermute | solution.py:413
  106.9 12.6 %collective-permute-start.29 = (f32[16,1024]{1,0:T(8,128)S(1)}, f32[16,1024]{1,0:T(8,128)S(1)}, u32[]{:S(2)}, u32[]{:S(2)}) collective-permute-start(f32[16,1024]{1,0:T(8,128)S(1)} %get-tuple-element.93.refs_1_.refs_4_), channel_id=1, source_target_pairs={{0,16},{8,24},{16,0},{24,8},{1,17},{9,25},{17,1},{25,9},{2,18},{10... | collective-permute-start | bytes 196616 | tf_op jit(solution)/shard_map/ppermute | solution.py:413
  109.9 9.6 %collective-permute-start.30 = (f32[16,1024]{1,0:T(8,128)S(1)}, f32[16,1024]{1,0:T(8,128)S(1)}, u32[]{:S(2)}, u32[]{:S(2)}) collective-permute-start(f32[16,1024]{1,0:T(8,128)S(1)} %get-tuple-element.93.refs_1_.refs_4_), channel_id=1, source_target_pairs={{0,24},{8,16},{16,8},{24,0},{1,25},{9,17},{17,9},{25,1},{2,26},{10... | collective-permute-start | bytes 196616 | tf_op jit(solution)/shard_map/ppermute | solution.py:413
  143.0 10.3 %collective-permute-start.49 = (f32[16,1024]{1,0:T(8,128)S(1)}, f32[16,1024]{1,0:T(8,128)S(1)}, u32[]{:S(2)}, u32[]{:S(2)}) collective-permute-start(f32[16,1024]{1,0:T(8,128)S(1)} %get-tuple-element.109), channel_id=1, source_target_pairs={{0,16},{8,24},{16,0},{24,8},{1,17},{9,25},{17,1},{25,9},{2,18},{10... | collective-permute-start | bytes 196616 | tf_op jit(solution)/shard_map/ppermute | solution.py:413
  144.2 9.1 %collective-permute-start.50 = (f32[16,1024]{1,0:T(8,128)S(1)}, f32[16,1024]{1,0:T(8,128)S(1)}, u32[]{:S(2)}, u32[]{:S(2)}) collective-permute-start(f32[16,1024]{1,0:T(8,128)S(1)} %get-tuple-element.110), channel_id=1, source_target_pairs={{0,24},{8,16},{16,8},{24,0},{1,25},{9,17},{17,9},{25,1},{2,26},{10... | collective-permute-start | bytes 196616 | tf_op jit(solution)/shard_map/ppermute | solution.py:413
  148.9 9.1 %collective-permute-start.43 = (f32[16,1024]{1,0:T(8,128)S(1)}, f32[16,1024]{1,0:T(8,128)S(1)}, u32[]{:S(2)}, u32[]{:S(2)}) collective-permute-start(f32[16,1024]{1,0:T(8,128)S(1)} %get-tuple-element.105), channel_id=1, source_target_pairs={{0,16},{8,24},{16,0},{24,8},{1,17},{9,25},{17,1},{25,9},{2,18},{10... | collective-permute-start | bytes 196616 | tf_op jit(solution)/shard_map/ppermute | solution.py:413
  153.3 10.2 %collective-permute-start.51 = (f32[16,1024]{1,0:T(8,128)S(1)}, f32[16,1024]{1,0:T(8,128)S(1)}, u32[]{:S(2)}, u32[]{:S(2)}) collective-permute-start(f32[16,1024]{1,0:T(8,128)S(1)} %grad_sum.7.refs_1_), channel_id=1, source_target_pairs={{0,8},{8,0},{16,24},{24,16},{1,9},{9,1},{17,25},{25,17},{2,10},{10... | collective-permute-start | bytes 196616 | tf_op jit(solution)/shard_map/ppermute | solution.py:413
  153.4 12.6 %collective-permute-start.52 = (f32[16,1024]{1,0:T(8,128)S(1)}, f32[16,1024]{1,0:T(8,128)S(1)}, u32[]{:S(2)}, u32[]{:S(2)}) collective-permute-start(f32[16,1024]{1,0:T(8,128)S(1)} %grad_sum.7.refs_1_), channel_id=1, source_target_pairs={{0,16},{8,24},{16,0},{24,8},{1,17},{9,25},{17,1},{25,9},{2,18},{10... | collective-permute-start | bytes 196616 | tf_op jit(solution)/shard_map/ppermute | solution.py:413
  155.3 10.6 %collective-permute-start.53 = (f32[16,1024]{1,0:T(8,128)S(1)}, f32[16,1024]{1,0:T(8,128)S(1)}, u32[]{:S(2)}, u32[]{:S(2)}) collective-permute-start(f32[16,1024]{1,0:T(8,128)S(1)} %grad_sum.7.refs_1_), channel_id=1, source_target_pairs={{0,24},{8,16},{16,8},{24,0},{1,25},{9,17},{17,9},{25,1},{2,26},{10... | collective-permute-start | bytes 196616 | tf_op jit(solution)/shard_map/ppermute | solution.py:413
  158.0 14.4 %collective-permute-start.45 = (f32[16,1024]{1,0:T(8,128)S(1)}, f32[16,1024]{1,0:T(8,128)S(1)}, u32[]{:S(2)}, u32[]{:S(2)}) collective-permute-start(f32[16,1024]{1,0:T(8,128)S(1)} %grad_sum.6.refs_1_), channel_id=1, source_target_pairs={{0,8},{8,0},{16,24},{24,16},{1,9},{9,1},{17,25},{25,17},{2,10},{10... | collective-permute-start | bytes 196616 | tf_op jit(solution)/shard_map/ppermute | solution.py:413
  163.5 8.8 %collective-permute-start.46 = (f32[16,1024]{1,0:T(8,128)S(1)}, f32[16,1024]{1,0:T(8,128)S(1)}, u32[]{:S(2)}, u32[]{:S(2)}) collective-permute-start(f32[16,1024]{1,0:T(8,128)S(1)} %grad_sum.6.refs_1_), channel_id=1, source_target_pairs={{0,16},{8,24},{16,0},{24,8},{1,17},{9,25},{17,1},{25,9},{2,18},{10... | collective-permute-start | bytes 196616 | tf_op jit(solution)/shard_map/ppermute | solution.py:413
  163.5 8.8 %collective-permute-start.47 = (f32[16,1024]{1,0:T(8,128)S(1)}, f32[16,1024]{1,0:T(8,128)S(1)}, u32[]{:S(2)}, u32[]{:S(2)}) collective-permute-start(f32[16,1024]{1,0:T(8,128)S(1)} %grad_sum.6.refs_1_), channel_id=1, source_target_pairs={{0,24},{8,16},{16,8},{24,0},{1,25},{9,17},{17,9},{25,1},{2,26},{10... | collective-permute-start | bytes 196616 | tf_op jit(solution)/shard_map/ppermute | solution.py:413
  202.5 11.0 %collective-permute-start.62 = (f32[16,1152]{1,0:T(8,128)S(1)}, f32[16,1152]{1,0:T(8,128)S(1)}, u32[]{:S(2)}, u32[]{:S(2)}) collective-permute-start(f32[16,1152]{1,0:T(8,128)S(1)} %get-tuple-element.118), channel_id=1, source_target_pairs={{0,8},{8,0},{16,24},{24,16},{1,9},{9,1},{17,25},{25,17},{2,10},{10... | collective-permute-start | bytes 221192 | tf_op jit(solution)/shard_map/ppermute | solution.py:413
  203.6 12.3 %collective-permute-start.63 = (f32[16,1152]{1,0:T(8,128)S(1)}, f32[16,1152]{1,0:T(8,128)S(1)}, u32[]{:S(2)}, u32[]{:S(2)}) collective-permute-start(f32[16,1152]{1,0:T(8,128)S(1)} %get-tuple-element.119), channel_id=1, source_target_pairs={{0,16},{8,24},{16,0},{24,8},{1,17},{9,25},{17,1},{25,9},{2,18},{10... | collective-permute-start | bytes 221192 | tf_op jit(solution)/shard_map/ppermute | solution.py:413
  204.5 11.4 %collective-permute-start.64 = (f32[16,1152]{1,0:T(8,128)S(1)}, f32[16,1152]{1,0:T(8,128)S(1)}, u32[]{:S(2)}, u32[]{:S(2)}) collective-permute-start(f32[16,1152]{1,0:T(8,128)S(1)} %get-tuple-element.120), channel_id=1, source_target_pairs={{0,24},{8,16},{16,8},{24,0},{1,25},{9,17},{17,9},{25,1},{2,26},{10... | collective-permute-start | bytes 221192 | tf_op jit(solution)/shard_map/ppermute | solution.py:413
  211.7 8.8 %collective-permute-start.69 = (f32[16,1024]{1,0:T(8,128)S(1)}, f32[16,1024]{1,0:T(8,128)S(1)}, u32[]{:S(2)}, u32[]{:S(2)}) collective-permute-start(f32[16,1024]{1,0:T(8,128)S(1)} %get-tuple-element.124), channel_id=1, source_target_pairs={{0,16},{8,24},{16,0},{24,8},{1,17},{9,25},{17,1},{25,9},{2,18},{10... | collective-permute-start | bytes 196616 | tf_op jit(solution)/shard_map/ppermute | solution.py:413
  216.0 10.2 %collective-permute-start.65 = (f32[16,1024]{1,0:T(8,128)S(1)}, f32[16,1024]{1,0:T(8,128)S(1)}, u32[]{:S(2)}, u32[]{:S(2)}) collective-permute-start(f32[16,1024]{1,0:T(8,128)S(1)} %get-tuple-element.121.refs_0_), channel_id=1, source_target_pairs={{0,8},{8,0},{16,24},{24,16},{1,9},{9,1},{17,25},{25,17},{2,10},{10... | collective-permute-start | bytes 196616 | tf_op jit(solution)/shard_map/ppermute | solution.py:413
  216.1 12.6 %collective-permute-start.66 = (f32[16,1024]{1,0:T(8,128)S(1)}, f32[16,1024]{1,0:T(8,128)S(1)}, u32[]{:S(2)}, u32[]{:S(2)}) collective-permute-start(f32[16,1024]{1,0:T(8,128)S(1)} %get-tuple-element.121.refs_0_), channel_id=1, source_target_pairs={{0,16},{8,24},{16,0},{24,8},{1,17},{9,25},{17,1},{25,9},{2,18},{10... | collective-permute-start | bytes 196616 | tf_op jit(solution)/shard_map/ppermute | solution.py:413
  218.0 10.7 %collective-permute-start.67 = (f32[16,1024]{1,0:T(8,128)S(1)}, f32[16,1024]{1,0:T(8,128)S(1)}, u32[]{:S(2)}, u32[]{:S(2)}) collective-permute-start(f32[16,1024]{1,0:T(8,128)S(1)} %get-tuple-element.121.refs_0_), channel_id=1, source_target_pairs={{0,24},{8,16},{16,8},{24,0},{1,25},{9,17},{17,9},{25,1},{2,26},{10... | collective-permute-start | bytes 196616 | tf_op jit(solution)/shard_map/ppermute | solution.py:413
  (50 other events, 374.6 us)

commit v4 on v3

--- a/solution.py
+++ b/solution.py
@@ -107,10 +107,10 @@
 
 
 def stream_near(sources, size, use):
-    for ref, first, count, at in sources:
-
-        def one(i, carry, ref=ref, first=first, at=at):
-            use(pl.ds(pl.multiple_of(at + i * size, size), size), ref[first + i])
+    for ref, first, count, at, lanes in sources:
+
+        def one(i, carry, ref=ref, first=first, at=at, lanes=lanes):
+            use(pl.ds(pl.multiple_of(at + i * size, size), size), ref[first + i, :, lanes])
             return carry
 
         lax.fori_loop(0, count, one, 0)
@@ -220,7 +220,7 @@
 
         stage(ins[:n_pieces], places, full, parts)
         if near:
-            stream_near([(w_ref[0], 0, count // size, 0)], size, use)
+            stream_near([(w_ref[0], 0, count // size, 0, slice(None))], size, use)
         else:
             stream(w_ref[0], held, sems, first, count, size, lanes, use)
         if halves:
@@ -263,7 +263,7 @@
         cross = dot(jnp.concatenate([high, mid, high, mid, high, low], axis=1), wide[...], NT)
         norm = jnp.sum(x * x, axis=1, keepdims=True) * gain
         tile = jnp.exp2((cross - norm) - norms[0:1, :])
-        tile_ref[...] = tile
+        tile_ref[0] = tile
         high, low = split(tile)
         both = dot(parts[...], high, NT)
         total[...] = both[:out] + both[out:] + dot(parts[0:out], low, NT)
@@ -280,12 +280,12 @@
             pl.BlockSpec((out, count), lambda i: (0, 0)),
         ],
         out_specs=[
-            pl.BlockSpec((size, count), lambda i: (i, 0)),
+            pl.BlockSpec((1, size, count), lambda i: (i, 0, 0)),
             pl.BlockSpec((half, size), lambda i: (0, i)),
             pl.BlockSpec((half, size), lambda i: (0, i)),
         ],
         out_shape=[
-            jax.ShapeDtypeStruct((rows, count), f32),
+            jax.ShapeDtypeStruct((rows // size, size, count), f32),
             jax.ShapeDtypeStruct((half, rows), f32),
             jax.ShapeDtypeStruct((half, rows), f32),
         ],
@@ -471,7 +471,7 @@
             tile, theirs, mine = tile_and_logits(features, centers, a)
         else:
             theirs, mine = across(
-                tile, a_pieces, rank_places_both, out, 0, rows_here, slice(0, count), "logits", halves=True, limit=NEAR_LIMIT
+                tile, a_pieces, rank_places_both, out, 0, rows_here, slice(0, count), "logits", halves=True, near=True
             )
         logits = add_up([mine, swap(theirs, "centers", 1)], "chip_logits")
         logits = [logits] + [swap(logits, "centers", 2 * k) for k in range(1, chips)]
@@ -479,7 +479,18 @@
         resids = [resid, swap(resid, "centers", 1)]
         grads = []
         for lanes, name in ((left, "grada"), (right, "gradb")):
-            cuts = down(tile, resids, core_places, out, 0, rows_here, lanes, name, chunks=depth_ranks, limit=NEAR_LIMIT)
+            cuts = down(
+                [tile],
+                resids,
+                core_places,
+                out,
+                0,
+                rows_here,
+                lanes,
+                name,
+                chunks=depth_ranks,
+                near=lambda size, lanes=lanes: [(0, rows_here // size, 0, lanes)],
+            )
             grads.append(all_rows(add_up(to_rank(cuts), "grad_sum")))
         places = rank_places
         if step == 0:
@@ -512,7 +523,7 @@
             left,
             "backa",
             squares="sum",
-            near=lambda size: [(my_rows() // size, row_half // size, 0)],
+            near=lambda size: [(my_rows() // size, row_half // size, 0, every)],
         )
         cuts = down(
             [near_left],
@@ -526,7 +537,7 @@
             chunks=depth_ranks,
             before=begun,
             squares=squares,
-            near=lambda size: [(other_rows() // size, row_half // size, 0)],
+            near=lambda size: [(other_rows() // size, row_half // size, 0, every)],
         )
         first, scale = update(to_rank(cuts), a_halves[0], center_total * out)
         cuts = down(
@@ -539,7 +550,10 @@
             right,
             "backc",
             chunks=depth_ranks,
-            near=lambda size: [(0, row_half // size, my_rows()), (0, row_half // size, other_rows())],
+            near=lambda size: [
+                (0, row_half // size, my_rows(), every),
+                (0, row_half // size, other_rows(), every),
+            ],
         )
         (second,) = update(to_rank(cuts), a_halves[1], center_total * out, scale)
         a_halves = [first, second]

time: 233 us -> 229 us (0.983)
  Pallas kernels: 71.3 us -> 66.6 us
    pallas_call x17, Pallas kernels: 62.1 us -> 57.4 us  [call(): pl.pallas_call(whole, in_specs=[WHOLE if near else FAR] * n_weights + [WH...]
  transfers between devices with their start and end apart: 74 -> 74, of which waited for: 24 -> 26; matrix products, arithmetic and copies ran while one was open for 0% -> 0% of each run, Pallas kernels for 18% -> 17%
where the time goes in v4:
time: 229 us
  starting transfers between devices  107 us (47%)
  Pallas kernels  66.6 us (29%)
  waiting for transfers between devices  51.4 us (22%)
  local copies, waits for them, and re-layouts  3.37 us (1%)
    ppermute x74, starting transfers between devices, swap(): return lax.ppermute(x, axis, [(i, i ^ mask) for i in range(size)])  107 us
    pallas_call x17, Pallas kernels, call(): pl.pallas_call(whole, in_specs=[WHOLE if near else FAR] * n_weights + [WH...  57.4 us
    ppermute x74, waiting for transfers between devices, swap(): return lax.ppermute(x, axis, [(i, i ^ mask) for i in range(size)])  51.4 us
    pallas_call x1, Pallas kernels, tile_and_logits(): pl.pallas_call(kernel, grid=(rows // size,), in_specs=[pl.BlockSpec((size...  7.57 us
  transfers between devices with their start and end apart: 74, of which 26 were waited for; matrix products, arithmetic and copies ran while one was open for 0% of the time, Pallas kernels for 17%

profile of v4, /device:TPU:0, one launch (start us, length us, event | category | flops | bytes accessed | tf_op | source)
XLA Modules:
  0.0 229.1 jit_solution(12157603413230866205)
XLA Ops:
  3.4 7.6 %tile_and_logits.1 = (f32[2,512,2048]{2,1,0:T(8,128)S(1)}, f32[32,1024]{1,0:T(8,128)S(1)}, f32[32,1024]{1,0:T(8,128)S(1)}) custom-call(f32[1024,128]{1,0:T(8,128)S(1)} %copy-done.5, f32[2048,128]{1,0:T(8,128)S(1)} %copy-done.4, f32[64,2048]{1,0:T(8,128)S(1)} %bitcast.7), custom_call_target="tpu_custom_call" | custom-call | flops 3221225472 | bytes 8388608 | tf_op jit(solution)/shard_map/tile_and_logits/pallas_call | solution.py:274
  12.5 2.9 %collective-permute-start.1 = (f32[32,1024]{1,0:T(8,128)S(1)}, f32[32,1024]{1,0:T(8,128)S(1)}, u32[]{:S(2)}, u32[]{:S(2)}) collective-permute-start(f32[32,1024]{1,0:T(8,128)S(1)} %chip_logits.2.refs_0_), channel_id=1, source_target_pairs={{0,2},{1,3},{2,0},{3,1},{4,6},{5,7},{6,4},{7,5},{8,10},{9,11},{10,... | collective-permute-start | bytes 393224 | tf_op jit(solution)/shard_map/ppermute | solution.py:413
  19.3 4.2 %collective-permute-done.2.refs_2_ = f32[32,1024]{1,0:T(8,128)S(1)} collective-permute-done((f32[32,1024]{1,0:T(8,128)S(1)}, f32[32,1024]{1,0:T(8,128)S(1)}, u32[]{:S(2)}, u32[]{:S(2)}) %collective-permute-start.2) | collective-permute-done | bytes 131104 | tf_op jit(solution)/shard_map/ppermute | solution.py:413
  32.4 3.5 %collective-permute-start.12 = (f32[16,1024]{1,0:T(8,128)S(1)}, f32[16,1024]{1,0:T(8,128)S(1)}, u32[]{:S(2)}, u32[]{:S(2)}) collective-permute-start(f32[16,1024]{1,0:T(8,128)S(1)} %get-tuple-element.76), channel_id=1, source_target_pairs={{0,16},{8,24},{16,0},{24,8},{1,17},{9,25},{17,1},{25,9},{2,18},{10... | collective-permute-start | bytes 196616 | tf_op jit(solution)/shard_map/ppermute | solution.py:413
  42.2 2.8 %collective-permute-start.14 = (f32[16,1024]{1,0:T(8,128)S(1)}, f32[16,1024]{1,0:T(8,128)S(1)}, u32[]{:S(2)}, u32[]{:S(2)}) collective-permute-start(f32[16,1024]{1,0:T(8,128)S(1)} %grad_sum.5.refs_1_), channel_id=1, source_target_pairs={{0,8},{8,0},{16,24},{24,16},{1,9},{9,1},{17,25},{25,17},{2,10},{10... | collective-permute-start | bytes 196616 | tf_op jit(solution)/shard_map/ppermute | solution.py:413
  45.0 2.6 %collective-permute-start.15 = (f32[16,1024]{1,0:T(8,128)S(1)}, f32[16,1024]{1,0:T(8,128)S(1)}, u32[]{:S(2)}, u32[]{:S(2)}) collective-permute-start(f32[16,1024]{1,0:T(8,128)S(1)} %grad_sum.5.refs_1_), channel_id=1, source_target_pairs={{0,16},{8,24},{16,0},{24,8},{1,17},{9,25},{17,1},{25,9},{2,18},{10... | collective-permute-start | bytes 196616 | tf_op jit(solution)/shard_map/ppermute | solution.py:413
  49.1 8.0 %fwda.2 = (f32[64,4096]{1,0:T(8,128)S(1)}, f32[8,512,1024]{2,1,0:T(8,128)S(1)}) custom-call(f32[4096,2048]{1,0:T(8,128)} %refs_0_.5, f32[16,1024]{1,0:T(8,128)S(1)} %grad_sum.4.refs_1_, f32[16,1024]{1,0:T(8,128)S(1)} %collective-permute-done.8.refs_2_, f32[16,1024]{1,0:T(8,128)S(1)} %collective-permute-done.9.refs_3_, ...), custom_call_target="tpu_custom_call" | custom-call | flops 1610612736 | bytes 16777216 | tf_op jit(solution)/shard_map/fwda/pallas_call | solution.py:144
  57.1 4.8 %fwdb.2 = (f32[64,2048]{1,0:T(8,128)S(1)}, f32[4,512,1024]{2,1,0:T(8,128)S(1)}) custom-call(f32[4096,2048]{1,0:T(8,128)} %refs_0_.5, f32[16,1024]{1,0:T(8,128)S(1)} %grad_sum.5.refs_1_, f32[16,1024]{1,0:T(8,128)S(1)} %collective-permute-done.14.refs_2_, f32[16,1024]{1,0:T(8,128)S(1)} %collective-permute-done.15.refs_3_, ...), custom_call_target="tpu_custom_call" | custom-call | flops 805306368 | bytes 8388608 | tf_op jit(solution)/shard_map/fwdb/pallas_call | solution.py:144
  62.1 4.9 %fwdc.2 = (f32[64,2048]{1,0:T(8,128)S(1)}, f32[4,512,1024]{2,1,0:T(8,128)S(1)}) custom-call(f32[4096,2048]{1,0:T(8,128)} %refs_0_.5, f32[16,1024]{1,0:T(8,128)S(1)} %grad_sum.5.refs_1_, f32[16,1024]{1,0:T(8,128)S(1)} %collective-permute-done.14.refs_2_, f32[16,1024]{1,0:T(8,128)S(1)} %collective-permute-done.15.refs_3_, ...), custom_call_target="tpu_custom_call" | custom-call | flops 805306368 | bytes 8388608 | tf_op jit(solution)/shard_map/fwdc/pallas_call | solution.py:144
  70.6 2.8 %collective-permute-done.18.refs_1_ = f32[16,2048]{1,0:T(8,128)S(1)} collective-permute-done((f32[16,2048]{1,0:T(8,128)S(1)}, f32[16,2048]{1,0:T(8,128)S(1)}, u32[]{:S(2)}, u32[]{:S(2)}) %collective-permute-start.18) | collective-permute-done | bytes 131104 | tf_op jit(solution)/shard_map/ppermute | solution.py:413
  80.3 2.9 %collective-permute-done.21.refs_1_.refs_2_.refs_3_ = f32[16,2048]{1,0:T(8,128)S(1)} collective-permute-done((f32[16,2048]{1,0:T(8,128)S(1)}, f32[16,2048]{1,0:T(8,128)S(1)}, u32[]{:S(2)}, u32[]{:S(2)}) %collective-permute-start.21) | collective-permute-done | bytes 131104 | tf_op jit(solution)/shard_map/ppermute | solution.py:413
  95.0 4.7 %backc.2 = (f32[16,1024]{1,0:T(8,128)S(1)}, f32[16,1024]{1,0:T(8,128)S(1)}, f32[16,1024]{1,0:T(8,128)S(1)}, f32[16,1024]{1,0:T(8,128)S(1)}) custom-call(f32[4,512,1024]{2,1,0:T(8,128)S(1)} %get-tuple-element.79.refs_0_, f32[4,512,1024]{2,1,0:T(8,128)S(1)} %get-tuple-element.94.refs_1_.refs_0_, f32[16,2048]{1,0:T(8,128)S(1)} %fwd_sum.2.refs_0_.refs_1_.refs_2_, ...), custom_call_target="tpu_custom_call" | custom-call | flops 1610612736 | bytes 16777216 | tf_op jit(solution)/shard_map/backc/pallas_call | solution.py:144
  100.2 2.6 %collective-permute-start.32 = (f32[16,1024]{1,0:T(8,128)S(1)}, f32[16,1024]{1,0:T(8,128)S(1)}, u32[]{:S(2)}, u32[]{:S(2)}) collective-permute-start(f32[16,1024]{1,0:T(8,128)S(1)} %get-tuple-element.97), channel_id=1, source_target_pairs={{0,16},{8,24},{16,0},{24,8},{1,17},{9,25},{17,1},{25,9},{2,18},{10... | collective-permute-start | bytes 196616 | tf_op jit(solution)/shard_map/ppermute | solution.py:413
  104.4 3.0 %collective-permute-start.29 = (f32[16,1024]{1,0:T(8,128)S(1)}, f32[16,1024]{1,0:T(8,128)S(1)}, u32[]{:S(2)}, u32[]{:S(2)}) collective-permute-start(f32[16,1024]{1,0:T(8,128)S(1)} %get-tuple-element.93.refs_1_.refs_4_), channel_id=1, source_target_pairs={{0,16},{8,24},{16,0},{24,8},{1,17},{9,25},{17,1},{25,9},{2,18},{10... | collective-permute-start | bytes 196616 | tf_op jit(solution)/shard_map/ppermute | solution.py:413
  109.5 3.7 %collective-permute-start.34 = (f32[16,1024]{1,0:T(8,128)S(1)}, f32[16,1024]{1,0:T(8,128)S(1)}, u32[]{:S(2)}, u32[]{:S(2)}) collective-permute-start(f32[16,1024]{1,0:T(8,128)S(1)} %update.5.refs_5_.refs_4_), channel_id=1, source_target_pairs={{0,8},{8,0},{16,24},{24,16},{1,9},{9,1},{17,25},{25,17},{2,10},{10... | collective-permute-start | bytes 196616 | tf_op jit(solution)/shard_map/ppermute | solution.py:413
  113.2 2.8 %collective-permute-start.35 = (f32[16,1024]{1,0:T(8,128)S(1)}, f32[16,1024]{1,0:T(8,128)S(1)}, u32[]{:S(2)}, u32[]{:S(2)}) collective-permute-start(f32[16,1024]{1,0:T(8,128)S(1)} %update.5.refs_5_.refs_4_), channel_id=1, source_target_pairs={{0,16},{8,24},{16,0},{24,8},{1,17},{9,25},{17,1},{25,9},{2,18},{10... | collective-permute-start | bytes 196616 | tf_op jit(solution)/shard_map/ppermute | solution.py:413
  118.4 3.9 %collective-permute-done.36.refs_8_ = f32[16,1024]{1,0:T(8,128)S(1)} collective-permute-done((f32[16,1024]{1,0:T(8,128)S(1)}, f32[16,1024]{1,0:T(8,128)S(1)}, u32[]{:S(2)}, u32[]{:S(2)}) %collective-permute-start.36) | collective-permute-done | bytes 65568 | tf_op jit(solution)/shard_map/ppermute | solution.py:413
  122.3 3.1 %logits.1 = (f32[32,1024]{1,0:T(8,128)S(1)}, f32[32,1024]{1,0:T(8,128)S(1)}) custom-call(f32[2,512,2048]{2,1,0:T(8,128)S(1)} %get-tuple-element.66.refs_0_, f32[16,1024]{1,0:T(8,128)S(1)} %get-tuple-element.93.refs_1_.refs_4_, f32[16,1024]{1,0:T(8,128)S(1)} %collective-permute-done.28.refs_2_, f32[16,1024]{1,0:T(8,128)S(1)} %collective-permute-done.29.refs_3_, ...), custom_call_target="tpu_custom_call" | custom-call | flops 805306368 | bytes 8388608 | tf_op jit(solution)/shard_map/logits/pallas_call | solution.py:144
  130.3 2.9 %collective-permute-done.38.refs_1_ = f32[32,1024]{1,0:T(8,128)S(1)} collective-permute-done((f32[32,1024]{1,0:T(8,128)S(1)}, f32[32,1024]{1,0:T(8,128)S(1)}, u32[]{:S(2)}, u32[]{:S(2)}) %collective-permute-start.38) | collective-permute-done | bytes 131104 | tf_op jit(solution)/shard_map/ppermute | solution.py:413
  133.2 2.8 %collective-permute-done.39.refs_2_ = f32[32,1024]{1,0:T(8,128)S(1)} collective-permute-done((f32[32,1024]{1,0:T(8,128)S(1)}, f32[32,1024]{1,0:T(8,128)S(1)}, u32[]{:S(2)}, u32[]{:S(2)}) %collective-permute-start.39) | collective-permute-done | bytes 131104 | tf_op jit(solution)/shard_map/ppermute | solution.py:413
  148.7 3.3 %collective-permute-start.51 = (f32[16,1024]{1,0:T(8,128)S(1)}, f32[16,1024]{1,0:T(8,128)S(1)}, u32[]{:S(2)}, u32[]{:S(2)}) collective-permute-start(f32[16,1024]{1,0:T(8,128)S(1)} %grad_sum.7.refs_1_), channel_id=1, source_target_pairs={{0,8},{8,0},{16,24},{24,16},{1,9},{9,1},{17,25},{25,17},{2,10},{10... | collective-permute-start | bytes 196616 | tf_op jit(solution)/shard_map/ppermute | solution.py:413
  154.9 2.7 %collective-permute-start.45 = (f32[16,1024]{1,0:T(8,128)S(1)}, f32[16,1024]{1,0:T(8,128)S(1)}, u32[]{:S(2)}, u32[]{:S(2)}) collective-permute-start(f32[16,1024]{1,0:T(8,128)S(1)} %grad_sum.6.refs_1_), channel_id=1, source_target_pairs={{0,8},{8,0},{16,24},{24,16},{1,9},{9,1},{17,25},{25,17},{2,10},{10... | collective-permute-start | bytes 196616 | tf_op jit(solution)/shard_map/ppermute | solution.py:413
  160.2 6.4 %fwda.3.refs_5_ = f32[64,4096]{1,0:T(8,128)S(1)} custom-call(f32[8,512,1024]{2,1,0:T(8,128)S(1)} %get-tuple-element.73.refs_0_, f32[16,1024]{1,0:T(8,128)S(1)} %grad_sum.7.refs_1_, f32[16,1024]{1,0:T(8,128)S(1)} %collective-permute-done.51.refs_2_, f32[16,1024]{1,0:T(8,128)S(1)} %collective-permute-done.52.refs_3_, ...), custom_call_target="tpu_custom_call" | custom-call | flops 1610612736 | bytes 16777216 | tf_op jit(solution)/shard_map/fwda/pallas_call | solution.py:144
  166.7 3.2 %fwdb.3 = f32[64,2048]{1,0:T(8,128)S(1)} custom-call(f32[4,512,1024]{2,1,0:T(8,128)S(1)} %get-tuple-element.94.refs_1_.refs_0_, f32[16,1024]{1,0:T(8,128)S(1)} %grad_sum.6.refs_1_, f32[16,1024]{1,0:T(8,128)S(1)} %collective-permute-done.45.refs_2_, f32[16,1024]{1,0:T(8,128)S(1)} %collective-permute-done.46.refs_3_, ...), custom_call_target="tpu_custom_call" | custom-call | flops 805306368 | bytes 8388608 | tf_op jit(solution)/shard_map/fwdb/pallas_call | solution.py:144
  170.0 3.2 %fwdc.3.a_ref = f32[64,2048]{1,0:T(8,128)S(1)} custom-call(f32[4,512,1024]{2,1,0:T(8,128)S(1)} %bitcast.4, f32[16,1024]{1,0:T(8,128)S(1)} %grad_sum.6.refs_1_, f32[16,1024]{1,0:T(8,128)S(1)} %collective-permute-done.45.refs_2_, f32[16,1024]{1,0:T(8,128)S(1)} %collective-permute-done.46.refs_3_, f32[16,1024]{1,0:T(8,128)S(1)} %collective-permute-done.47.refs_4_, ...), custom_call_target="tpu_custom_call" | custom-call | flops 805306368 | bytes 8388608 | tf_op jit(solution)/shard_map/fwdc/pallas_call | solution.py:144
  176.9 2.8 %collective-permute-done.55.refs_1_ = f32[16,2048]{1,0:T(8,128)S(1)} collective-permute-done((f32[16,2048]{1,0:T(8,128)S(1)}, f32[16,2048]{1,0:T(8,128)S(1)}, u32[]{:S(2)}, u32[]{:S(2)}) %collective-permute-start.55) | collective-permute-done | bytes 131104 | tf_op jit(solution)/shard_map/ppermute | solution.py:413
  179.7 3.1 %collective-permute-done.56.refs_2_ = f32[16,2048]{1,0:T(8,128)S(1)} collective-permute-done((f32[16,2048]{1,0:T(8,128)S(1)}, f32[16,2048]{1,0:T(8,128)S(1)}, u32[]{:S(2)}, u32[]{:S(2)}) %collective-permute-start.56) | collective-permute-done | bytes 131104 | tf_op jit(solution)/shard_map/ppermute | solution.py:413
  188.7 2.9 %collective-permute-done.59.refs_2_.refs_3_.refs_4_ = f32[16,2048]{1,0:T(8,128)S(1)} collective-permute-done((f32[16,2048]{1,0:T(8,128)S(1)}, f32[16,2048]{1,0:T(8,128)S(1)}, u32[]{:S(2)}, u32[]{:S(2)}) %collective-permute-start.59) | collective-permute-done | bytes 131104 | tf_op jit(solution)/shard_map/ppermute | solution.py:413
  196.8 2.9 %collective-permute-start.62 = (f32[16,1152]{1,0:T(8,128)S(1)}, f32[16,1152]{1,0:T(8,128)S(1)}, u32[]{:S(2)}, u32[]{:S(2)}) collective-permute-start(f32[16,1152]{1,0:T(8,128)S(1)} %get-tuple-element.118), channel_id=1, source_target_pairs={{0,8},{8,0},{16,24},{24,16},{1,9},{9,1},{17,25},{25,17},{2,10},{10... | collective-permute-start | bytes 221192 | tf_op jit(solution)/shard_map/ppermute | solution.py:413
  202.1 4.5 %backc.3 = (f32[16,1024]{1,0:T(8,128)S(1)}, f32[16,1024]{1,0:T(8,128)S(1)}, f32[16,1024]{1,0:T(8,128)S(1)}, f32[16,1024]{1,0:T(8,128)S(1)}) custom-call(f32[4,512,1024]{2,1,0:T(8,128)S(1)} %bitcast.4, f32[4,512,1024]{2,1,0:T(8,128)S(1)} %get-tuple-element.94.refs_1_.refs_0_, f32[16,2048]{1,0:T(8,128)S(1)} %fwd_sum.3.refs_0_.refs_1_.refs_2_, ...), custom_call_target="tpu_custom_call" | custom-call | flops 1610612736 | bytes 16777216 | tf_op jit(solution)/shard_map/backc/pallas_call | solution.py:144
  216.6 5.5 %collective-permute-start.71 = (f32[16,1024]{1,0:T(8,128)S(1)}, f32[16,1024]{1,0:T(8,128)S(1)}, u32[]{:S(2)}, u32[]{:S(2)}) collective-permute-start(f32[16,1024]{1,0:T(8,128)S(1)} %update.7.refs_4_), channel_id=1, source_target_pairs={{0,8},{8,0},{16,24},{24,16},{1,9},{9,1},{17,25},{25,17},{2,10},{10... | collective-permute-start | bytes 196616 | tf_op jit(solution)/shard_map/ppermute | solution.py:413
  224.6 2.9 %collective-permute-done.72.refs_6_ = f32[16,1024]{1,0:T(8,128)S(1)} collective-permute-done((f32[16,1024]{1,0:T(8,128)S(1)}, f32[16,1024]{1,0:T(8,128)S(1)}, u32[]{:S(2)}, u32[]{:S(2)}) %collective-permute-start.72) | collective-permute-done | bytes 65568 | tf_op jit(solution)/shard_map/ppermute | solution.py:413
  (171 shorter events, 108.7 us)
Async XLA Ops:
  26.1 9.8 %collective-permute-start.5 = (f32[16,1024]{1,0:T(8,128)S(1)}, f32[16,1024]{1,0:T(8,128)S(1)}, u32[]{:S(2)}, u32[]{:S(2)}) collective-permute-start(f32[16,1024]{1,0:T(8,128)S(1)} %get-tuple-element.70), channel_id=1, source_target_pairs={{0,8},{8,0},{16,24},{24,16},{1,9},{9,1},{17,25},{25,17},{2,10},{10... | collective-permute-start | bytes 196616 | tf_op jit(solution)/shard_map/ppermute | solution.py:413
  27.7 8.4 %collective-permute-start.6 = (f32[16,1024]{1,0:T(8,128)S(1)}, f32[16,1024]{1,0:T(8,128)S(1)}, u32[]{:S(2)}, u32[]{:S(2)}) collective-permute-start(f32[16,1024]{1,0:T(8,128)S(1)} %get-tuple-element.71), channel_id=1, source_target_pairs={{0,16},{8,24},{16,0},{24,8},{1,17},{9,25},{17,1},{25,9},{2,18},{10... | collective-permute-start | bytes 196616 | tf_op jit(solution)/shard_map/ppermute | solution.py:413
  31.7 9.1 %collective-permute-start.11 = (f32[16,1024]{1,0:T(8,128)S(1)}, f32[16,1024]{1,0:T(8,128)S(1)}, u32[]{:S(2)}, u32[]{:S(2)}) collective-permute-start(f32[16,1024]{1,0:T(8,128)S(1)} %get-tuple-element.75), channel_id=1, source_target_pairs={{0,8},{8,0},{16,24},{24,16},{1,9},{9,1},{17,25},{25,17},{2,10},{10... | collective-permute-start | bytes 196616 | tf_op jit(solution)/shard_map/ppermute | solution.py:413
  32.4 9.8 %collective-permute-start.12 = (f32[16,1024]{1,0:T(8,128)S(1)}, f32[16,1024]{1,0:T(8,128)S(1)}, u32[]{:S(2)}, u32[]{:S(2)}) collective-permute-start(f32[16,1024]{1,0:T(8,128)S(1)} %get-tuple-element.76), channel_id=1, source_target_pairs={{0,16},{8,24},{16,0},{24,8},{1,17},{9,25},{17,1},{25,9},{2,18},{10... | collective-permute-start | bytes 196616 | tf_op jit(solution)/shard_map/ppermute | solution.py:413
  37.2 10.5 %collective-permute-start.8 = (f32[16,1024]{1,0:T(8,128)S(1)}, f32[16,1024]{1,0:T(8,128)S(1)}, u32[]{:S(2)}, u32[]{:S(2)}) collective-permute-start(f32[16,1024]{1,0:T(8,128)S(1)} %grad_sum.4.refs_1_), channel_id=1, source_target_pairs={{0,8},{8,0},{16,24},{24,16},{1,9},{9,1},{17,25},{25,17},{2,10},{10... | collective-permute-start | bytes 196616 | tf_op jit(solution)/shard_map/ppermute | solution.py:413
  38.6 10.5 %collective-permute-start.9 = (f32[16,1024]{1,0:T(8,128)S(1)}, f32[16,1024]{1,0:T(8,128)S(1)}, u32[]{:S(2)}, u32[]{:S(2)}) collective-permute-start(f32[16,1024]{1,0:T(8,128)S(1)} %grad_sum.4.refs_1_), channel_id=1, source_target_pairs={{0,16},{8,24},{16,0},{24,8},{1,17},{9,25},{17,1},{25,9},{2,18},{10... | collective-permute-start | bytes 196616 | tf_op jit(solution)/shard_map/ppermute | solution.py:413
  42.2 14.9 %collective-permute-start.14 = (f32[16,1024]{1,0:T(8,128)S(1)}, f32[16,1024]{1,0:T(8,128)S(1)}, u32[]{:S(2)}, u32[]{:S(2)}) collective-permute-start(f32[16,1024]{1,0:T(8,128)S(1)} %grad_sum.5.refs_1_), channel_id=1, source_target_pairs={{0,8},{8,0},{16,24},{24,16},{1,9},{9,1},{17,25},{25,17},{2,10},{10... | collective-permute-start | bytes 196616 | tf_op jit(solution)/shard_map/ppermute | solution.py:413
  45.0 12.1 %collective-permute-start.15 = (f32[16,1024]{1,0:T(8,128)S(1)}, f32[16,1024]{1,0:T(8,128)S(1)}, u32[]{:S(2)}, u32[]{:S(2)}) collective-permute-start(f32[16,1024]{1,0:T(8,128)S(1)} %grad_sum.5.refs_1_), channel_id=1, source_target_pairs={{0,16},{8,24},{16,0},{24,8},{1,17},{9,25},{17,1},{25,9},{2,18},{10... | collective-permute-start | bytes 196616 | tf_op jit(solution)/shard_map/ppermute | solution.py:413
  47.7 9.5 %collective-permute-start.16 = (f32[16,1024]{1,0:T(8,128)S(1)}, f32[16,1024]{1,0:T(8,128)S(1)}, u32[]{:S(2)}, u32[]{:S(2)}) collective-permute-start(f32[16,1024]{1,0:T(8,128)S(1)} %grad_sum.5.refs_1_), channel_id=1, source_target_pairs={{0,24},{8,16},{16,8},{24,0},{1,25},{9,17},{17,9},{25,1},{2,26},{10... | collective-permute-start | bytes 196616 | tf_op jit(solution)/shard_map/ppermute | solution.py:413
  90.6 12.2 %collective-permute-start.25 = (f32[16,1152]{1,0:T(8,128)S(1)}, f32[16,1152]{1,0:T(8,128)S(1)}, u32[]{:S(2)}, u32[]{:S(2)}) collective-permute-start(f32[16,1152]{1,0:T(8,128)S(1)} %get-tuple-element.89), channel_id=1, source_target_pairs={{0,8},{8,0},{16,24},{24,16},{1,9},{9,1},{17,25},{25,17},{2,10},{10... | collective-permute-start | bytes 221192 | tf_op jit(solution)/shard_map/ppermute | solution.py:413
  91.9 12.3 %collective-permute-start.26 = (f32[16,1152]{1,0:T(8,128)S(1)}, f32[16,1152]{1,0:T(8,128)S(1)}, u32[]{:S(2)}, u32[]{:S(2)}) collective-permute-start(f32[16,1152]{1,0:T(8,128)S(1)} %get-tuple-element.90), channel_id=1, source_target_pairs={{0,16},{8,24},{16,0},{24,8},{1,17},{9,25},{17,1},{25,9},{2,18},{10... | collective-permute-start | bytes 221192 | tf_op jit(solution)/shard_map/ppermute | solution.py:413
  93.7 10.6 %collective-permute-start.27 = (f32[16,1152]{1,0:T(8,128)S(1)}, f32[16,1152]{1,0:T(8,128)S(1)}, u32[]{:S(2)}, u32[]{:S(2)}) collective-permute-start(f32[16,1152]{1,0:T(8,128)S(1)} %get-tuple-element.91), channel_id=1, source_target_pairs={{0,24},{8,16},{16,8},{24,0},{1,25},{9,17},{17,9},{25,1},{2,26},{10... | collective-permute-start | bytes 221192 | tf_op jit(solution)/shard_map/ppermute | solution.py:413
  100.2 8.5 %collective-permute-start.32 = (f32[16,1024]{1,0:T(8,128)S(1)}, f32[16,1024]{1,0:T(8,128)S(1)}, u32[]{:S(2)}, u32[]{:S(2)}) collective-permute-start(f32[16,1024]{1,0:T(8,128)S(1)} %get-tuple-element.97), channel_id=1, source_target_pairs={{0,16},{8,24},{16,0},{24,8},{1,17},{9,25},{17,1},{25,9},{2,18},{10... | collective-permute-start | bytes 196616 | tf_op jit(solution)/shard_map/ppermute | solution.py:413
  104.3 11.8 %collective-permute-start.28 = (f32[16,1024]{1,0:T(8,128)S(1)}, f32[16,1024]{1,0:T(8,128)S(1)}, u32[]{:S(2)}, u32[]{:S(2)}) collective-permute-start(f32[16,1024]{1,0:T(8,128)S(1)} %get-tuple-element.93.refs_1_.refs_4_), channel_id=1, source_target_pairs={{0,8},{8,0},{16,24},{24,16},{1,9},{9,1},{17,25},{25,17},{2,10},{10... | collective-permute-start | bytes 196616 | tf_op jit(solution)/shard_map/ppermute | solution.py:413
  104.4 13.1 %collective-permute-start.29 = (f32[16,1024]{1,0:T(8,128)S(1)}, f32[16,1024]{1,0:T(8,128)S(1)}, u32[]{:S(2)}, u32[]{:S(2)}) collective-permute-start(f32[16,1024]{1,0:T(8,128)S(1)} %get-tuple-element.93.refs_1_.refs_4_), channel_id=1, source_target_pairs={{0,16},{8,24},{16,0},{24,8},{1,17},{9,25},{17,1},{25,9},{2,18},{10... | collective-permute-start | bytes 196616 | tf_op jit(solution)/shard_map/ppermute | solution.py:413
  107.4 10.1 %collective-permute-start.30 = (f32[16,1024]{1,0:T(8,128)S(1)}, f32[16,1024]{1,0:T(8,128)S(1)}, u32[]{:S(2)}, u32[]{:S(2)}) collective-permute-start(f32[16,1024]{1,0:T(8,128)S(1)} %get-tuple-element.93.refs_1_.refs_4_), channel_id=1, source_target_pairs={{0,24},{8,16},{16,8},{24,0},{1,25},{9,17},{17,9},{25,1},{2,26},{10... | collective-permute-start | bytes 196616 | tf_op jit(solution)/shard_map/ppermute | solution.py:413
  139.4 9.3 %collective-permute-start.49 = (f32[16,1024]{1,0:T(8,128)S(1)}, f32[16,1024]{1,0:T(8,128)S(1)}, u32[]{:S(2)}, u32[]{:S(2)}) collective-permute-start(f32[16,1024]{1,0:T(8,128)S(1)} %get-tuple-element.109), channel_id=1, source_target_pairs={{0,16},{8,24},{16,0},{24,8},{1,17},{9,25},{17,1},{25,9},{2,18},{10... | collective-permute-start | bytes 196616 | tf_op jit(solution)/shard_map/ppermute | solution.py:413
  144.3 10.6 %collective-permute-start.43 = (f32[16,1024]{1,0:T(8,128)S(1)}, f32[16,1024]{1,0:T(8,128)S(1)}, u32[]{:S(2)}, u32[]{:S(2)}) collective-permute-start(f32[16,1024]{1,0:T(8,128)S(1)} %get-tuple-element.105), channel_id=1, source_target_pairs={{0,16},{8,24},{16,0},{24,8},{1,17},{9,25},{17,1},{25,9},{2,18},{10... | collective-permute-start | bytes 196616 | tf_op jit(solution)/shard_map/ppermute | solution.py:413
  146.2 8.6 %collective-permute-start.44 = (f32[16,1024]{1,0:T(8,128)S(1)}, f32[16,1024]{1,0:T(8,128)S(1)}, u32[]{:S(2)}, u32[]{:S(2)}) collective-permute-start(f32[16,1024]{1,0:T(8,128)S(1)} %get-tuple-element.106), channel_id=1, source_target_pairs={{0,24},{8,16},{16,8},{24,0},{1,25},{9,17},{17,9},{25,1},{2,26},{10... | collective-permute-start | bytes 196616 | tf_op jit(solution)/shard_map/ppermute | solution.py:413
  148.7 8.9 %collective-permute-start.51 = (f32[16,1024]{1,0:T(8,128)S(1)}, f32[16,1024]{1,0:T(8,128)S(1)}, u32[]{:S(2)}, u32[]{:S(2)}) collective-permute-start(f32[16,1024]{1,0:T(8,128)S(1)} %grad_sum.7.refs_1_), channel_id=1, source_target_pairs={{0,8},{8,0},{16,24},{24,16},{1,9},{9,1},{17,25},{25,17},{2,10},{10... | collective-permute-start | bytes 196616 | tf_op jit(solution)/shard_map/ppermute | solution.py:413
  152.0 8.3 %collective-permute-start.52 = (f32[16,1024]{1,0:T(8,128)S(1)}, f32[16,1024]{1,0:T(8,128)S(1)}, u32[]{:S(2)}, u32[]{:S(2)}) collective-permute-start(f32[16,1024]{1,0:T(8,128)S(1)} %grad_sum.7.refs_1_), channel_id=1, source_target_pairs={{0,16},{8,24},{16,0},{24,8},{1,17},{9,25},{17,1},{25,9},{2,18},{10... | collective-permute-start | bytes 196616 | tf_op jit(solution)/shard_map/ppermute | solution.py:413
  154.9 11.8 %collective-permute-start.45 = (f32[16,1024]{1,0:T(8,128)S(1)}, f32[16,1024]{1,0:T(8,128)S(1)}, u32[]{:S(2)}, u32[]{:S(2)}) collective-permute-start(f32[16,1024]{1,0:T(8,128)S(1)} %grad_sum.6.refs_1_), channel_id=1, source_target_pairs={{0,8},{8,0},{16,24},{24,16},{1,9},{9,1},{17,25},{25,17},{2,10},{10... | collective-permute-start | bytes 196616 | tf_op jit(solution)/shard_map/ppermute | solution.py:413
  157.6 9.1 %collective-permute-start.46 = (f32[16,1024]{1,0:T(8,128)S(1)}, f32[16,1024]{1,0:T(8,128)S(1)}, u32[]{:S(2)}, u32[]{:S(2)}) collective-permute-start(f32[16,1024]{1,0:T(8,128)S(1)} %grad_sum.6.refs_1_), channel_id=1, source_target_pairs={{0,16},{8,24},{16,0},{24,8},{1,17},{9,25},{17,1},{25,9},{2,18},{10... | collective-permute-start | bytes 196616 | tf_op jit(solution)/shard_map/ppermute | solution.py:413
  157.6 9.1 %collective-permute-start.47 = (f32[16,1024]{1,0:T(8,128)S(1)}, f32[16,1024]{1,0:T(8,128)S(1)}, u32[]{:S(2)}, u32[]{:S(2)}) collective-permute-start(f32[16,1024]{1,0:T(8,128)S(1)} %grad_sum.6.refs_1_), channel_id=1, source_target_pairs={{0,24},{8,16},{16,8},{24,0},{1,25},{9,17},{17,9},{25,1},{2,26},{10... | collective-permute-start | bytes 196616 | tf_op jit(solution)/shard_map/ppermute | solution.py:413
  174.4 8.4 %collective-permute-start.56 = (f32[16,2048]{1,0:T(8,128)S(1)}, f32[16,2048]{1,0:T(8,128)S(1)}, u32[]{:S(2)}, u32[]{:S(2)}) collective-permute-start(f32[16,2048]{1,0:T(8,128)S(1)} %get-tuple-element.113), channel_id=1, source_target_pairs={{0,4},{1,5},{2,6},{3,7},{4,0},{5,1},{6,2},{7,3},{8,12},{9,13},{10,... | collective-permute-start | bytes 393224 | tf_op jit(solution)/shard_map/ppermute | solution.py:413
  196.8 11.9 %collective-permute-start.62 = (f32[16,1152]{1,0:T(8,128)S(1)}, f32[16,1152]{1,0:T(8,128)S(1)}, u32[]{:S(2)}, u32[]{:S(2)}) collective-permute-start(f32[16,1152]{1,0:T(8,128)S(1)} %get-tuple-element.118), channel_id=1, source_target_pairs={{0,8},{8,0},{16,24},{24,16},{1,9},{9,1},{17,25},{25,17},{2,10},{10... | collective-permute-start | bytes 221192 | tf_op jit(solution)/shard_map/ppermute | solution.py:413
  199.7 11.4 %collective-permute-start.63 = (f32[16,1152]{1,0:T(8,128)S(1)}, f32[16,1152]{1,0:T(8,128)S(1)}, u32[]{:S(2)}, u32[]{:S(2)}) collective-permute-start(f32[16,1152]{1,0:T(8,128)S(1)} %get-tuple-element.119), channel_id=1, source_target_pairs={{0,16},{8,24},{16,0},{24,8},{1,17},{9,25},{17,1},{25,9},{2,18},{10... | collective-permute-start | bytes 221192 | tf_op jit(solution)/shard_map/ppermute | solution.py:413
  199.7 11.4 %collective-permute-start.64 = (f32[16,1152]{1,0:T(8,128)S(1)}, f32[16,1152]{1,0:T(8,128)S(1)}, u32[]{:S(2)}, u32[]{:S(2)}) collective-permute-start(f32[16,1152]{1,0:T(8,128)S(1)} %get-tuple-element.120), channel_id=1, source_target_pairs={{0,24},{8,16},{16,8},{24,0},{1,25},{9,17},{17,9},{25,1},{2,26},{10... | collective-permute-start | bytes 221192 | tf_op jit(solution)/shard_map/ppermute | solution.py:413
  207.8 8.8 %collective-permute-start.69 = (f32[16,1024]{1,0:T(8,128)S(1)}, f32[16,1024]{1,0:T(8,128)S(1)}, u32[]{:S(2)}, u32[]{:S(2)}) collective-permute-start(f32[16,1024]{1,0:T(8,128)S(1)} %get-tuple-element.124), channel_id=1, source_target_pairs={{0,16},{8,24},{16,0},{24,8},{1,17},{9,25},{17,1},{25,9},{2,18},{10... | collective-permute-start | bytes 196616 | tf_op jit(solution)/shard_map/ppermute | solution.py:413
  211.2 10.9 %collective-permute-start.65 = (f32[16,1024]{1,0:T(8,128)S(1)}, f32[16,1024]{1,0:T(8,128)S(1)}, u32[]{:S(2)}, u32[]{:S(2)}) collective-permute-start(f32[16,1024]{1,0:T(8,128)S(1)} %get-tuple-element.121.refs_0_), channel_id=1, source_target_pairs={{0,8},{8,0},{16,24},{24,16},{1,9},{9,1},{17,25},{25,17},{2,10},{10... | collective-permute-start | bytes 196616 | tf_op jit(solution)/shard_map/ppermute | solution.py:413
  211.4 13.1 %collective-permute-start.66 = (f32[16,1024]{1,0:T(8,128)S(1)}, f32[16,1024]{1,0:T(8,128)S(1)}, u32[]{:S(2)}, u32[]{:S(2)}) collective-permute-start(f32[16,1024]{1,0:T(8,128)S(1)} %get-tuple-element.121.refs_0_), channel_id=1, source_target_pairs={{0,16},{8,24},{16,0},{24,8},{1,17},{9,25},{17,1},{25,9},{2,18},{10... | collective-permute-start | bytes 196616 | tf_op jit(solution)/shard_map/ppermute | solution.py:413
  213.2 11.3 %collective-permute-start.67 = (f32[16,1024]{1,0:T(8,128)S(1)}, f32[16,1024]{1,0:T(8,128)S(1)}, u32[]{:S(2)}, u32[]{:S(2)}) collective-permute-start(f32[16,1024]{1,0:T(8,128)S(1)} %get-tuple-element.121.refs_0_), channel_id=1, source_target_pairs={{0,24},{8,16},{16,8},{24,0},{1,25},{9,17},{17,9},{25,1},{2,26},{10... | collective-permute-start | bytes 196616 | tf_op jit(solution)/shard_map/ppermute | solution.py:413
  (50 other events, 373.0 us)

commit v5 on v4

--- a/solution.py
+++ b/solution.py
@@ -460,10 +460,11 @@
         return (1 - core_of()) * row_half
 
     def to_rank(cuts):
-        return [cuts[0]] + [swap(cuts[k], "rows", k) for k in range(1, depth_ranks)]
+        return [cuts[0]] + [swap(cuts[k], "rows", k) for k in reversed(range(1, depth_ranks))]
 
     def all_rows(x):
-        return [x] + [swap(x, "rows", k) for k in range(1, depth_ranks)]
+        far_first = [swap(x, "rows", k) for k in reversed(range(1, depth_ranks))]
+        return [x] + far_first[::-1]
 
     a_pieces = None
     for step in range(STEPS):

time: 229 us -> 221 us (0.965)
  starting transfers between devices: 107 us -> 97.8 us
    ppermute x74, starting transfers between devices: 107 us -> 97.8 us  [swap(): return lax.ppermute(x, axis, [(i, i ^ mask) for i in range(size)])]
  transfers between devices with their start and end apart: 74 -> 74, of which waited for: 26 -> 28; matrix products, arithmetic and copies ran while one was open for 0% -> 0% of each run, Pallas kernels for 17% -> 18%
where the time goes in v5:
time: 221 us
  starting transfers between devices  97.8 us (44%)
  Pallas kernels  66.6 us (30%)
  waiting for transfers between devices  52.4 us (24%)
  local copies, waits for them, and re-layouts  3.37 us (2%)
    ppermute x74, starting transfers between devices, swap(): return lax.ppermute(x, axis, [(i, i ^ mask) for i in range(size)])  97.8 us
    pallas_call x17, Pallas kernels, call(): pl.pallas_call(whole, in_specs=[WHOLE if near else FAR] * n_weights + [WH...  57.4 us
    ppermute x74, waiting for transfers between devices, swap(): return lax.ppermute(x, axis, [(i, i ^ mask) for i in range(size)])  52.4 us
    pallas_call x1, Pallas kernels, tile_and_logits(): pl.pallas_call(kernel, grid=(rows // size,), in_specs=[pl.BlockSpec((size...  7.57 us
  transfers between devices with their start and end apart: 74, of which 28 were waited for; matrix products, arithmetic and copies ran while one was open for 0% of the time, Pallas kernels for 18%

profile of v5, /device:TPU:0, one launch (start us, length us, event | category | flops | bytes accessed | tf_op | source)
XLA Modules:
  0.0 220.6 jit_solution(5393445973174644827)
XLA Ops:
  3.4 7.6 %tile_and_logits.1 = (f32[2,512,2048]{2,1,0:T(8,128)S(1)}, f32[32,1024]{1,0:T(8,128)S(1)}, f32[32,1024]{1,0:T(8,128)S(1)}) custom-call(f32[1024,128]{1,0:T(8,128)S(1)} %copy-done.5, f32[2048,128]{1,0:T(8,128)S(1)} %copy-done.4, f32[64,2048]{1,0:T(8,128)S(1)} %bitcast.7), custom_call_target="tpu_custom_call" | custom-call | flops 3221225472 | bytes 8388608 | tf_op jit(solution)/shard_map/tile_and_logits/pallas_call | solution.py:274
  12.5 2.9 %collective-permute-start.1 = (f32[32,1024]{1,0:T(8,128)S(1)}, f32[32,1024]{1,0:T(8,128)S(1)}, u32[]{:S(2)}, u32[]{:S(2)}) collective-permute-start(f32[32,1024]{1,0:T(8,128)S(1)} %chip_logits.2.refs_0_), channel_id=1, source_target_pairs={{0,2},{1,3},{2,0},{3,1},{4,6},{5,7},{6,4},{7,5},{8,10},{9,11},{10,... | collective-permute-start | bytes 393224 | tf_op jit(solution)/shard_map/ppermute | solution.py:413
  19.3 4.2 %collective-permute-done.2.refs_2_ = f32[32,1024]{1,0:T(8,128)S(1)} collective-permute-done((f32[32,1024]{1,0:T(8,128)S(1)}, f32[32,1024]{1,0:T(8,128)S(1)}, u32[]{:S(2)}, u32[]{:S(2)}) %collective-permute-start.2) | collective-permute-done | bytes 131104 | tf_op jit(solution)/shard_map/ppermute | solution.py:413
  26.1 3.7 %collective-permute-start.5 = (f32[16,1024]{1,0:T(8,128)S(1)}, f32[16,1024]{1,0:T(8,128)S(1)}, u32[]{:S(2)}, u32[]{:S(2)}) collective-permute-start(f32[16,1024]{1,0:T(8,128)S(1)} %get-tuple-element.70), channel_id=1, source_target_pairs={{0,24},{8,16},{16,8},{24,0},{1,25},{9,17},{17,9},{25,1},{2,26},{10... | collective-permute-start | bytes 196616 | tf_op jit(solution)/shard_map/ppermute | solution.py:413
  31.7 3.7 %collective-permute-start.11 = (f32[16,1024]{1,0:T(8,128)S(1)}, f32[16,1024]{1,0:T(8,128)S(1)}, u32[]{:S(2)}, u32[]{:S(2)}) collective-permute-start(f32[16,1024]{1,0:T(8,128)S(1)} %get-tuple-element.75), channel_id=1, source_target_pairs={{0,24},{8,16},{16,8},{24,0},{1,25},{9,17},{17,9},{25,1},{2,26},{10... | collective-permute-start | bytes 196616 | tf_op jit(solution)/shard_map/ppermute | solution.py:413
  37.5 2.9 %collective-permute-start.9 = (f32[16,1024]{1,0:T(8,128)S(1)}, f32[16,1024]{1,0:T(8,128)S(1)}, u32[]{:S(2)}, u32[]{:S(2)}) collective-permute-start(f32[16,1024]{1,0:T(8,128)S(1)} %grad_sum.4.refs_1_), channel_id=1, source_target_pairs={{0,16},{8,24},{16,0},{24,8},{1,17},{9,25},{17,1},{25,9},{2,18},{10... | collective-permute-start | bytes 196616 | tf_op jit(solution)/shard_map/ppermute | solution.py:413
  43.3 2.9 %collective-permute-start.15 = (f32[16,1024]{1,0:T(8,128)S(1)}, f32[16,1024]{1,0:T(8,128)S(1)}, u32[]{:S(2)}, u32[]{:S(2)}) collective-permute-start(f32[16,1024]{1,0:T(8,128)S(1)} %grad_sum.5.refs_1_), channel_id=1, source_target_pairs={{0,16},{8,24},{16,0},{24,8},{1,17},{9,25},{17,1},{25,9},{2,18},{10... | collective-permute-start | bytes 196616 | tf_op jit(solution)/shard_map/ppermute | solution.py:413
  46.9 8.0 %fwda.2 = (f32[64,4096]{1,0:T(8,128)S(1)}, f32[8,512,1024]{2,1,0:T(8,128)S(1)}) custom-call(f32[4096,2048]{1,0:T(8,128)} %refs_0_.5, f32[16,1024]{1,0:T(8,128)S(1)} %grad_sum.4.refs_1_, f32[16,1024]{1,0:T(8,128)S(1)} %collective-permute-done.8.refs_2_, f32[16,1024]{1,0:T(8,128)S(1)} %collective-permute-done.9.refs_3_, ...), custom_call_target="tpu_custom_call" | custom-call | flops 1610612736 | bytes 16777216 | tf_op jit(solution)/shard_map/fwda/pallas_call | solution.py:144
  54.9 4.8 %fwdb.2 = (f32[64,2048]{1,0:T(8,128)S(1)}, f32[4,512,1024]{2,1,0:T(8,128)S(1)}) custom-call(f32[4096,2048]{1,0:T(8,128)} %refs_0_.5, f32[16,1024]{1,0:T(8,128)S(1)} %grad_sum.5.refs_1_, f32[16,1024]{1,0:T(8,128)S(1)} %collective-permute-done.14.refs_2_, f32[16,1024]{1,0:T(8,128)S(1)} %collective-permute-done.15.refs_3_, ...), custom_call_target="tpu_custom_call" | custom-call | flops 805306368 | bytes 8388608 | tf_op jit(solution)/shard_map/fwdb/pallas_call | solution.py:144
  59.8 4.9 %fwdc.2 = (f32[64,2048]{1,0:T(8,128)S(1)}, f32[4,512,1024]{2,1,0:T(8,128)S(1)}) custom-call(f32[4096,2048]{1,0:T(8,128)} %refs_0_.5, f32[16,1024]{1,0:T(8,128)S(1)} %grad_sum.5.refs_1_, f32[16,1024]{1,0:T(8,128)S(1)} %collective-permute-done.14.refs_2_, f32[16,1024]{1,0:T(8,128)S(1)} %collective-permute-done.15.refs_3_, ...), custom_call_target="tpu_custom_call" | custom-call | flops 805306368 | bytes 8388608 | tf_op jit(solution)/shard_map/fwdc/pallas_call | solution.py:144
  68.4 2.8 %collective-permute-done.18.refs_1_ = f32[16,2048]{1,0:T(8,128)S(1)} collective-permute-done((f32[16,2048]{1,0:T(8,128)S(1)}, f32[16,2048]{1,0:T(8,128)S(1)}, u32[]{:S(2)}, u32[]{:S(2)}) %collective-permute-start.18) | collective-permute-done | bytes 131104 | tf_op jit(solution)/shard_map/ppermute | solution.py:413
  78.1 2.9 %collective-permute-done.21.refs_1_.refs_2_.refs_3_ = f32[16,2048]{1,0:T(8,128)S(1)} collective-permute-done((f32[16,2048]{1,0:T(8,128)S(1)}, f32[16,2048]{1,0:T(8,128)S(1)}, u32[]{:S(2)}, u32[]{:S(2)}) %collective-permute-start.21) | collective-permute-done | bytes 131104 | tf_op jit(solution)/shard_map/ppermute | solution.py:413
  88.4 3.2 %collective-permute-start.25 = (f32[16,1152]{1,0:T(8,128)S(1)}, f32[16,1152]{1,0:T(8,128)S(1)}, u32[]{:S(2)}, u32[]{:S(2)}) collective-permute-start(f32[16,1152]{1,0:T(8,128)S(1)} %get-tuple-element.89), channel_id=1, source_target_pairs={{0,24},{8,16},{16,8},{24,0},{1,25},{9,17},{17,9},{25,1},{2,26},{10... | collective-permute-start | bytes 221192 | tf_op jit(solution)/shard_map/ppermute | solution.py:413
  93.0 4.7 %backc.2 = (f32[16,1024]{1,0:T(8,128)S(1)}, f32[16,1024]{1,0:T(8,128)S(1)}, f32[16,1024]{1,0:T(8,128)S(1)}, f32[16,1024]{1,0:T(8,128)S(1)}) custom-call(f32[4,512,1024]{2,1,0:T(8,128)S(1)} %get-tuple-element.79.refs_0_, f32[4,512,1024]{2,1,0:T(8,128)S(1)} %get-tuple-element.94.refs_1_.refs_0_, f32[16,2048]{1,0:T(8,128)S(1)} %fwd_sum.2.refs_0_.refs_1_.refs_2_, ...), custom_call_target="tpu_custom_call" | custom-call | flops 1610612736 | bytes 16777216 | tf_op jit(solution)/shard_map/backc/pallas_call | solution.py:144
  97.7 3.0 %collective-permute-start.31 = (f32[16,1024]{1,0:T(8,128)S(1)}, f32[16,1024]{1,0:T(8,128)S(1)}, u32[]{:S(2)}, u32[]{:S(2)}) collective-permute-start(f32[16,1024]{1,0:T(8,128)S(1)} %get-tuple-element.96), channel_id=1, source_target_pairs={{0,24},{8,16},{16,8},{24,0},{1,25},{9,17},{17,9},{25,1},{2,26},{10... | collective-permute-start | bytes 196616 | tf_op jit(solution)/shard_map/ppermute | solution.py:413
  108.6 3.5 %collective-permute-start.35 = (f32[16,1024]{1,0:T(8,128)S(1)}, f32[16,1024]{1,0:T(8,128)S(1)}, u32[]{:S(2)}, u32[]{:S(2)}) collective-permute-start(f32[16,1024]{1,0:T(8,128)S(1)} %update.5.refs_5_.refs_4_), channel_id=1, source_target_pairs={{0,16},{8,24},{16,0},{24,8},{1,17},{9,25},{17,1},{25,9},{2,18},{10... | collective-permute-start | bytes 196616 | tf_op jit(solution)/shard_map/ppermute | solution.py:413
  112.9 3.8 %collective-permute-done.35.refs_7_ = f32[16,1024]{1,0:T(8,128)S(1)} collective-permute-done((f32[16,1024]{1,0:T(8,128)S(1)}, f32[16,1024]{1,0:T(8,128)S(1)}, u32[]{:S(2)}, u32[]{:S(2)}) %collective-permute-start.35) | collective-permute-done | bytes 65568 | tf_op jit(solution)/shard_map/ppermute | solution.py:413
  118.3 3.1 %logits.1 = (f32[32,1024]{1,0:T(8,128)S(1)}, f32[32,1024]{1,0:T(8,128)S(1)}) custom-call(f32[2,512,2048]{2,1,0:T(8,128)S(1)} %get-tuple-element.66.refs_0_, f32[16,1024]{1,0:T(8,128)S(1)} %get-tuple-element.93.refs_1_.refs_4_, f32[16,1024]{1,0:T(8,128)S(1)} %collective-permute-done.28.refs_2_, f32[16,1024]{1,0:T(8,128)S(1)} %collective-permute-done.29.refs_3_, ...), custom_call_target="tpu_custom_call" | custom-call | flops 805306368 | bytes 8388608 | tf_op jit(solution)/shard_map/logits/pallas_call | solution.py:144
  126.4 2.9 %collective-permute-done.38.refs_1_ = f32[32,1024]{1,0:T(8,128)S(1)} collective-permute-done((f32[32,1024]{1,0:T(8,128)S(1)}, f32[32,1024]{1,0:T(8,128)S(1)}, u32[]{:S(2)}, u32[]{:S(2)}) %collective-permute-start.38) | collective-permute-done | bytes 131104 | tf_op jit(solution)/shard_map/ppermute | solution.py:413
  129.2 2.8 %collective-permute-done.39.refs_2_ = f32[32,1024]{1,0:T(8,128)S(1)} collective-permute-done((f32[32,1024]{1,0:T(8,128)S(1)}, f32[32,1024]{1,0:T(8,128)S(1)}, u32[]{:S(2)}, u32[]{:S(2)}) %collective-permute-start.39) | collective-permute-done | bytes 131104 | tf_op jit(solution)/shard_map/ppermute | solution.py:413
  144.8 3.7 %collective-permute-start.52 = (f32[16,1024]{1,0:T(8,128)S(1)}, f32[16,1024]{1,0:T(8,128)S(1)}, u32[]{:S(2)}, u32[]{:S(2)}) collective-permute-start(f32[16,1024]{1,0:T(8,128)S(1)} %grad_sum.7.refs_1_), channel_id=1, source_target_pairs={{0,16},{8,24},{16,0},{24,8},{1,17},{9,25},{17,1},{25,9},{2,18},{10... | collective-permute-start | bytes 196616 | tf_op jit(solution)/shard_map/ppermute | solution.py:413
  150.1 3.8 %collective-permute-start.46 = (f32[16,1024]{1,0:T(8,128)S(1)}, f32[16,1024]{1,0:T(8,128)S(1)}, u32[]{:S(2)}, u32[]{:S(2)}) collective-permute-start(f32[16,1024]{1,0:T(8,128)S(1)} %grad_sum.6.refs_1_), channel_id=1, source_target_pairs={{0,16},{8,24},{16,0},{24,8},{1,17},{9,25},{17,1},{25,9},{2,18},{10... | collective-permute-start | bytes 196616 | tf_op jit(solution)/shard_map/ppermute | solution.py:413
  155.1 6.4 %fwda.3.refs_5_ = f32[64,4096]{1,0:T(8,128)S(1)} custom-call(f32[8,512,1024]{2,1,0:T(8,128)S(1)} %get-tuple-element.73.refs_0_, f32[16,1024]{1,0:T(8,128)S(1)} %grad_sum.7.refs_1_, f32[16,1024]{1,0:T(8,128)S(1)} %collective-permute-done.51.refs_2_, f32[16,1024]{1,0:T(8,128)S(1)} %collective-permute-done.52.refs_3_, ...), custom_call_target="tpu_custom_call" | custom-call | flops 1610612736 | bytes 16777216 | tf_op jit(solution)/shard_map/fwda/pallas_call | solution.py:144
  161.5 3.2 %fwdb.3 = f32[64,2048]{1,0:T(8,128)S(1)} custom-call(f32[4,512,1024]{2,1,0:T(8,128)S(1)} %get-tuple-element.94.refs_1_.refs_0_, f32[16,1024]{1,0:T(8,128)S(1)} %grad_sum.6.refs_1_, f32[16,1024]{1,0:T(8,128)S(1)} %collective-permute-done.45.refs_2_, f32[16,1024]{1,0:T(8,128)S(1)} %collective-permute-done.46.refs_3_, ...), custom_call_target="tpu_custom_call" | custom-call | flops 805306368 | bytes 8388608 | tf_op jit(solution)/shard_map/fwdb/pallas_call | solution.py:144
  164.8 3.2 %fwdc.3.a_ref = f32[64,2048]{1,0:T(8,128)S(1)} custom-call(f32[4,512,1024]{2,1,0:T(8,128)S(1)} %bitcast.4, f32[16,1024]{1,0:T(8,128)S(1)} %grad_sum.6.refs_1_, f32[16,1024]{1,0:T(8,128)S(1)} %collective-permute-done.45.refs_2_, f32[16,1024]{1,0:T(8,128)S(1)} %collective-permute-done.46.refs_3_, f32[16,1024]{1,0:T(8,128)S(1)} %collective-permute-done.47.refs_4_, ...), custom_call_target="tpu_custom_call" | custom-call | flops 805306368 | bytes 8388608 | tf_op jit(solution)/shard_map/fwdc/pallas_call | solution.py:144
  171.7 2.8 %collective-permute-done.55.refs_1_ = f32[16,2048]{1,0:T(8,128)S(1)} collective-permute-done((f32[16,2048]{1,0:T(8,128)S(1)}, f32[16,2048]{1,0:T(8,128)S(1)}, u32[]{:S(2)}, u32[]{:S(2)}) %collective-permute-start.55) | collective-permute-done | bytes 131104 | tf_op jit(solution)/shard_map/ppermute | solution.py:413
  174.5 3.1 %collective-permute-done.56.refs_2_ = f32[16,2048]{1,0:T(8,128)S(1)} collective-permute-done((f32[16,2048]{1,0:T(8,128)S(1)}, f32[16,2048]{1,0:T(8,128)S(1)}, u32[]{:S(2)}, u32[]{:S(2)}) %collective-permute-start.56) | collective-permute-done | bytes 131104 | tf_op jit(solution)/shard_map/ppermute | solution.py:413
  183.5 2.9 %collective-permute-done.59.refs_2_.refs_3_.refs_4_ = f32[16,2048]{1,0:T(8,128)S(1)} collective-permute-done((f32[16,2048]{1,0:T(8,128)S(1)}, f32[16,2048]{1,0:T(8,128)S(1)}, u32[]{:S(2)}, u32[]{:S(2)}) %collective-permute-start.59) | collective-permute-done | bytes 131104 | tf_op jit(solution)/shard_map/ppermute | solution.py:413
  191.6 2.7 %collective-permute-start.62 = (f32[16,1152]{1,0:T(8,128)S(1)}, f32[16,1152]{1,0:T(8,128)S(1)}, u32[]{:S(2)}, u32[]{:S(2)}) collective-permute-start(f32[16,1152]{1,0:T(8,128)S(1)} %get-tuple-element.118), channel_id=1, source_target_pairs={{0,24},{8,16},{16,8},{24,0},{1,25},{9,17},{17,9},{25,1},{2,26},{10... | collective-permute-start | bytes 221192 | tf_op jit(solution)/shard_map/ppermute | solution.py:413
  196.0 4.5 %backc.3 = (f32[16,1024]{1,0:T(8,128)S(1)}, f32[16,1024]{1,0:T(8,128)S(1)}, f32[16,1024]{1,0:T(8,128)S(1)}, f32[16,1024]{1,0:T(8,128)S(1)}) custom-call(f32[4,512,1024]{2,1,0:T(8,128)S(1)} %bitcast.4, f32[4,512,1024]{2,1,0:T(8,128)S(1)} %get-tuple-element.94.refs_1_.refs_0_, f32[16,2048]{1,0:T(8,128)S(1)} %fwd_sum.3.refs_0_.refs_1_.refs_2_, ...), custom_call_target="tpu_custom_call" | custom-call | flops 1610612736 | bytes 16777216 | tf_op jit(solution)/shard_map/backc/pallas_call | solution.py:144
  205.4 2.9 %collective-permute-start.66 = (f32[16,1024]{1,0:T(8,128)S(1)}, f32[16,1024]{1,0:T(8,128)S(1)}, u32[]{:S(2)}, u32[]{:S(2)}) collective-permute-start(f32[16,1024]{1,0:T(8,128)S(1)} %get-tuple-element.121.refs_0_), channel_id=1, source_target_pairs={{0,16},{8,24},{16,0},{24,8},{1,17},{9,25},{17,1},{25,9},{2,18},{10... | collective-permute-start | bytes 196616 | tf_op jit(solution)/shard_map/ppermute | solution.py:413
  215.3 3.3 %collective-permute-done.72.refs_6_ = f32[16,1024]{1,0:T(8,128)S(1)} collective-permute-done((f32[16,1024]{1,0:T(8,128)S(1)}, f32[16,1024]{1,0:T(8,128)S(1)}, u32[]{:S(2)}, u32[]{:S(2)}) %collective-permute-start.72) | collective-permute-done | bytes 65568 | tf_op jit(solution)/shard_map/ppermute | solution.py:413
  (171 shorter events, 99.4 us)
Async XLA Ops:
  15.4 8.1 %collective-permute-start.2 = (f32[32,1024]{1,0:T(8,128)S(1)}, f32[32,1024]{1,0:T(8,128)S(1)}, u32[]{:S(2)}, u32[]{:S(2)}) collective-permute-start(f32[32,1024]{1,0:T(8,128)S(1)} %chip_logits.2.refs_0_), channel_id=1, source_target_pairs={{0,4},{1,5},{2,6},{3,7},{4,0},{5,1},{6,2},{7,3},{8,12},{9,13},{10,... | collective-permute-start | bytes 393224 | tf_op jit(solution)/shard_map/ppermute | solution.py:413
  26.1 9.3 %collective-permute-start.5 = (f32[16,1024]{1,0:T(8,128)S(1)}, f32[16,1024]{1,0:T(8,128)S(1)}, u32[]{:S(2)}, u32[]{:S(2)}) collective-permute-start(f32[16,1024]{1,0:T(8,128)S(1)} %get-tuple-element.70), channel_id=1, source_target_pairs={{0,24},{8,16},{16,8},{24,0},{1,25},{9,17},{17,9},{25,1},{2,26},{10... | collective-permute-start | bytes 196616 | tf_op jit(solution)/shard_map/ppermute | solution.py:413
  31.7 8.7 %collective-permute-start.11 = (f32[16,1024]{1,0:T(8,128)S(1)}, f32[16,1024]{1,0:T(8,128)S(1)}, u32[]{:S(2)}, u32[]{:S(2)}) collective-permute-start(f32[16,1024]{1,0:T(8,128)S(1)} %get-tuple-element.75), channel_id=1, source_target_pairs={{0,24},{8,16},{16,8},{24,0},{1,25},{9,17},{17,9},{25,1},{2,26},{10... | collective-permute-start | bytes 196616 | tf_op jit(solution)/shard_map/ppermute | solution.py:413
  36.6 9.5 %collective-permute-start.8 = (f32[16,1024]{1,0:T(8,128)S(1)}, f32[16,1024]{1,0:T(8,128)S(1)}, u32[]{:S(2)}, u32[]{:S(2)}) collective-permute-start(f32[16,1024]{1,0:T(8,128)S(1)} %grad_sum.4.refs_1_), channel_id=1, source_target_pairs={{0,8},{8,0},{16,24},{24,16},{1,9},{9,1},{17,25},{25,17},{2,10},{10... | collective-permute-start | bytes 196616 | tf_op jit(solution)/shard_map/ppermute | solution.py:413
  37.5 9.4 %collective-permute-start.9 = (f32[16,1024]{1,0:T(8,128)S(1)}, f32[16,1024]{1,0:T(8,128)S(1)}, u32[]{:S(2)}, u32[]{:S(2)}) collective-permute-start(f32[16,1024]{1,0:T(8,128)S(1)} %grad_sum.4.refs_1_), channel_id=1, source_target_pairs={{0,16},{8,24},{16,0},{24,8},{1,17},{9,25},{17,1},{25,9},{2,18},{10... | collective-permute-start | bytes 196616 | tf_op jit(solution)/shard_map/ppermute | solution.py:413
  42.4 12.5 %collective-permute-start.14 = (f32[16,1024]{1,0:T(8,128)S(1)}, f32[16,1024]{1,0:T(8,128)S(1)}, u32[]{:S(2)}, u32[]{:S(2)}) collective-permute-start(f32[16,1024]{1,0:T(8,128)S(1)} %grad_sum.5.refs_1_), channel_id=1, source_target_pairs={{0,8},{8,0},{16,24},{24,16},{1,9},{9,1},{17,25},{25,17},{2,10},{10... | collective-permute-start | bytes 196616 | tf_op jit(solution)/shard_map/ppermute | solution.py:413
  43.3 11.6 %collective-permute-start.15 = (f32[16,1024]{1,0:T(8,128)S(1)}, f32[16,1024]{1,0:T(8,128)S(1)}, u32[]{:S(2)}, u32[]{:S(2)}) collective-permute-start(f32[16,1024]{1,0:T(8,128)S(1)} %grad_sum.5.refs_1_), channel_id=1, source_target_pairs={{0,16},{8,24},{16,0},{24,8},{1,17},{9,25},{17,1},{25,9},{2,18},{10... | collective-permute-start | bytes 196616 | tf_op jit(solution)/shard_map/ppermute | solution.py:413
  46.1 8.8 %collective-permute-start.16 = (f32[16,1024]{1,0:T(8,128)S(1)}, f32[16,1024]{1,0:T(8,128)S(1)}, u32[]{:S(2)}, u32[]{:S(2)}) collective-permute-start(f32[16,1024]{1,0:T(8,128)S(1)} %grad_sum.5.refs_1_), channel_id=1, source_target_pairs={{0,24},{8,16},{16,8},{24,0},{1,25},{9,17},{17,9},{25,1},{2,26},{10... | collective-permute-start | bytes 196616 | tf_op jit(solution)/shard_map/ppermute | solution.py:413
  75.4 7.8 %collective-permute-start.22 = (f32[16,2048]{1,0:T(8,128)S(1)}, f32[16,2048]{1,0:T(8,128)S(1)}, u32[]{:S(2)}, u32[]{:S(2)}) collective-permute-start(f32[16,2048]{1,0:T(8,128)S(1)} %fwd_sum.2.refs_0_.refs_1_.refs_2_), channel_id=1, source_target_pairs={{0,4},{1,5},{2,6},{3,7},{4,0},{5,1},{6,2},{7,3},{8,12},{9,13},{10,... | collective-permute-start | bytes 393224 | tf_op jit(solution)/shard_map/ppermute | solution.py:413
  88.4 12.9 %collective-permute-start.25 = (f32[16,1152]{1,0:T(8,128)S(1)}, f32[16,1152]{1,0:T(8,128)S(1)}, u32[]{:S(2)}, u32[]{:S(2)}) collective-permute-start(f32[16,1152]{1,0:T(8,128)S(1)} %get-tuple-element.89), channel_id=1, source_target_pairs={{0,24},{8,16},{16,8},{24,0},{1,25},{9,17},{17,9},{25,1},{2,26},{10... | collective-permute-start | bytes 221192 | tf_op jit(solution)/shard_map/ppermute | solution.py:413
  91.6 10.6 %collective-permute-start.26 = (f32[16,1152]{1,0:T(8,128)S(1)}, f32[16,1152]{1,0:T(8,128)S(1)}, u32[]{:S(2)}, u32[]{:S(2)}) collective-permute-start(f32[16,1152]{1,0:T(8,128)S(1)} %get-tuple-element.90), channel_id=1, source_target_pairs={{0,16},{8,24},{16,0},{24,8},{1,17},{9,25},{17,1},{25,9},{2,18},{10... | collective-permute-start | bytes 221192 | tf_op jit(solution)/shard_map/ppermute | solution.py:413
  93.0 9.2 %collective-permute-start.27 = (f32[16,1152]{1,0:T(8,128)S(1)}, f32[16,1152]{1,0:T(8,128)S(1)}, u32[]{:S(2)}, u32[]{:S(2)}) collective-permute-start(f32[16,1152]{1,0:T(8,128)S(1)} %get-tuple-element.91), channel_id=1, source_target_pairs={{0,8},{8,0},{16,24},{24,16},{1,9},{9,1},{17,25},{25,17},{2,10},{10... | collective-permute-start | bytes 221192 | tf_op jit(solution)/shard_map/ppermute | solution.py:413
  97.7 8.1 %collective-permute-start.31 = (f32[16,1024]{1,0:T(8,128)S(1)}, f32[16,1024]{1,0:T(8,128)S(1)}, u32[]{:S(2)}, u32[]{:S(2)}) collective-permute-start(f32[16,1024]{1,0:T(8,128)S(1)} %get-tuple-element.96), channel_id=1, source_target_pairs={{0,24},{8,16},{16,8},{24,0},{1,25},{9,17},{17,9},{25,1},{2,26},{10... | collective-permute-start | bytes 196616 | tf_op jit(solution)/shard_map/ppermute | solution.py:413
  102.3 9.9 %collective-permute-start.28 = (f32[16,1024]{1,0:T(8,128)S(1)}, f32[16,1024]{1,0:T(8,128)S(1)}, u32[]{:S(2)}, u32[]{:S(2)}) collective-permute-start(f32[16,1024]{1,0:T(8,128)S(1)} %get-tuple-element.93.refs_1_.refs_4_), channel_id=1, source_target_pairs={{0,8},{8,0},{16,24},{24,16},{1,9},{9,1},{17,25},{25,17},{2,10},{10... | collective-permute-start | bytes 196616 | tf_op jit(solution)/shard_map/ppermute | solution.py:413
  103.4 9.2 %collective-permute-start.29 = (f32[16,1024]{1,0:T(8,128)S(1)}, f32[16,1024]{1,0:T(8,128)S(1)}, u32[]{:S(2)}, u32[]{:S(2)}) collective-permute-start(f32[16,1024]{1,0:T(8,128)S(1)} %get-tuple-element.93.refs_1_.refs_4_), channel_id=1, source_target_pairs={{0,16},{8,24},{16,0},{24,8},{1,17},{9,25},{17,1},{25,9},{2,18},{10... | collective-permute-start | bytes 196616 | tf_op jit(solution)/shard_map/ppermute | solution.py:413
  108.6 8.0 %collective-permute-start.35 = (f32[16,1024]{1,0:T(8,128)S(1)}, f32[16,1024]{1,0:T(8,128)S(1)}, u32[]{:S(2)}, u32[]{:S(2)}) collective-permute-start(f32[16,1024]{1,0:T(8,128)S(1)} %update.5.refs_5_.refs_4_), channel_id=1, source_target_pairs={{0,16},{8,24},{16,0},{24,8},{1,17},{9,25},{17,1},{25,9},{2,18},{10... | collective-permute-start | bytes 196616 | tf_op jit(solution)/shard_map/ppermute | solution.py:413
  123.9 8.1 %collective-permute-start.39 = (f32[32,1024]{1,0:T(8,128)S(1)}, f32[32,1024]{1,0:T(8,128)S(1)}, u32[]{:S(2)}, u32[]{:S(2)}) collective-permute-start(f32[32,1024]{1,0:T(8,128)S(1)} %chip_logits.3.refs_0_), channel_id=1, source_target_pairs={{0,4},{1,5},{2,6},{3,7},{4,0},{5,1},{6,2},{7,3},{8,12},{9,13},{10,... | collective-permute-start | bytes 393224 | tf_op jit(solution)/shard_map/ppermute | solution.py:413
  136.5 8.2 %collective-permute-start.49 = (f32[16,1024]{1,0:T(8,128)S(1)}, f32[16,1024]{1,0:T(8,128)S(1)}, u32[]{:S(2)}, u32[]{:S(2)}) collective-permute-start(f32[16,1024]{1,0:T(8,128)S(1)} %get-tuple-element.109), channel_id=1, source_target_pairs={{0,16},{8,24},{16,0},{24,8},{1,17},{9,25},{17,1},{25,9},{2,18},{10... | collective-permute-start | bytes 196616 | tf_op jit(solution)/shard_map/ppermute | solution.py:413
  136.5 8.2 %collective-permute-start.50 = (f32[16,1024]{1,0:T(8,128)S(1)}, f32[16,1024]{1,0:T(8,128)S(1)}, u32[]{:S(2)}, u32[]{:S(2)}) collective-permute-start(f32[16,1024]{1,0:T(8,128)S(1)} %get-tuple-element.110), channel_id=1, source_target_pairs={{0,8},{8,0},{16,24},{24,16},{1,9},{9,1},{17,25},{25,17},{2,10},{10... | collective-permute-start | bytes 196616 | tf_op jit(solution)/shard_map/ppermute | solution.py:413
  140.2 8.3 %collective-permute-start.42 = (f32[16,1024]{1,0:T(8,128)S(1)}, f32[16,1024]{1,0:T(8,128)S(1)}, u32[]{:S(2)}, u32[]{:S(2)}) collective-permute-start(f32[16,1024]{1,0:T(8,128)S(1)} %get-tuple-element.104), channel_id=1, source_target_pairs={{0,24},{8,16},{16,8},{24,0},{1,25},{9,17},{17,9},{25,1},{2,26},{10... | collective-permute-start | bytes 196616 | tf_op jit(solution)/shard_map/ppermute | solution.py:413
  144.7 9.1 %collective-permute-start.51 = (f32[16,1024]{1,0:T(8,128)S(1)}, f32[16,1024]{1,0:T(8,128)S(1)}, u32[]{:S(2)}, u32[]{:S(2)}) collective-permute-start(f32[16,1024]{1,0:T(8,128)S(1)} %grad_sum.7.refs_1_), channel_id=1, source_target_pairs={{0,8},{8,0},{16,24},{24,16},{1,9},{9,1},{17,25},{25,17},{2,10},{10... | collective-permute-start | bytes 196616 | tf_op jit(solution)/shard_map/ppermute | solution.py:413
  144.8 9.7 %collective-permute-start.52 = (f32[16,1024]{1,0:T(8,128)S(1)}, f32[16,1024]{1,0:T(8,128)S(1)}, u32[]{:S(2)}, u32[]{:S(2)}) collective-permute-start(f32[16,1024]{1,0:T(8,128)S(1)} %grad_sum.7.refs_1_), channel_id=1, source_target_pairs={{0,16},{8,24},{16,0},{24,8},{1,17},{9,25},{17,1},{25,9},{2,18},{10... | collective-permute-start | bytes 196616 | tf_op jit(solution)/shard_map/ppermute | solution.py:413
  149.7 11.7 %collective-permute-start.45 = (f32[16,1024]{1,0:T(8,128)S(1)}, f32[16,1024]{1,0:T(8,128)S(1)}, u32[]{:S(2)}, u32[]{:S(2)}) collective-permute-start(f32[16,1024]{1,0:T(8,128)S(1)} %grad_sum.6.refs_1_), channel_id=1, source_target_pairs={{0,8},{8,0},{16,24},{24,16},{1,9},{9,1},{17,25},{25,17},{2,10},{10... | collective-permute-start | bytes 196616 | tf_op jit(solution)/shard_map/ppermute | solution.py:413
  150.1 11.4 %collective-permute-start.46 = (f32[16,1024]{1,0:T(8,128)S(1)}, f32[16,1024]{1,0:T(8,128)S(1)}, u32[]{:S(2)}, u32[]{:S(2)}) collective-permute-start(f32[16,1024]{1,0:T(8,128)S(1)} %grad_sum.6.refs_1_), channel_id=1, source_target_pairs={{0,16},{8,24},{16,0},{24,8},{1,17},{9,25},{17,1},{25,9},{2,18},{10... | collective-permute-start | bytes 196616 | tf_op jit(solution)/shard_map/ppermute | solution.py:413
  169.2 8.4 %collective-permute-start.56 = (f32[16,2048]{1,0:T(8,128)S(1)}, f32[16,2048]{1,0:T(8,128)S(1)}, u32[]{:S(2)}, u32[]{:S(2)}) collective-permute-start(f32[16,2048]{1,0:T(8,128)S(1)} %get-tuple-element.113), channel_id=1, source_target_pairs={{0,4},{1,5},{2,6},{3,7},{4,0},{5,1},{6,2},{7,3},{8,12},{9,13},{10,... | collective-permute-start | bytes 393224 | tf_op jit(solution)/shard_map/ppermute | solution.py:413
  178.7 7.7 %collective-permute-start.59 = (f32[16,2048]{1,0:T(8,128)S(1)}, f32[16,2048]{1,0:T(8,128)S(1)}, u32[]{:S(2)}, u32[]{:S(2)}) collective-permute-start(f32[16,2048]{1,0:T(8,128)S(1)} %fwd_sum.3.refs_0_.refs_1_.refs_2_), channel_id=1, source_target_pairs={{0,4},{1,5},{2,6},{3,7},{4,0},{5,1},{6,2},{7,3},{8,12},{9,13},{10,... | collective-permute-start | bytes 393224 | tf_op jit(solution)/shard_map/ppermute | solution.py:413
  191.6 11.7 %collective-permute-start.62 = (f32[16,1152]{1,0:T(8,128)S(1)}, f32[16,1152]{1,0:T(8,128)S(1)}, u32[]{:S(2)}, u32[]{:S(2)}) collective-permute-start(f32[16,1152]{1,0:T(8,128)S(1)} %get-tuple-element.118), channel_id=1, source_target_pairs={{0,24},{8,16},{16,8},{24,0},{1,25},{9,17},{17,9},{25,1},{2,26},{10... | collective-permute-start | bytes 221192 | tf_op jit(solution)/shard_map/ppermute | solution.py:413
  194.3 10.8 %collective-permute-start.63 = (f32[16,1152]{1,0:T(8,128)S(1)}, f32[16,1152]{1,0:T(8,128)S(1)}, u32[]{:S(2)}, u32[]{:S(2)}) collective-permute-start(f32[16,1152]{1,0:T(8,128)S(1)} %get-tuple-element.119), channel_id=1, source_target_pairs={{0,16},{8,24},{16,0},{24,8},{1,17},{9,25},{17,1},{25,9},{2,18},{10... | collective-permute-start | bytes 221192 | tf_op jit(solution)/shard_map/ppermute | solution.py:413
  194.5 10.5 %collective-permute-start.64 = (f32[16,1152]{1,0:T(8,128)S(1)}, f32[16,1152]{1,0:T(8,128)S(1)}, u32[]{:S(2)}, u32[]{:S(2)}) collective-permute-start(f32[16,1152]{1,0:T(8,128)S(1)} %get-tuple-element.120), channel_id=1, source_target_pairs={{0,8},{8,0},{16,24},{24,16},{1,9},{9,1},{17,25},{25,17},{2,10},{10... | collective-permute-start | bytes 221192 | tf_op jit(solution)/shard_map/ppermute | solution.py:413
  200.6 7.8 %collective-permute-start.68 = (f32[16,1024]{1,0:T(8,128)S(1)}, f32[16,1024]{1,0:T(8,128)S(1)}, u32[]{:S(2)}, u32[]{:S(2)}) collective-permute-start(f32[16,1024]{1,0:T(8,128)S(1)} %get-tuple-element.123), channel_id=1, source_target_pairs={{0,24},{8,16},{16,8},{24,0},{1,25},{9,17},{17,9},{25,1},{2,26},{10... | collective-permute-start | bytes 196616 | tf_op jit(solution)/shard_map/ppermute | solution.py:413
  205.1 8.5 %collective-permute-start.65 = (f32[16,1024]{1,0:T(8,128)S(1)}, f32[16,1024]{1,0:T(8,128)S(1)}, u32[]{:S(2)}, u32[]{:S(2)}) collective-permute-start(f32[16,1024]{1,0:T(8,128)S(1)} %get-tuple-element.121.refs_0_), channel_id=1, source_target_pairs={{0,8},{8,0},{16,24},{24,16},{1,9},{9,1},{17,25},{25,17},{2,10},{10... | collective-permute-start | bytes 196616 | tf_op jit(solution)/shard_map/ppermute | solution.py:413
  205.4 9.8 %collective-permute-start.66 = (f32[16,1024]{1,0:T(8,128)S(1)}, f32[16,1024]{1,0:T(8,128)S(1)}, u32[]{:S(2)}, u32[]{:S(2)}) collective-permute-start(f32[16,1024]{1,0:T(8,128)S(1)} %get-tuple-element.121.refs_0_), channel_id=1, source_target_pairs={{0,16},{8,24},{16,0},{24,8},{1,17},{9,25},{17,1},{25,9},{2,18},{10... | collective-permute-start | bytes 196616 | tf_op jit(solution)/shard_map/ppermute | solution.py:413
  (50 other events, 362.0 us)
